TPU v7x, 256 devices: a whole 4x4x8 slice. The times are simulated.
256 devices in a mesh: ctx: 256 (over x, y, z, core).
Axes of the slice: x: 4, y: 4, z: 8, core: 2. Of those that a mesh axis runs over, the one named last changes fastest.
Arguments:
- queries: bfloat16 [32768, 512], P('ctx'), may hold values from -6 to 6
- keys: bfloat16 [32768, 512], P('ctx'), may hold values from -6 to 6
- values: bfloat16 [32768, 512], P('ctx'), may hold values from -6 to 6
- out_weight: bfloat16 [4096, 512], P('ctx'), may hold values from -0.25 to 0.25
- cotangent: bfloat16 [32768, 4096], P('ctx'), may hold values from -24 to 24
Outputs:
- mixed: bfloat16 [32768, 4096], P('ctx')
- query_gradient: bfloat16 [32768, 512], P('ctx')
- key_gradient: bfloat16 [32768, 512], P('ctx')
- value_gradient: bfloat16 [32768, 512], P('ctx')
- weight_grad: float32 [4096, 512], P('ctx')
All inputs are finite; a program needn't handle non-finite values.
Results may differ from a plain program's by a relative error of at most 0.014.
Values may be sent and summed in bfloat16 or wider, within the bound.
No kernel may reach another device: no remote copies, remote signals or barrier semaphores. Data moves between devices by JAX's collectives and lax.ppermute only.
A program may use at most 320 MiB of HBM per device.

v0:
```python
import jax
import jax.numpy as jnp
from jax import lax
from jax.sharding import PartitionSpec as P

HEADS = 4
HEAD = 128


def carried_in(value, axis, combine, identity):
    size, index = (lax.axis_size(axis), lax.axis_index(axis))
    everything = lax.all_gather(value, axis)
    start = jnp.broadcast_to(jnp.asarray(identity, value.dtype), value.shape)

    def step(k, before):
        reached = k < index
        new = combine(before, everything[k])
        return jnp.where(reached, new, before)

    return lax.fori_loop(0, size, step, start)


def carried_in_2(value, axis, join, neutral):
    count = lax.axis_size(axis)
    place = lax.axis_index(axis)
    ahead = count - 1 - place
    gathered = lax.all_gather(value.astype(jnp.bfloat16), axis)
    state = jnp.zeros_like(value) + jnp.asarray(neutral, value.dtype)

    def one(step, state):
        source = count - 1 - step
        return join(state, lax.dynamic_index_in_dim(gathered, source, 0, False).astype(value.dtype))

    return lax.fori_loop(0, ahead, one, state)


def combine_sum(earlier, later):
    return jax.tree.map(jnp.add, earlier, later)


def body(queries, keys, values, out_weight, cotangent):
    tok_count = queries.shape[0]
    offset = lax.axis_index("ctx") * tok_count
    positions = offset + jnp.arange(tok_count, dtype=jnp.int32)
    position_scale = lax.rsqrt(HEAD * (positions + 1).astype(jnp.float32))
    head_shape = (tok_count, HEADS, HEAD)
    head_queries = queries.reshape(head_shape)
    head_keys = keys.reshape(head_shape)
    head_values = values.reshape(head_shape)
    full_weight = lax.all_gather(out_weight, "ctx", axis=0, tiled=True)
    grad_attended = jnp.dot(cotangent, full_weight, preferred_element_type=jnp.float32)
    scaled_grad = (grad_attended * position_scale[:, None]).astype(jnp.bfloat16)
    head_gradient = scaled_grad.reshape(head_shape)
    local_keys = jnp.einsum(
        "ixj,ixg->xjg", head_keys, head_values, preferred_element_type=jnp.float32
    )
    local_grads = jnp.einsum(
        "ixj,ixg->xjg", head_queries, head_gradient, preferred_element_type=jnp.float32
    )
    zero_state = jnp.zeros_like(local_keys)
    earlier_keys = carried_in(local_keys, "ctx", combine_sum, zero_state)
    later_grads = carried_in_2(local_grads, "ctx", combine_sum, zero_state)
    prefix_key_state = earlier_keys.astype(jnp.bfloat16)
    state_gradient = later_grads.astype(jnp.bfloat16)
    row_index = jnp.arange(tok_count, dtype=jnp.int32)
    causal = (row_index[:, None] >= row_index[None, :])[None]
    scores = jnp.einsum("shd,thd->hst", head_queries, head_keys, preferred_element_type=jnp.float32)
    masked_scores = jnp.where(causal, scores, 0.0).astype(jnp.bfloat16)
    local_part = jnp.einsum(
        "kun,nkr->ukr", masked_scores, head_values, preferred_element_type=jnp.float32
    )
    carried_over = jnp.einsum(
        "mqw,qwi->mqi", head_queries, prefix_key_state, preferred_element_type=jnp.float32
    )
    attended = (
        ((local_part + carried_over) * position_scale[:, None, None])
        .astype(jnp.bfloat16)
        .reshape(tok_count, -1)
    )
    mixed = lax.dot_general(
        attended, full_weight, (((1,), (1,)), ((), ())), preferred_element_type=jnp.float32
    ).astype(jnp.bfloat16)
    grad_scores = jnp.einsum(
        "shd,thd->hst", head_gradient, head_values, preferred_element_type=jnp.float32
    )
    masked_gradient = jnp.where(causal, grad_scores, 0.0).astype(jnp.bfloat16)
    query_gradient = jnp.einsum(
        "kun,nkr->ukr", masked_gradient, head_keys, preferred_element_type=jnp.float32
    )
    query_gradient = query_gradient + jnp.einsum(
        "riq,ipq->rip", head_gradient, prefix_key_state, preferred_element_type=jnp.float32
    )
    key_gradient = jnp.einsum(
        "olf,loy->foy", masked_gradient, head_queries, preferred_element_type=jnp.float32
    )
    key_gradient = key_gradient + jnp.einsum(
        "rwd,wed->rwe", head_values, state_gradient, preferred_element_type=jnp.float32
    )
    value_gradient = jnp.einsum(
        "olf,loy->foy", masked_scores, head_gradient, preferred_element_type=jnp.float32
    )
    value_gradient = value_gradient + jnp.einsum(
        "pyd,yda->pya", head_keys, state_gradient, preferred_element_type=jnp.float32
    )
    flat_shape = (tok_count, -1)
    query_gradient = query_gradient.reshape(flat_shape).astype(jnp.bfloat16)
    key_gradient = key_gradient.reshape(flat_shape).astype(jnp.bfloat16)
    value_gradient = value_gradient.reshape(flat_shape).astype(jnp.bfloat16)
    weight_term = lax.dot_general(
        cotangent, attended, (((0,), (0,)), ((), ())), preferred_element_type=jnp.float32
    )
    weight_grad = lax.psum_scatter(weight_term, "ctx", scatter_dimension=0, tiled=True)
    return (mixed, query_gradient, key_gradient, value_gradient, weight_grad)


def solution(mesh):
    return jax.shard_map(
        body,
        mesh=mesh,
        in_specs=(P("ctx", None), P("ctx", None), P("ctx", None), P("ctx", None), P("ctx", None)),
        out_specs=(P("ctx", None), P("ctx", None), P("ctx", None), P("ctx", None), P("ctx", None)),
        check_vma=False,
    )
```

profile of v0, /device:TPU:1, one launch (start us, length us, event | category | flops | bytes accessed | tf_op | source)
XLA Modules:
  0.0 1912.8 jit_solution(2054513788528808630)
XLA Ops:
  9.0 1.8 fusion.15
  10.9 120.3 %all-gather.6.cloned.1.call-done = bf16[4096,512]{1,0:T(8,128)(2,1)} async-done(((bf16[16,512]{1,0:T(8,128)(2,1)}), bf16[4096,512]{1,0:T(8,128)(2,1)}) %all-gather.6.cloned.1.call-update) | async-done | bytes 4194320 | tf_op jit(solution)/shard_map/all_gather | solution.py:50
  131.2 2.9 fusion.10
  135.8 209.6 %all-gather.8.cloned.1.call-done = f32[1024,128,128]{2,1,0:T(8,128)} async-done(((f32[4,128,128]{2,1,0:T(8,128)}), f32[1024,128,128]{2,1,0:T(8,128)}) %all-gather.8.cloned.1.call-update) | async-done | bytes 67108880 | tf_op jit(solution)/shard_map/all_gather | solution.py:12
  345.3 273.4 %while.27 = (s32[]{:T(128)}, f32[4,128,128]{2,1,0:T(8,128)S(1)}, s32[]{:T(128)}, f32[256,4,128,128]{3,2,1,0:T(8,128)}, s32[]{:T(128)}, /*index=5*/s32[]{:T(128)}) while((s32[]{:T(128)}, f32[4,128,128]{2,1,0:T(8,128)S(1)}, s32[]{:T(128)}, f32[256,4,128,128]{3,2,1,0:T(8,128)}, s32[]{:T(128)}, /*index=5*/s32[]{:T(128)}) %tuple.60), condition=%wide.region_1.2_spmd.clone, body=%wide.region_0.1_spmd.clone.sunk | while | flops 196612 | bytes 786533 | solution.py:20
  358.1 1.0 add_select_fusion.2
  364.5 1.0 add_select_fusion.2
  370.9 1.0 add_select_fusion.2
  396.4 1.1 add_select_fusion.2
  401.8 1.0 add_select_fusion.2
  403.9 1.0 add_select_fusion.2
  405.0 1.0 add_select_fusion.2
  408.2 1.0 add_select_fusion.2
  409.3 1.1 add_select_fusion.2
  410.4 1.1 add_select_fusion.2
  434.9 1.1 add_select_fusion.2
  436.0 1.1 add_select_fusion.2
  437.2 1.1 add_select_fusion.2
  441.5 1.0 add_select_fusion.2
  443.6 1.1 add_select_fusion.2
  446.8 1.1 add_select_fusion.2
  448.0 1.1 add_select_fusion.2
  451.2 1.1 add_select_fusion.2
  452.2 1.0 add_select_fusion.2
  454.4 1.1 add_select_fusion.2
  455.5 1.1 add_select_fusion.2
  456.6 1.0 add_select_fusion.2
  459.8 1.1 add_select_fusion.2
  460.9 1.1 add_select_fusion.2
  462.0 1.1 add_select_fusion.2
  463.1 1.1 add_select_fusion.2
  464.2 1.0 add_select_fusion.2
  466.3 1.1 add_select_fusion.2
  469.6 1.1 add_select_fusion.2
  470.6 1.1 add_select_fusion.2
  471.7 1.0 add_select_fusion.2
  474.9 1.1 add_select_fusion.2
  477.1 1.0 add_select_fusion.2
  479.2 1.0 add_select_fusion.2
  481.3 1.0 add_select_fusion.2
  484.5 1.1 add_select_fusion.2
  486.7 1.0 add_select_fusion.2
  494.2 1.1 add_select_fusion.2
  619.0 4.5 convolution_bitcast_fusion
  623.5 9.0 copy.58
  633.2 250.6 %while.26 = (s32[]{:T(128)}, f32[4,128,128]{2,1,0:T(8,128)S(1)}, s32[]{:T(128)}, bf16[256,4,128,128]{3,2,1,0:T(8,128)(2,1)}, s32[]{:T(128)}, /*index=5*/s32[]{:T(128)}, s32[]{:T(128)}, s32[]{:T(128)}) while((s32[]{:T(128)}, f32[4,128,128]{2,1,0:T(8,128)S(1)}, s32[]{:T(128)}, bf16[256,4,128,128]{3,2,1,0:T(8,128)(2,1)}, s32[]{:T(128)}, ...), condition=%wide.region_3.4_spmd, body=%wide.region_2.3_spmd.sunk | while | flops 131078 | bytes 655503 | solution.py:34
  887.0 4.7 convolution_convert_fusion
  891.7 1014.6 %reduce-scatter.4.cloned.1.call-done = f32[16,512]{1,0:T(8,128)} async-done(((f32[4096,512]{1,0:T(8,128)}), f32[16,512]{1,0:T(8,128)}) %reduce-scatter.4.cloned.1.call-update) | async-done | bytes 32784
  (510 shorter events, 479.2 us)
Async XLA Ops:
  7.2 124.0 %copy-start = (bf16[128,4096]{1,0:T(8,128)(2,1)S(1)}, bf16[128,4096]{1,0:T(8,128)(2,1)}, u32[]{:S(2)}) copy-start(bf16[128,4096]{1,0:T(8,128)(2,1)} %param.13) | copy-start | bytes 3145732
  7.2 128.1 %copy-start.3 = (bf16[128,512]{1,0:T(8,128)(2,1)S(1)}, bf16[128,512]{1,0:T(8,128)(2,1)}, u32[]{:S(2)}) copy-start(bf16[128,512]{1,0:T(8,128)(2,1)} %param.10) | copy-start | bytes 393220
  7.2 128.3 %copy-start.2 = (bf16[128,512]{1,0:T(8,128)(2,1)S(1)}, bf16[128,512]{1,0:T(8,128)(2,1)}, u32[]{:S(2)}) copy-start(bf16[128,512]{1,0:T(8,128)(2,1)} %param.11) | copy-start | bytes 393220
  7.2 127.0 %copy-start.1 = (bf16[128,512]{1,0:T(8,128)(2,1)S(1)}, bf16[128,512]{1,0:T(8,128)(2,1)}, u32[]{:S(2)}) copy-start(bf16[128,512]{1,0:T(8,128)(2,1)} %param.9) | copy-start | bytes 393220
  7.2 124.0 %all-gather.6.cloned.1.call-start = ((), (), s32[]{:S(2)}) async-start(), calls=%async_computation.1 | async-start | bytes 4210688 | tf_op jit(solution)/shard_map/all_gather | solution.py:50
  7.9 337.4 %all-gather.8.cloned.1.call-start = ((), (), s32[]{:S(2)}) async-start(), calls=%async_computation.2 | async-start | bytes 67371008 | tf_op jit(solution)/shard_map/all_gather | solution.py:12
  10.8 622.3 %all-gather.10.cloned.1.call-start = ((), (), s32[]{:S(2)}) async-start(), calls=%async_computation.3 | async-start | bytes 33685504 | tf_op jit(solution)/shard_map/all_gather | solution.py:27
  135.2 1771.0 %reduce-scatter.4.cloned.1.call-start = ((), (), s32[]{:S(2)}) async-start(), calls=%async_computation.4 | async-start | bytes 8421376
Sparse Core Ops, SparseCore 0:
  11.8 119.3 all-gather.5
  135.5 209.7 all-gather.7
  349.5 149.6 all-gather.9
  632.6 1273.5 reduce-scatter.3
where the time goes:
time: 1930 us; the launch traced here: 1910 us
  waiting for transfers between devices  1350 us (70%)
  other arithmetic  512 us (27%)
    unnamed x5, waiting for transfers between devices  1020 us
    select_n x256, other arithmetic, step(): return jnp.where(reached, new, before)  267 us
    add x254, other arithmetic, combine_sum(): return jax.tree.map(jnp.add, earlier, later)  245 us
    all_gather x1, waiting for transfers between devices, carried_in(): everything = lax.all_gather(value, axis)  210 us
    all_gather x1, waiting for transfers between devices, body(): full_weight = lax.all_gather(out_weight, 'ctx', axis=0, tiled=True)  120 us
  transfers between devices with their start and end apart: 4, of which 3 were waited for; matrix products, arithmetic and copies ran while one was open for 28% of the time, Pallas kernels for 0%

commit v1 on v0

v1 whole, which is shorter than its diff:
```python
import jax
import jax.numpy as jnp
from jax import lax
from jax.sharding import Mesh, PartitionSpec as P

HEADS = 4
HEAD = 128
XY = ("x", "y")
ZC = ("z", "c")
BF16 = jnp.bfloat16
F32 = jnp.float32


def exchange(value, axes):
    return lax.all_to_all(value, axes, 0, 0, tiled=True)


def earlier_sums(parts):
    running = jnp.zeros(parts.shape[1:], F32)
    before = []
    for i in range(parts.shape[0]):
        before.append(running)
        running = running + parts[i].astype(F32)
    return jnp.stack(before), running


def later_sums(parts):
    running = jnp.zeros(parts.shape[1:], F32)
    after = []
    for i in reversed(range(parts.shape[0])):
        after.append(running)
        running = running + parts[i].astype(F32)
    return jnp.stack(after[::-1]), running


def masked_sum(parts, keep):
    return jnp.sum(jnp.where(keep[:, None, None], parts.astype(F32), 0.0), axis=0)


def body(queries, keys, values, out_weight, cotangent):
    groups = lax.axis_size(XY)
    members = lax.axis_size(ZC)
    group = lax.axis_index(XY)
    member = lax.axis_index(ZC)
    core = lax.axis_index("c")
    tokens, features = queries.shape
    rows = out_weight.shape[0]
    model = cotangent.shape[1]
    half = features // 2
    state_rows = HEADS * HEAD // members
    offset = (group * members + member) * tokens
    positions = offset + jnp.arange(tokens, dtype=jnp.int32)
    position_scale = lax.rsqrt(HEAD * (positions + 1).astype(F32))
    swap = [(0, 1), (1, 0)]

    column = exchange(jnp.broadcast_to(out_weight[None], (groups,) + out_weight.shape), XY)
    full_weight = lax.all_gather(column, ZC, axis=0)
    other_cotangent = lax.ppermute(cotangent, "c", swap)

    head_shape = (tokens, HEADS, HEAD)
    head_queries = queries.reshape(head_shape)
    head_keys = keys.reshape(head_shape)
    head_values = values.reshape(head_shape)

    local_keys = jnp.einsum("ixj,ixg->xjg", head_keys, head_values, preferred_element_type=F32)
    first = exchange(local_keys.astype(BF16).reshape(members, state_rows, HEAD), ZC)
    inside, total = earlier_sums(first)
    second = exchange(jnp.broadcast_to(total.astype(BF16)[None], (groups, state_rows, HEAD)), XY)
    before = masked_sum(second, jnp.arange(groups) < group)
    key_state = exchange((inside + before[None]).astype(BF16), ZC).reshape(HEADS, HEAD, HEAD)

    row_index = jnp.arange(tokens, dtype=jnp.int32)
    causal = (row_index[:, None] >= row_index[None, :])[None]
    scores = jnp.einsum("shd,thd->hst", head_queries, head_keys, preferred_element_type=F32)
    scores = jnp.where(causal, scores, 0.0).astype(BF16)
    local_part = jnp.einsum("kun,nkr->ukr", scores, head_values, preferred_element_type=F32)
    carried = jnp.einsum("mqw,qwi->mqi", head_queries, key_state, preferred_element_type=F32)
    attended = ((local_part + carried) * position_scale[:, None, None]).astype(BF16)
    attended = attended.reshape(tokens, features)

    full_weight = full_weight.transpose(1, 0, 2, 3).reshape(model, features)
    grad_attended = jnp.dot(cotangent, full_weight, preferred_element_type=F32)
    scaled_grad = (grad_attended * position_scale[:, None]).astype(BF16)
    head_gradient = scaled_grad.reshape(head_shape)
    local_grads = jnp.einsum("ixj,ixg->xjg", head_queries, head_gradient, preferred_element_type=F32)
    first = exchange(local_grads.astype(BF16).reshape(members, state_rows, HEAD), ZC)
    inside, total = later_sums(first)

    mine = lax.dynamic_slice_in_dim(attended, core * half, half, 1)
    theirs = lax.dynamic_slice_in_dim(attended, (1 - core) * half, half, 1)
    other = lax.ppermute(theirs, "c", swap)
    contract = (((0,), (0,)), ((), ()))
    weight_term = lax.dot_general(cotangent, mine, contract, preferred_element_type=F32)
    weight_term = weight_term + lax.dot_general(other_cotangent, other, contract, preferred_element_type=F32)
    weight_term = weight_term.astype(BF16).reshape(groups, model // groups, half)
    pack = state_rows * HEAD // half
    total = jnp.broadcast_to(total.astype(BF16).reshape(1, pack, half), (groups, pack, half))
    second = exchange(jnp.concatenate([weight_term, total], axis=1), XY)
    share = model // groups
    after = masked_sum(second[:, share:].reshape(groups, state_rows, HEAD), jnp.arange(groups) > group)
    weight_part = jnp.sum(second[:, :share].astype(F32), axis=0).astype(BF16).reshape(members, rows, half)
    states = (inside + after[None]).astype(BF16).reshape(members, pack, half)
    third = exchange(jnp.concatenate([weight_part, states], axis=1), ZC)
    grad_state = third[:, rows:].reshape(HEADS, HEAD, HEAD)
    weight_grad = jnp.sum(third[:, :rows].astype(F32).reshape(members // 2, 2, rows, half), axis=0)
    weight_grad = weight_grad.transpose(1, 0, 2).reshape(rows, features)

    mixed = lax.dot_general(
        attended, full_weight, (((1,), (1,)), ((), ())), preferred_element_type=F32
    ).astype(BF16)
    grad_scores = jnp.einsum("shd,thd->hst", head_gradient, head_values, preferred_element_type=F32)
    grad_scores = jnp.where(causal, grad_scores, 0.0).astype(BF16)
    query_gradient = jnp.einsum("kun,nkr->ukr", grad_scores, head_keys, preferred_element_type=F32)
    query_gradient += jnp.einsum("riq,ipq->rip", head_gradient, key_state, preferred_element_type=F32)
    key_gradient = jnp.einsum("olf,loy->foy", grad_scores, head_queries, preferred_element_type=F32)
    key_gradient += jnp.einsum("rwd,wed->rwe", head_values, grad_state, preferred_element_type=F32)
    value_gradient = jnp.einsum("olf,loy->foy", scores, head_gradient, preferred_element_type=F32)
    value_gradient += jnp.einsum("pyd,yda->pya", head_keys, grad_state, preferred_element_type=F32)
    flat = (tokens, features)
    query_gradient = query_gradient.reshape(flat).astype(BF16)
    key_gradient = key_gradient.reshape(flat).astype(BF16)
    value_gradient = value_gradient.reshape(flat).astype(BF16)
    return (mixed, query_gradient, key_gradient, value_gradient, weight_grad)


def solution(mesh):
    grid = Mesh(mesh.devices.reshape(4, 4, 8, 2), ("x", "y", "z", "c"))
    spec = P(("x", "y", "z", "c"), None)
    return jax.shard_map(
        body, mesh=grid, in_specs=(spec,) * 5, out_specs=(spec,) * 5, check_vma=False
    )
```

time: 1930 us -> 161 us (0.08)
  waiting for transfers between devices: 1350 us -> 62.9 us
  other arithmetic: 512 us -> 5.22 us
  starting transfers between devices: 0.16 us -> 32.6 us
    unnamed x5 -> x1, waiting for transfers between devices: 1020 us -> 0.02 us
    all_gather x3 -> x1, waiting for transfers between devices: 330 us -> 0.01 us  [body(): full_weight = lax.all_gather(column, ZC, axis=0)]
    select_n x256 -> x0, other arithmetic: 267 us -> none  [step(): return jnp.where(reached, new, before)]
    add x254 -> x1, other arithmetic: 245 us -> 0.03 us  [later_sums(): running = running + parts[i].astype(F32)]
    all_to_all x0 -> x6, waiting for transfers between devices: none -> 62.9 us  [exchange(): return lax.all_to_all(value, axes, 0, 0, tiled=True)]
    all_to_all x0 -> x6, starting transfers between devices: none -> 31.9 us  [exchange(): return lax.all_to_all(value, axes, 0, 0, tiled=True)]
  transfers between devices with their start and end apart: 4 -> 9, of which waited for: 3 -> 6; matrix products, arithmetic and copies ran while one was open for 28% -> 16% of each run, Pallas kernels for 0% -> 0%
where the time goes in v1:
time: 161 us; the launch traced here: 160 us
  waiting for transfers between devices  62.9 us (39%)
  starting transfers between devices  32.6 us (20%)
  matrix products  16 us (10%)
  blocking collectives  14.9 us (9%)
  between operations  14.7 us (9%)
  local copies, waits for them, and re-layouts  14 us (9%)
  other arithmetic  5.22 us (3%)
    all_to_all x6, waiting for transfers between devices, exchange(): return lax.all_to_all(value, axes, 0, 0, tiled=True)  62.9 us
    all_to_all x6, starting transfers between devices, exchange(): return lax.all_to_all(value, axes, 0, 0, tiled=True)  31.9 us
    all_to_all x1, blocking collectives, exchange(): return lax.all_to_all(value, axes, 0, 0, tiled=True)  14.9 us
    dot_general x1, matrix products, body(): lax.dot_general(attended, full_weight, (((1,), (1,)), ((), ())), preferre...  4.65 us
    unnamed x30, local copies, waits for them, and re-layouts  4.34 us
  transfers between devices with their start and end apart: 9, of which 6 were waited for; matrix products, arithmetic and copies ran while one was open for 16% of the time, Pallas kernels for 0%

profile of v1, /device:TPU:1, one launch (start us, length us, event | category | flops | bytes accessed | tf_op | source)
XLA Modules:
  0.0 160.4 jit_solution(4493785501662741001)
XLA Ops:
  7.2 0.8 broadcast_in_dim.72
  8.1 14.9 %all_to_all.35 = bf16[16,16,512]{2,1,0:T(8,128)(2,1)} all-to-all(bf16[16,16,512]{2,1,0:T(8,128)(2,1)S(1)} %broadcast_in_dim.72), channel_id=1, replica_groups=mesh['x'=4,'y'=4,'z'=8,'c'=2] {'x','y'}, dimensions={0} | all-to-all | bytes 524288 | tf_op jit(solution)/shard_map/all_to_all | solution.py:15
  23.0 1.0 copy.197
  24.1 0.8 convolution_convert_fusion.2
  24.9 10.5 %all-to-all-start = ((bf16[16,32,128]{2,1,0:T(8,128)(2,1)}), bf16[16,32,128]{2,1,0:T(8,128)(2,1)S(1)}, u32[]{:S(2)}, u32[]{:S(2)}) async-start(bf16[16,32,128]{2,1,0:T(8,128)(2,1)} %bitcast.1), calls=%async_computation | async-start | bytes 262144 | tf_op jit(solution)/shard_map/all_to_all | solution.py:15
  35.4 0.2 collective-permute-start.1
  35.6 1.0 copy.168
  36.7 1.1 fusion.9
  37.8 7.9 %all-to-all-done = bf16[16,32,128]{2,1,0:T(8,128)(2,1)S(1)} async-done(((bf16[16,32,128]{2,1,0:T(8,128)(2,1)}), bf16[16,32,128]{2,1,0:T(8,128)(2,1)S(1)}, u32[]{:S(2)}, u32[]{:S(2)}) %all-to-all-start) | async-done | bytes 131104 | tf_op jit(solution)/shard_map/all_to_all | solution.py:15
  45.7 0.7 broadcast_in_dim.70
  46.4 3.5 %all-to-all-start.1 = ((bf16[16,32,128]{2,1,0:T(8,128)(2,1)}), bf16[16,32,128]{2,1,0:T(8,128)(2,1)S(1)}, u32[]{:S(2)}, u32[]{:S(2)}) async-start(bf16[16,32,128]{2,1,0:T(8,128)(2,1)} %broadcast_in_dim.70), calls=%async_computation.1 | async-start | bytes 262144 | tf_op jit(solution)/shard_map/all_to_all | solution.py:15
  50.1 6.5 %all-to-all-done.1 = bf16[16,32,128]{2,1,0:T(8,128)(2,1)S(1)} async-done(((bf16[16,32,128]{2,1,0:T(8,128)(2,1)}), bf16[16,32,128]{2,1,0:T(8,128)(2,1)S(1)}, u32[]{:S(2)}, u32[]{:S(2)}) %all-to-all-start.1) | async-done | bytes 131104 | tf_op jit(solution)/shard_map/all_to_all | solution.py:15
  56.7 0.1 select_reduce_fusion.1
  56.8 0.7 add_convert_fusion.1
  57.4 4.8 %all-to-all-start.2 = ((bf16[16,32,128]{2,1,0:T(8,128)(2,1)}), bf16[16,32,128]{2,1,0:T(8,128)(2,1)S(1)}, u32[]{:S(2)}, u32[]{:S(2)}) async-start(bf16[16,32,128]{2,1,0:T(8,128)(2,1)} %add_convert_fusion.1), calls=%async_computation.2 | async-start | bytes 262144 | tf_op jit(solution)/shard_map/all_to_all | solution.py:15
  62.2 0.2 convolution_bitcast_fusion.5
  62.5 8.9 %all-to-all-done.2 = bf16[16,32,128]{2,1,0:T(8,128)(2,1)S(1)} async-done(((bf16[16,32,128]{2,1,0:T(8,128)(2,1)}), bf16[16,32,128]{2,1,0:T(8,128)(2,1)S(1)}, u32[]{:S(2)}, u32[]{:S(2)}) %all-to-all-start.2) | async-done | bytes 131104 | tf_op jit(solution)/shard_map/all_to_all | solution.py:15
  71.4 0.2 fusion.6
  71.6 0.5 collective-permute-start
  72.1 2.7 %fusion.25 = f32[256,4096]{1,0:T(8,128)} fusion(bf16[128,4096]{1,0:T(8,128)(2,1)S(1)} %copy-done.2, bf16[128,512]{0,1:T(8,128)(2,1)S(1)} %bitcast.131, s32[]{:T(128)S(6)} %select_n.24), kind=kOutput, calls=%fused_computation.79 | convolution fusion | flops 268435456 | bytes 5308420 | tf_op jit(solution)/shard_map/dot_general | solution.py:93
  74.8 2.7 %copy.142 = bf16[16,16,16,512]{3,2,1,0:T(8,128)(2,1)S(1)} copy(bf16[16,16,16,512]{3,2,0,1:T(8,128)(2,1)} %bitcast.117) | data formatting | bytes 8388608 | tf_op jit(solution)/shard_map/transpose | solution.py:81
  77.5 1.9 %copy-done.1 = bf16[16,16,16,512]{3,2,1,0:T(8,128)(2,1)} copy-done((bf16[16,16,16,512]{3,2,1,0:T(8,128)(2,1)}, bf16[16,16,16,512]{3,2,1,0:T(8,128)(2,1)S(1)}, u32[]{:S(2)}) %copy-start.1) | copy-done | bytes 4194328
  79.4 0.7 fusion.12
  80.1 0.1 copy.169
  80.2 0.9 convolution_convert_fusion.1
  81.1 3.4 %all-to-all-start.4 = ((bf16[16,32,128]{2,1,0:T(8,128)(2,1)}), bf16[16,32,128]{2,1,0:T(8,128)(2,1)S(1)}, u32[]{:S(2)}, u32[]{:S(2)}) async-start(bf16[16,32,128]{2,1,0:T(8,128)(2,1)} %bitcast.16), calls=%async_computation.4 | async-start | bytes 262144 | tf_op jit(solution)/shard_map/all_to_all | solution.py:15
  84.6 3.2 %fusion.1 = bf16[4096,256]{0,1:T(8,128)(2,1)S(1)} fusion(f32[256,4096]{1,0:T(8,128)} %fusion.25, bf16[128,256]{0,1:T(8,128)(2,1)S(1)} %collective-permute-done, bf16[128,4096]{1,0:T(8,128)(2,1)} %collective-permute-done.1), kind=kOutput, calls=%fused_computation.2 | convolution fusion | flops 270532608 | bytes 7405568 | tf_op jit(solution)/shard_map/dot_general | solution.py:94
  87.8 2.6 %copy.165 = bf16[4096,256]{1,0:T(8,128)(2,1)} copy(bf16[4096,256]{0,1:T(8,128)(2,1)S(1)} %fusion.1) | data formatting | bytes 4194304 | tf_op jit(solution)/shard_map/reshape | solution.py:95
  90.3 0.2 fusion.10
  90.6 3.2 %all-to-all-done.4 = bf16[16,32,128]{2,1,0:T(8,128)(2,1)S(1)} async-done(((bf16[16,32,128]{2,1,0:T(8,128)(2,1)}), bf16[16,32,128]{2,1,0:T(8,128)(2,1)S(1)}, u32[]{:S(2)}, u32[]{:S(2)}) %all-to-all-start.4) | async-done | bytes 131104 | tf_op jit(solution)/shard_map/all_to_all | solution.py:15
  93.9 3.1 %pad_maximum_fusion = bf16[16,272,256]{2,1,0:T(8,128)(2,1)} fusion(bf16[16,16,256]{2,1,0:T(8,128)(2,1)S(1)} %broadcast_in_dim.73, bf16[16,256,256]{2,1,0:T(8,128)(2,1)} %bitcast.116), kind=kLoop, calls=%fused_computation.4 | loop fusion | flops 4456448 | bytes 4456448 | tf_op jit(solution)/shard_map/concatenate | solution.py:98
  97.0 3.9 %all-to-all-start.5 = ((bf16[16,272,256]{2,1,0:T(8,128)(2,1)}), bf16[16,272,256]{2,1,0:T(8,128)(2,1)S(1)}, u32[]{:S(2)}, u32[]{:S(2)}) async-start(bf16[16,272,256]{2,1,0:T(8,128)(2,1)} %pad_maximum_fusion), calls=%async_computation.5 | async-start | bytes 4456448 | tf_op jit(solution)/shard_map/all_to_all | solution.py:15
  100.9 0.2 convolution_bitcast_fusion.3
  101.1 0.2 fusion.7
  101.2 0.8 copy.160
  102.4 29.5 %all-to-all-done.5 = bf16[16,272,256]{2,1,0:T(8,128)(2,1)S(1)} async-done(((bf16[16,272,256]{2,1,0:T(8,128)(2,1)}), bf16[16,272,256]{2,1,0:T(8,128)(2,1)S(1)}, u32[]{:S(2)}, u32[]{:S(2)}) %all-to-all-start.5) | async-done | bytes 2228256 | tf_op jit(solution)/shard_map/all_to_all | solution.py:15
  132.0 0.3 slice_reduce_fusion
  132.3 0.7 pad_maximum_fusion.1
  133.1 5.8 %all-to-all-start.6 = ((bf16[16,32,256]{2,1,0:T(8,128)(2,1)}), bf16[16,32,256]{2,1,0:T(8,128)(2,1)S(1)}, u32[]{:S(2)}, u32[]{:S(2)}) async-start(bf16[16,32,256]{2,1,0:T(8,128)(2,1)} %pad_maximum_fusion.1), calls=%async_computation.6 | async-start | bytes 524288 | tf_op jit(solution)/shard_map/all_to_all | solution.py:15
  138.9 0.2 fusion.30
  139.1 4.6 %convolution_convert_fusion = bf16[128,4096]{1,0:T(8,128)(2,1)} fusion(bf16[128,512]{0,1:T(8,128)(2,1)S(1)} %bitcast.132, bf16[4096,512]{1,0:T(8,128)(2,1)} %bitcast.115), kind=kOutput, calls=%fused_computation.3 | convolution fusion | flops 537395200 | bytes 5373952 | tf_op jit(solution)/shard_map/dot_general | solution.py:108
  143.7 6.9 %all-to-all-done.6 = bf16[16,32,256]{2,1,0:T(8,128)(2,1)S(1)} async-done(((bf16[16,32,256]{2,1,0:T(8,128)(2,1)}), bf16[16,32,256]{2,1,0:T(8,128)(2,1)S(1)}, u32[]{:S(2)}, u32[]{:S(2)}) %all-to-all-start.6) | async-done | bytes 262176 | tf_op jit(solution)/shard_map/all_to_all | solution.py:15
  150.7 0.6 copy.172
  151.3 0.2 convolution_bitcast_fusion.1
  151.6 0.2 fusion.11
  151.8 0.8 copy.162
  152.6 0.2 fusion.8
  152.8 0.8 copy.161
  (75 shorter events, 0.7 us)
Async XLA Ops:
  7.2 16.9 %copy-start = (bf16[128,512]{1,0:T(8,128)(2,1)S(1)}, bf16[128,512]{1,0:T(8,128)(2,1)}, u32[]{:S(2)}) copy-start(bf16[128,512]{1,0:T(8,128)(2,1)} %param.7) | copy-start | bytes 393220
  7.2 64.9 %copy-start.2 = (bf16[128,4096]{1,0:T(8,128)(2,1)S(1)}, bf16[128,4096]{1,0:T(8,128)(2,1)}, u32[]{:S(2)}) copy-start(bf16[128,4096]{1,0:T(8,128)(2,1)} %param.9) | copy-start | bytes 3145732
  7.2 67.6 %all-gather.3.cloned.1.call-start = ((), (), s32[]{:S(2)}) async-start(), calls=%async_computation.7 | async-start | bytes 4456448 | tf_op jit(solution)/shard_map/all_gather | solution.py:57
  24.9 20.8 %all-to-all-start = ((bf16[16,32,128]{2,1,0:T(8,128)(2,1)}), bf16[16,32,128]{2,1,0:T(8,128)(2,1)S(1)}, u32[]{:S(2)}, u32[]{:S(2)}) async-start(bf16[16,32,128]{2,1,0:T(8,128)(2,1)} %bitcast.1), calls=%async_computation | async-start | bytes 262144 | tf_op jit(solution)/shard_map/all_to_all | solution.py:15
  35.4 49.2 %collective-permute-start.1 = (bf16[128,4096]{1,0:T(8,128)(2,1)}, bf16[128,4096]{1,0:T(8,128)(2,1)}, u32[]{:S(2)}, u32[]{:S(2)}) collective-permute-start(bf16[128,4096]{1,0:T(8,128)(2,1)} %param.9), channel_id=1, source_target_pairs={{0,1},{1,0},{2,3},{3,2},{4,5},{5,4},{6,7},{7,6},{8,9},{9,8},{10,11... | collective-permute-start | bytes 3145736 | tf_op jit(solution)/shard_map/ppermute | solution.py:58
  46.4 10.2 %all-to-all-start.1 = ((bf16[16,32,128]{2,1,0:T(8,128)(2,1)}), bf16[16,32,128]{2,1,0:T(8,128)(2,1)S(1)}, u32[]{:S(2)}, u32[]{:S(2)}) async-start(bf16[16,32,128]{2,1,0:T(8,128)(2,1)} %broadcast_in_dim.70), calls=%async_computation.1 | async-start | bytes 262144 | tf_op jit(solution)/shard_map/all_to_all | solution.py:15
  57.4 13.9 %all-to-all-start.2 = ((bf16[16,32,128]{2,1,0:T(8,128)(2,1)}), bf16[16,32,128]{2,1,0:T(8,128)(2,1)S(1)}, u32[]{:S(2)}, u32[]{:S(2)}) async-start(bf16[16,32,128]{2,1,0:T(8,128)(2,1)} %add_convert_fusion.1), calls=%async_computation.2 | async-start | bytes 262144 | tf_op jit(solution)/shard_map/all_to_all | solution.py:15
  71.6 12.9 %collective-permute-start = (bf16[128,256]{0,1:T(8,128)(2,1)S(1)}, bf16[128,256]{0,1:T(8,128)(2,1)S(1)}, u32[]{:S(2)}, u32[]{:S(2)}) collective-permute-start(bf16[128,256]{0,1:T(8,128)(2,1)S(1)} %constant_dynamic-slice_fusion), channel_id=1, source_target_pairs={{0,1},{1,0},{2,3},{3,2},{4,5},{5,4},{6,7},{7,6},{8,9},{9,8},{10,11... | collective-permute-start | bytes 196616 | tf_op jit(solution)/shard_map/ppermute | solution.py:91
  77.4 1.9 %copy-start.1 = (bf16[16,16,16,512]{3,2,1,0:T(8,128)(2,1)}, bf16[16,16,16,512]{3,2,1,0:T(8,128)(2,1)S(1)}, u32[]{:S(2)}) copy-start(bf16[16,16,16,512]{3,2,1,0:T(8,128)(2,1)S(1)} %copy.142) | copy-start | bytes 12582916
  81.1 12.6 %all-to-all-start.4 = ((bf16[16,32,128]{2,1,0:T(8,128)(2,1)}), bf16[16,32,128]{2,1,0:T(8,128)(2,1)S(1)}, u32[]{:S(2)}, u32[]{:S(2)}) async-start(bf16[16,32,128]{2,1,0:T(8,128)(2,1)} %bitcast.16), calls=%async_computation.4 | async-start | bytes 262144 | tf_op jit(solution)/shard_map/all_to_all | solution.py:15
  97.0 34.9 %all-to-all-start.5 = ((bf16[16,272,256]{2,1,0:T(8,128)(2,1)}), bf16[16,272,256]{2,1,0:T(8,128)(2,1)S(1)}, u32[]{:S(2)}, u32[]{:S(2)}) async-start(bf16[16,272,256]{2,1,0:T(8,128)(2,1)} %pad_maximum_fusion), calls=%async_computation.5 | async-start | bytes 4456448 | tf_op jit(solution)/shard_map/all_to_all | solution.py:15
  132.3 19.2 %copy-start.3 = (bf16[128,512]{1,0:T(8,128)(2,1)S(1)}, bf16[128,512]{1,0:T(8,128)(2,1)}, u32[]{:S(2)}) copy-start(bf16[128,512]{1,0:T(8,128)(2,1)} %param.6) | copy-start | bytes 393220
  133.1 17.5 %all-to-all-start.6 = ((bf16[16,32,256]{2,1,0:T(8,128)(2,1)}), bf16[16,32,256]{2,1,0:T(8,128)(2,1)S(1)}, u32[]{:S(2)}, u32[]{:S(2)}) async-start(bf16[16,32,256]{2,1,0:T(8,128)(2,1)} %pad_maximum_fusion.1), calls=%async_computation.6 | async-start | bytes 524288 | tf_op jit(solution)/shard_map/all_to_all | solution.py:15
Sparse Core Ops, SparseCore 0:
  23.2 47.4 all-gather.2

commit v2 on v1

v2 whole, which is shorter than its diff:
```python
import functools

import jax
import jax.numpy as jnp
from jax import lax
from jax.experimental import pallas as pl
from jax.experimental.pallas import tpu as pltpu
from jax.sharding import Mesh, PartitionSpec as P

HEADS = 4
HEAD = 128
TOKENS = 128
FEATURES = HEADS * HEAD
MODEL = 4096
GROUPS = 16
MEMBERS = 16
ROWS = MODEL // (GROUPS * MEMBERS)
SHARE = MODEL // GROUPS
STATE_ROWS = FEATURES // MEMBERS
CHUNKS = 4
XY = ("x", "y")
ZC = ("z", "c")
BF16 = jnp.bfloat16
F32 = jnp.float32
NN = (((1,), (0,)), ((), ()))
NT = (((1,), (1,)), ((), ()))
TN = (((0,), (0,)), ((), ()))
VMEM = pl.BlockSpec(memory_space=pltpu.VMEM)
SMEM = pl.BlockSpec(memory_space=pltpu.SMEM)
HBM = pl.BlockSpec(memory_space=pltpu.HBM)


def mul(a, b, dims):
    return lax.dot_general(a, b, dims, preferred_element_type=F32)


def shape(dims, dtype):
    return jax.ShapeDtypeStruct(dims, dtype)


def call(kernel, ins, outs, args, flops, limit=32, **kw):
    out_bytes = sum(o.size * o.dtype.itemsize for o in outs)
    in_bytes = sum(a.size * a.dtype.itemsize for a in args)
    one = len(outs) == 1
    return pl.pallas_call(
        kernel,
        in_specs=ins,
        out_specs=VMEM if one else [VMEM] * len(outs),
        out_shape=outs[0] if one else outs,
        compiler_params=pltpu.CompilerParams(vmem_limit_bytes=limit << 20),
        cost_estimate=pl.CostEstimate(
            flops=flops, bytes_accessed=in_bytes + out_bytes, transcendentals=0
        ),
        **kw,
    )(*args)


def head(ref, h):
    return ref[:, h * HEAD : (h + 1) * HEAD]


def state(ref, h):
    return ref[h * HEAD : (h + 1) * HEAD, :]


def causal(x):
    row = lax.broadcasted_iota(jnp.int32, x.shape, 0)
    col = lax.broadcasted_iota(jnp.int32, x.shape, 1)
    return jnp.where(row >= col, x, 0.0).astype(BF16)


def keys_kernel(k, v, out):
    for h in range(HEADS):
        out[h * HEAD : (h + 1) * HEAD, :] = mul(head(k, h), head(v, h), TN).astype(BF16)


def attend_kernel(place, q, k, v, key_state, scale, out, own, out_c, out_y, out_yc, by_head):
    for h in range(HEADS):
        qh = head(q, h)
        scores = causal(mul(qh, head(k, h), NT))
        total = mul(scores, head(v, h), NN) + mul(qh, state(key_state, h), NN)
        result = (total * scale[...]).astype(BF16)
        out[:, h * HEAD : (h + 1) * HEAD] = result
        by_head[h] = result
    me = place[0]
    own[...] = by_head[me]
    out_c[...] = by_head[me ^ 2]
    out_y[...] = by_head[me ^ 1]
    out_yc[...] = by_head[me ^ 3]


def weight_copies(w, held, sems):
    part = GROUPS // CHUNKS
    copies = []
    for i in range(CHUNKS):
        at = pl.ds(i * part, part)
        copies.append(pltpu.make_async_copy(w.at[:, at], held.at[:, at], sems.at[i]))
    return copies


def share_of(held, j):
    return held[:, j].reshape(SHARE, FEATURES)


def gradient_kernel(cot, w, q, scale, grad, sums, held, sems, cots, cot_sem):
    cot_copy = pltpu.make_async_copy(cot, cots, cot_sem)
    cot_copy.start()
    copies = weight_copies(w, held, sems)
    for copy in copies:
        copy.start()
    cot_copy.wait()
    total = None
    part = GROUPS // CHUNKS
    for i in range(CHUNKS):
        copies[i].wait()
        rows = [share_of(held, j) for j in range(i * part, (i + 1) * part)]
        at = slice(i * part * SHARE, (i + 1) * part * SHARE)
        term = mul(cots[:, at], jnp.concatenate(rows, axis=0), NN)
        total = term if total is None else total + term
    g = (total * scale[...]).astype(BF16)
    grad[...] = g
    for h in range(HEADS):
        gh = g[:, h * HEAD : (h + 1) * HEAD]
        sums[h * HEAD : (h + 1) * HEAD, :] = mul(head(q, h), gh, TN).astype(BF16)


def mixed_kernel(att, w, out, held, sems):
    copies = weight_copies(w, held, sems)
    for copy in copies:
        copy.start()
    for j in range(GROUPS):
        if j % (GROUPS // CHUNKS) == 0:
            copies[j // (GROUPS // CHUNKS)].wait()
        out[:, j * SHARE : (j + 1) * SHARE] = mul(att[...], share_of(held, j), NT).astype(BF16)


def weight_kernel(c0, c1, c2, c3, c4, c5, a0, a1, a2, a3, out):
    turned = jnp.concatenate([a[...].T for a in (a0, a1, a2, a3)], axis=1)
    for j in range(out.shape[0]):
        at = slice(j * SHARE, (j + 1) * SHARE)
        cots = jnp.concatenate([c[:, at] for c in (c0, c1, c2, c3, c4, c5)], axis=0)
        term = mul(turned, cots, NN).astype(BF16)
        for half in range(2):
            out[j, half * HEAD : (half + 1) * HEAD, :] = term[:, half * HEAD : (half + 1) * HEAD]
        out[j, SHARE:, :] = jnp.zeros((STATE_ROWS, HEAD), BF16)


def local_kernel(q, k, v, g, key_state, qg, kg, vg):
    for h in range(HEADS):
        at = slice(h * HEAD, (h + 1) * HEAD)
        qh, kh, vh, gh = head(q, h), head(k, h), head(v, h), head(g, h)
        scores = causal(mul(qh, kh, NT))
        grads = causal(mul(gh, vh, NT))
        qg[:, at] = (mul(grads, kh, NN) + mul(gh, state(key_state, h), NT)).astype(BF16)
        kg[:, at] = mul(grads, qh, TN)
        vg[:, at] = mul(scores, gh, TN)


def reduce_kernel(group, got, inside, out):
    me = group[0]
    after = jnp.zeros((STATE_ROWS, HEAD), F32)
    for j in range(GROUPS):
        piece = got[j, SHARE:, :].astype(F32)
        after = after + jnp.where(j > me, piece, 0.0)
    for m in range(MEMBERS):
        out[m, 2 * ROWS :, :] = (inside[m] + after).astype(BF16)
    for odd in range(2):
        for half in range(2):
            total = None
            for j in range(odd, GROUPS, 2):
                piece = got[j, half * HEAD : (half + 1) * HEAD, :].astype(F32)
                total = piece if total is None else total + piece
            turned = total.T.astype(BF16)
            for m in range(HEAD // ROWS):
                out[half * (HEAD // ROWS) + m, odd * ROWS : (odd + 1) * ROWS, :] = turned[
                    m * ROWS : (m + 1) * ROWS
                ]


def final_kernel(got, k, v, kg_local, vg_local, kg, vg, wg):
    per = HEAD // STATE_ROWS
    for h in range(HEADS):
        at = slice(h * HEAD, (h + 1) * HEAD)
        grad_state = jnp.concatenate(
            [got[h * per + i, 2 * ROWS :, :] for i in range(per)], axis=0
        )
        kg[:, at] = (kg_local[:, at] + mul(head(v, h), grad_state, NT)).astype(BF16)
        vg[:, at] = (vg_local[:, at] + mul(head(k, h), grad_state, NN)).astype(BF16)
    for core in range(2):
        for odd in range(2):
            total = None
            for m in range(core, MEMBERS, 2):
                piece = got[m, odd * ROWS : (odd + 1) * ROWS, :].astype(F32)
                total = piece if total is None else total + piece
            at = (core * 2 + odd) * HEAD
            wg[:, at : at + HEAD] = total


def exchange(value, axes):
    return lax.all_to_all(value, axes, 0, 0, tiled=True)


def sums_before(parts):
    running, before = jnp.zeros(parts[0].shape, F32), []
    for part in parts:
        before.append(running)
        running = running + part.astype(F32)
    return before, running


def body(queries, keys, values, out_weight, cotangent):
    group = lax.axis_index(XY)
    member = lax.axis_index(ZC)
    core = lax.axis_index("c")
    odd = lax.rem(lax.axis_index("y"), 2)
    positions = (group * MEMBERS + member) * TOKENS + jnp.arange(TOKENS, dtype=jnp.int32)
    scale = lax.rsqrt(HEAD * (positions + 1).astype(F32))[:, None]
    swap = [(0, 1), (1, 0)]
    swap_y = [(0, 1), (1, 0), (2, 3), (3, 2)]
    rows_shape = (MEMBERS, STATE_ROWS, HEAD)
    small = 2 * TOKENS * HEAD * FEATURES
    large = 2 * TOKENS * MODEL * FEATURES

    local_keys = call(
        keys_kernel, [VMEM] * 2, [shape((FEATURES, HEAD), BF16)], (keys, values), small
    )
    column = exchange(jnp.broadcast_to(out_weight[None], (GROUPS, ROWS, FEATURES)), XY)
    column, local_keys = lax.optimization_barrier((column, local_keys))
    weight = lax.all_gather(column, ZC, axis=0)
    cot_c = lax.ppermute(cotangent, "c", swap)
    cot_y1 = lax.ppermute(cotangent[: TOKENS // 2], "y", swap_y)

    first = exchange(local_keys.reshape(rows_shape), ZC)
    before, total = sums_before([first[i] for i in range(MEMBERS)])
    second = exchange(jnp.broadcast_to(total.astype(BF16)[None], rows_shape), XY)
    earlier = (jnp.arange(GROUPS) < group)[:, None, None]
    carried = jnp.sum(jnp.where(earlier, second.astype(F32), 0.0), axis=0)
    states = (jnp.stack(before) + carried[None]).astype(BF16)
    states, cot_c, cot_y1, late = lax.optimization_barrier(
        (states, cot_c, cot_y1, cotangent[TOKENS // 2 :])
    )
    cot_yc1 = lax.ppermute(cot_y1, "c", swap)
    cot_y2 = lax.ppermute(late, "y", swap_y)
    third = exchange(states, ZC)
    key_state, cot_yc1 = lax.optimization_barrier((third.reshape(FEATURES, HEAD), cot_yc1))
    place = (core * 2 + odd).astype(jnp.int32).reshape(1)
    attended, own, give_c, give_y, give_yc = call(
        attend_kernel,
        [SMEM] + [VMEM] * 5,
        [shape((TOKENS, FEATURES), BF16)] + [shape((TOKENS, HEAD), BF16)] * 4,
        (place, queries, keys, values, key_state, scale),
        3 * small,
        scratch_shapes=[pltpu.VMEM((HEADS, TOKENS, HEAD), BF16)],
    )
    late_y = lax.optimization_barrier((cot_y2, attended))[0]
    cot_yc2 = lax.ppermute(late_y, "c", swap)
    got_c = lax.ppermute(give_c, "c", swap)
    got_y = lax.ppermute(give_y, "y", swap_y)
    got_yc = lax.ppermute(give_yc, ("y", "c"), [(i, i ^ 3) for i in range(8)])

    held = [
        pltpu.VMEM((MEMBERS, GROUPS, ROWS, FEATURES), BF16),
        pltpu.SemaphoreType.DMA((CHUNKS,)),
    ]
    gradient, local_grads = call(
        gradient_kernel,
        [HBM, HBM, VMEM, VMEM],
        [shape((TOKENS, FEATURES), BF16), shape((FEATURES, HEAD), BF16)],
        (cotangent, weight, queries, scale),
        large,
        limit=58,
        scratch_shapes=held
        + [pltpu.VMEM((TOKENS, MODEL), BF16), pltpu.SemaphoreType.DMA(())],
    )
    got_c, got_y, got_yc, local_grads, cot_yc2 = lax.optimization_barrier(
        (got_c, got_y, got_yc, local_grads, cot_yc2)
    )
    first = exchange(local_grads.reshape(rows_shape), ZC)
    after, total = sums_before([first[i] for i in reversed(range(MEMBERS))])
    inside = jnp.stack(after[::-1])

    width = SHARE + STATE_ROWS
    steps = 4
    terms = pl.pallas_call(
        weight_kernel,
        grid=(steps,),
        in_specs=[pl.BlockSpec((TOKENS, MODEL // steps), lambda i: (0, i))] * 2
        + [pl.BlockSpec((TOKENS // 2, MODEL // steps), lambda i: (0, i))] * 4
        + [pl.BlockSpec((TOKENS, HEAD), lambda i: (0, 0))] * 4,
        out_specs=pl.BlockSpec((GROUPS // steps, width, HEAD), lambda i: (i, 0, 0)),
        out_shape=shape((GROUPS, width, HEAD), BF16),
        compiler_params=pltpu.CompilerParams(vmem_limit_bytes=32 << 20),
        cost_estimate=pl.CostEstimate(flops=large, bytes_accessed=6 << 20, transcendentals=0),
    )(cotangent, cot_c, cot_y1, cot_y2, cot_yc1, cot_yc2, own, got_c, got_y, got_yc)
    terms = terms.at[:, SHARE:, :].set(total.astype(BF16)[None])
    got = exchange(terms, XY)
    local_args = lax.optimization_barrier((queries, keys, values, gradient, key_state, total))[:5]
    query_gradient, kg_local, vg_local = call(
        local_kernel,
        [VMEM] * 5,
        [shape((TOKENS, FEATURES), BF16)] + [shape((TOKENS, FEATURES), F32)] * 2,
        local_args,
        6 * small,
    )
    mixed_args = lax.optimization_barrier((attended, weight, total))[:2]
    mixed = call(
        mixed_kernel,
        [VMEM, HBM],
        [shape((TOKENS, MODEL), BF16)],
        mixed_args,
        large,
        limit=58,
        scratch_shapes=held,
    )
    got = lax.optimization_barrier((got, mixed, query_gradient))[0]
    back = call(
        reduce_kernel,
        [SMEM, VMEM, VMEM],
        [shape((MEMBERS, 2 * ROWS + STATE_ROWS, HEAD), BF16)],
        (group.astype(jnp.int32).reshape(1), got, inside),
        small,
    )
    last = exchange(back, ZC)
    key_gradient, value_gradient, weight_grad = call(
        final_kernel,
        [VMEM] * 5,
        [shape((TOKENS, FEATURES), BF16)] * 2 + [shape((ROWS, FEATURES), F32)],
        (last, keys, values, kg_local, vg_local),
        2 * small,
    )
    return (mixed, query_gradient, key_gradient, value_gradient, weight_grad)


def solution(mesh):
    grid = Mesh(mesh.devices.reshape(4, 4, 8, 2), ("x", "y", "z", "c"))
    spec = P(("x", "y", "z", "c"), None)
    return jax.shard_map(
        body, mesh=grid, in_specs=(spec,) * 5, out_specs=(spec,) * 5, check_vma=False
    )
```

time: 161 us -> 147 us (0.913)
  waiting for transfers between devices: 62.9 us -> 38.9 us
  Pallas kernels: 0 us -> 18.5 us
  matrix products: 16 us -> 0 us
  starting transfers between devices: 32.6 us -> 39.4 us
  other arithmetic: 5.22 us -> 9.11 us
  local copies, waits for them, and re-layouts: 14 us -> 10.6 us
    all_to_all x6, waiting for transfers between devices: 62.9 us -> 38.9 us  [exchange(): return lax.all_to_all(value, axes, 0, 0, tiled=True)]
    pallas_call x0 -> x8, Pallas kernels: none -> 18.5 us  [the longest x7 14.3 us: call(): pl.pallas_call(kernel, in_specs=ins, out_specs=VMEM if one else [VMEM] *...]
    dot_general x16 -> x0, matrix products: 16 us -> none  [the longest x1 4.65 us: body(): lax.dot_general(attended, full_weight, (((1,), (1,)), ((), ())), preferre...]
    unnamed x10 -> x22, other arithmetic: 0.07 us -> 6.14 us
    reshape x6 -> x0, local copies, waits for them, and re-layouts: 5.39 us -> none  [the longest x1 2.57 us: body(): weight_term.astype(BF16).reshape(groups, model // groups, half)]
    ppermute x2 -> x8, starting transfers between devices: 0.65 us -> 5.84 us  [the longest x1 2.1 us: body(): cot_c = lax.ppermute(cotangent, 'c', swap)]
    concatenate x2 -> x0, other arithmetic: 3.86 us -> none  [the longest x1 3.13 us: body(): second = exchange(jnp.concatenate([weight_term, total], axis=1), XY)]
    transpose x1 -> x0, local copies, waits for them, and re-layouts: 2.65 us -> none  [body(): full_weight = full_weight.transpose(1, 0, 2, 3).reshape(model, features)]
  transfers between devices with their start and end apart: 9 -> 15, of which waited for: 6 -> 5; matrix products, arithmetic and copies ran while one was open for 16% -> 9% of each run, Pallas kernels for 0% -> 12%
where the time goes in v2:
time: 147 us; the launch traced here: 146 us
  starting transfers between devices  39.4 us (27%)
  waiting for transfers between devices  38.9 us (26%)
  Pallas kernels  18.5 us (13%)
  blocking collectives  15.4 us (10%)
  between operations  14.4 us (10%)
  local copies, waits for them, and re-layouts  10.6 us (7%)
  other arithmetic  9.11 us (6%)
    all_to_all x6, waiting for transfers between devices, exchange(): return lax.all_to_all(value, axes, 0, 0, tiled=True)  38.9 us
    all_to_all x6, starting transfers between devices, exchange(): return lax.all_to_all(value, axes, 0, 0, tiled=True)  33.5 us
    all_to_all x1, blocking collectives, exchange(): return lax.all_to_all(value, axes, 0, 0, tiled=True)  15.4 us
    pallas_call x7, Pallas kernels, call(): pl.pallas_call(kernel, in_specs=ins, out_specs=VMEM if one else [VMEM] *...  14.3 us
    unnamed x35, local copies, waits for them, and re-layouts  6.66 us
    unnamed x22, other arithmetic  6.14 us
    pallas_call x1, Pallas kernels, body(): pl.pallas_call(weight_kernel, grid=(steps,), in_specs=[pl.BlockSpec((TOKE...  4.21 us
  transfers between devices with their start and end apart: 15, of which 5 were waited for; matrix products, arithmetic and copies ran while one was open for 9% of the time, Pallas kernels for 12%

profile of v2, /device:TPU:1, one launch (start us, length us, event | category | flops | bytes accessed | tf_op | source)
XLA Modules:
  0.0 146.2 jit_solution(6962149863923090403)
XLA Ops:
  7.2 1.5 %broadcast_in_dim.20 = bf16[16,16,512]{2,1,0:T(8,128)(2,1)} broadcast(bf16[16,512]{1,0:T(8,128)(2,1)} %param.10), dimensions={1,2} | broadcast | bytes 278528 | tf_op jit(solution)/shard_map/broadcast_in_dim | solution.py:227
  8.7 7.6 %all-to-all-start = ((bf16[16,16,512]{2,1,0:T(8,128)(2,1)}), bf16[16,16,512]{2,1,0:T(8,128)(2,1)S(1)}, u32[]{:S(2)}, u32[]{:S(2)}) async-start(bf16[16,16,512]{2,1,0:T(8,128)(2,1)} %broadcast_in_dim.20), calls=%async_computation | async-start | bytes 524288 | tf_op jit(solution)/shard_map/all_to_all | solution.py:200
  16.4 0.9 copy-done.2
  17.3 0.9 copy-done.4
  18.2 0.9 shard_map.92
  19.0 4.7 %all-to-all-done = bf16[16,16,512]{2,1,0:T(8,128)(2,1)S(1)} async-done(((bf16[16,16,512]{2,1,0:T(8,128)(2,1)}), bf16[16,16,512]{2,1,0:T(8,128)(2,1)S(1)}, u32[]{:S(2)}, u32[]{:S(2)}) %all-to-all-start) | async-done | bytes 262176 | tf_op jit(solution)/shard_map/all_to_all | solution.py:200
  23.8 0.7 copy-done.13
  24.5 2.1 %collective-permute-start = (bf16[128,4096]{1,0:T(8,128)(2,1)S(1)}, bf16[128,4096]{1,0:T(8,128)(2,1)S(1)}, u32[]{:S(2)}, u32[]{:S(2)}) collective-permute-start(bf16[128,4096]{1,0:T(8,128)(2,1)S(1)} %copy-done), channel_id=1, source_target_pairs={{0,1},{1,0},{2,3},{3,2},{4,5},{5,4},{6,7},{7,6},{8,9},{9,8},{10,11... | collective-permute-start | bytes 3145736 | tf_op jit(solution)/shard_map/ppermute | solution.py:230
  26.6 8.6 %all-to-all-start.1 = ((bf16[16,32,128]{2,1,0:T(8,128)(2,1)}), bf16[16,32,128]{2,1,0:T(8,128)(2,1)S(1)}, u32[]{:S(2)}, u32[]{:S(2)}) async-start(bf16[16,32,128]{2,1,0:T(8,128)(2,1)} %bitcast.1), calls=%async_computation.1 | async-start | bytes 262144 | tf_op jit(solution)/shard_map/all_to_all | solution.py:200
  35.2 1.0 fusion.4
  36.5 0.6 constant_dynamic-update-slice_fusion.15
  37.1 8.0 %all-to-all-done.1 = bf16[16,32,128]{2,1,0:T(8,128)(2,1)S(1)} async-done(((bf16[16,32,128]{2,1,0:T(8,128)(2,1)}), bf16[16,32,128]{2,1,0:T(8,128)(2,1)S(1)}, u32[]{:S(2)}, u32[]{:S(2)}) %all-to-all-start.1) | async-done | bytes 131104 | tf_op jit(solution)/shard_map/all_to_all | solution.py:200
  45.1 0.6 constant_dynamic-update-slice_fusion.14
  45.7 0.6 fusion.2
  46.3 0.7 broadcast_in_dim.38
  47.0 3.5 %all-to-all-start.2 = ((bf16[16,32,128]{2,1,0:T(8,128)(2,1)}), bf16[16,32,128]{2,1,0:T(8,128)(2,1)S(1)}, u32[]{:S(2)}, u32[]{:S(2)}) async-start(bf16[16,32,128]{2,1,0:T(8,128)(2,1)} %broadcast_in_dim.38), calls=%async_computation.2 | async-start | bytes 262144 | tf_op jit(solution)/shard_map/all_to_all | solution.py:200
  50.5 0.6 constant_dynamic-update-slice_fusion.12
  51.1 0.6 constant_dynamic-update-slice_fusion.11
  51.7 0.6 constant_dynamic-update-slice_fusion.10
  52.3 0.6 constant_dynamic-update-slice_fusion.9
  53.0 0.6 constant_dynamic-update-slice_fusion.8
  53.6 0.6 constant_dynamic-update-slice_fusion.7
  54.2 0.6 constant_dynamic-update-slice_fusion.6
  54.8 0.6 constant_dynamic-update-slice_fusion.5
  55.4 0.6 constant_dynamic-update-slice_fusion.4
  56.0 0.6 constant_dynamic-update-slice_fusion.3
  56.6 0.6 constant_dynamic-update-slice_fusion.2
  57.2 0.6 constant_dynamic-update-slice_fusion.1
  57.8 0.6 constant_dynamic-update-slice_fusion
  58.5 1.6 %add_convert_fusion = bf16[16,32,128]{2,1,0:T(8,128)(2,1)} fusion(f32[16,32,128]{2,1,0:T(8,128)} %constant_dynamic-update-slice_fusion, f32[32,128]{1,0:T(8,128)S(1)} %select_reduce_fusion), kind=kLoop, calls=%fused_computation | loop fusion | flops 131072 | bytes 409600 | tf_op jit(solution)/shard_map/convert_element_type | solution.py:238
  60.1 1.4 collective-permute-start.6
  61.5 4.0 %all-to-all-start.3 = ((bf16[16,32,128]{2,1,0:T(8,128)(2,1)}), bf16[16,32,128]{2,1,0:T(8,128)(2,1)S(1)}, u32[]{:S(2)}, u32[]{:S(2)}) async-start(bf16[16,32,128]{2,1,0:T(8,128)(2,1)} %add_convert_fusion), calls=%async_computation.3 | async-start | bytes 262144 | tf_op jit(solution)/shard_map/all_to_all | solution.py:200
  65.5 9.2 %all-to-all-done.3 = bf16[16,32,128]{2,1,0:T(8,128)(2,1)S(1)} async-done(((bf16[16,32,128]{2,1,0:T(8,128)(2,1)}), bf16[16,32,128]{2,1,0:T(8,128)(2,1)S(1)}, u32[]{:S(2)}, u32[]{:S(2)}) %all-to-all-start.3) | async-done | bytes 131104 | tf_op jit(solution)/shard_map/all_to_all | solution.py:200
  75.2 0.6 copy-done.12
  75.8 0.5 collective-permute-start.3
  76.5 1.4 collective-permute-start.5
  78.0 5.2 %shard_map.94 = (bf16[128,512]{1,0:T(8,128)(2,1)}, bf16[512,128]{1,0:T(8,128)(2,1)}) custom-call(bf16[128,4096]{1,0:T(8,128)(2,1)} %c0.1, bf16[16,16,16,512]{3,2,1,0:T(8,128)(2,1)} %bitcast.18, bf16[128,512]{1,0:T(8,128)(2,1)} %q.4, f32[128,1]{1,0:T(8,128)} %copy-done.8), custom_call_target="tpu_custom_call" | custom-call | flops 536870912 | bytes 5636608 | tf_op jit(solution)/shard_map/pallas_call | solution.py:45
  83.2 3.6 %all-to-all-start.4 = ((bf16[16,32,128]{2,1,0:T(8,128)(2,1)}), bf16[16,32,128]{2,1,0:T(8,128)(2,1)S(1)}, u32[]{:S(2)}, u32[]{:S(2)}) async-start(bf16[16,32,128]{2,1,0:T(8,128)(2,1)} %bitcast.20), calls=%async_computation.4 | async-start | bytes 262144 | tf_op jit(solution)/shard_map/all_to_all | solution.py:200
  86.8 1.0 copy-done.10
  87.8 4.2 %shard_map.97 = bf16[16,288,128]{2,1,0:T(8,128)(2,1)} custom-call(bf16[128,4096]{1,0:T(8,128)(2,1)S(1)} %copy-done.1, bf16[128,4096]{1,0:T(8,128)(2,1)S(1)} %collective-permute-done.c1, bf16[64,4096]{1,0:T(8,128)(2,1)S(1)} %collective-permute-done.1.c2, bf16[64,4096]{1,0:T(8,128)(2,1)} %collective-permute-done.6.c3, bf16[64,4096]{1,0:T(8,128)(2,1)S(1)} %copy-done.10, ...), custom_call_target="tpu_custom_call" | custom-call | flops 536870912 | bytes 6291456 | tf_op jit(solution)/shard_map/pallas_call | solution.py:284
  92.0 4.0 %all-to-all-done.4 = bf16[16,32,128]{2,1,0:T(8,128)(2,1)S(1)} async-done(((bf16[16,32,128]{2,1,0:T(8,128)(2,1)}), bf16[16,32,128]{2,1,0:T(8,128)(2,1)S(1)}, u32[]{:S(2)}, u32[]{:S(2)}) %all-to-all-start.4) | async-done | bytes 131104 | tf_op jit(solution)/shard_map/all_to_all | solution.py:200
  96.1 0.7 broadcast_dynamic-update-slice_fusion
  96.8 6.2 %all-to-all-start.5 = ((bf16[16,288,128]{2,1,0:T(8,128)(2,1)}), bf16[16,288,128]{2,1,0:T(8,128)(2,1)S(1)}, u32[]{:S(2)}, u32[]{:S(2)}) async-start(bf16[16,288,128]{2,1,0:T(8,128)(2,1)} %broadcast_dynamic-update-slice_fusion), calls=%async_computation.5 | async-start | bytes 2359296 | tf_op jit(solution)/shard_map/all_to_all | solution.py:200
  103.1 5.1 %shard_map.95 = bf16[128,4096]{1,0:T(8,128)(2,1)} custom-call(bf16[128,512]{1,0:T(8,128)(2,1)} %copy-done.12, bf16[16,16,16,512]{3,2,1,0:T(8,128)(2,1)} %bitcast.19), custom_call_target="tpu_custom_call" | custom-call | flops 536870912 | bytes 5373952 | tf_op jit(solution)/shard_map/pallas_call | solution.py:45
  108.2 1.5 %shard_map.96 = (bf16[128,512]{1,0:T(8,128)(2,1)}, f32[128,512]{1,0:T(8,128)S(1)}, f32[128,512]{1,0:T(8,128)S(1)}) custom-call(bf16[128,512]{1,0:T(8,128)(2,1)S(1)} %copy-done.7, bf16[128,512]{1,0:T(8,128)(2,1)S(1)} %copy-done.3, bf16[128,512]{1,0:T(8,128)(2,1)S(1)} %copy-done.5, bf16[128,512]{1,0:T(8,128)(2,1)S(1)} %copy-done.11, bf16[512,128]{1,0:T(8,128)(2,1)S(1)} %bitcast.17), custom_call_target="tpu_custom_call" | custom-call | flops 100663296 | bytes 1310720 | tf_op jit(solution)/shard_map/pallas_call | solution.py:45
  109.9 13.0 %all-to-all-done.5.got = bf16[16,288,128]{2,1,0:T(8,128)(2,1)S(1)} async-done(((bf16[16,288,128]{2,1,0:T(8,128)(2,1)}), bf16[16,288,128]{2,1,0:T(8,128)(2,1)S(1)}, u32[]{:S(2)}, u32[]{:S(2)}) %all-to-all-start.5) | async-done | bytes 1179680 | tf_op jit(solution)/shard_map/all_to_all | solution.py:200
  123.0 15.4 %all_to_all.35.got = bf16[16,64,128]{2,1,0:T(8,128)(2,1)S(1)} all-to-all(bf16[16,64,128]{2,1,0:T(8,128)(2,1)S(1)} %shard_map.98), channel_id=1, replica_groups=mesh['x'=4,'y'=4,'z'=8,'c'=2] {'z','c'}, dimensions={0} | all-to-all | bytes 524288 | tf_op jit(solution)/shard_map/all_to_all | solution.py:200
  138.4 1.0 shard_map.99
  (60 shorter events, 1.4 us)
Async XLA Ops:
  7.2 17.3 %copy-start = (bf16[128,4096]{1,0:T(8,128)(2,1)S(1)}, bf16[128,4096]{1,0:T(8,128)(2,1)}, u32[]{:S(2)}) copy-start(bf16[128,4096]{1,0:T(8,128)(2,1)} %c0.1) | copy-start | bytes 3145732
  8.7 15.0 %all-to-all-start = ((bf16[16,16,512]{2,1,0:T(8,128)(2,1)}), bf16[16,16,512]{2,1,0:T(8,128)(2,1)S(1)}, u32[]{:S(2)}, u32[]{:S(2)}) async-start(bf16[16,16,512]{2,1,0:T(8,128)(2,1)} %broadcast_in_dim.20), calls=%async_computation | async-start | bytes 524288 | tf_op jit(solution)/shard_map/all_to_all | solution.py:200
  16.3 61.7 %all-gather.3.cloned.1.call-start = ((), (), s32[]{:S(2)}) async-start(), calls=%async_computation.7 | async-start | bytes 4456448 | tf_op jit(solution)/shard_map/all_gather | solution.py:229
  16.4 0.9 copy-start.2
  17.3 0.9 copy-start.4
  23.8 0.7 copy-start.13
  24.5 35.6 %collective-permute-start = (bf16[128,4096]{1,0:T(8,128)(2,1)S(1)}, bf16[128,4096]{1,0:T(8,128)(2,1)S(1)}, u32[]{:S(2)}, u32[]{:S(2)}) collective-permute-start(bf16[128,4096]{1,0:T(8,128)(2,1)S(1)} %copy-done), channel_id=1, source_target_pairs={{0,1},{1,0},{2,3},{3,2},{4,5},{5,4},{6,7},{7,6},{8,9},{9,8},{10,11... | collective-permute-start | bytes 3145736 | tf_op jit(solution)/shard_map/ppermute | solution.py:230
  26.6 18.5 %all-to-all-start.1 = ((bf16[16,32,128]{2,1,0:T(8,128)(2,1)}), bf16[16,32,128]{2,1,0:T(8,128)(2,1)S(1)}, u32[]{:S(2)}, u32[]{:S(2)}) async-start(bf16[16,32,128]{2,1,0:T(8,128)(2,1)} %bitcast.1), calls=%async_computation.1 | async-start | bytes 262144 | tf_op jit(solution)/shard_map/all_to_all | solution.py:200
  36.2 38.5 %copy-start.3 = (bf16[128,512]{1,0:T(8,128)(2,1)S(1)}, bf16[128,512]{1,0:T(8,128)(2,1)}, u32[]{:S(2)}) copy-start(bf16[128,512]{1,0:T(8,128)(2,1)} %k.6) | copy-start | bytes 393220
  36.2 38.5 %copy-start.5 = (bf16[128,512]{1,0:T(8,128)(2,1)S(1)}, bf16[128,512]{1,0:T(8,128)(2,1)}, u32[]{:S(2)}) copy-start(bf16[128,512]{1,0:T(8,128)(2,1)} %v.6) | copy-start | bytes 393220
  36.2 38.5 %copy-start.6 = (bf16[128,512]{1,0:T(8,128)(2,1)S(1)}, bf16[128,512]{1,0:T(8,128)(2,1)}, u32[]{:S(2)}) copy-start(bf16[128,512]{1,0:T(8,128)(2,1)} %q.4) | copy-start | bytes 393220
  36.2 23.9 %collective-permute-start.1 = (bf16[64,4096]{1,0:T(8,128)(2,1)}, bf16[64,4096]{1,0:T(8,128)(2,1)S(1)}, u32[]{:S(2)}, u32[]{:S(2)}) collective-permute-start(bf16[64,4096]{1,0:T(8,128)(2,1)} %get-tuple-element.96), channel_id=1, source_target_pairs={{0,16},{16,0},{32,48},{48,32},{1,17},{17,1},{33,49},{49,33},{2,18}... | collective-permute-start | bytes 1572872 | tf_op jit(solution)/shard_map/ppermute | solution.py:231
  47.0 11.4 %all-to-all-start.2 = ((bf16[16,32,128]{2,1,0:T(8,128)(2,1)}), bf16[16,32,128]{2,1,0:T(8,128)(2,1)S(1)}, u32[]{:S(2)}, u32[]{:S(2)}) async-start(bf16[16,32,128]{2,1,0:T(8,128)(2,1)} %broadcast_in_dim.38), calls=%async_computation.2 | async-start | bytes 262144 | tf_op jit(solution)/shard_map/all_to_all | solution.py:200
  60.1 14.6 %collective-permute-start.2 = (bf16[64,4096]{1,0:T(8,128)(2,1)S(1)}, bf16[64,4096]{1,0:T(8,128)(2,1)S(1)}, u32[]{:S(2)}, u32[]{:S(2)}) collective-permute-start(bf16[64,4096]{1,0:T(8,128)(2,1)S(1)} %collective-permute-done.1.c2), channel_id=1, source_target_pairs={{0,1},{1,0},{2,3},{3,2},{4,5},{5,4},{6,7},{7,6},{8,9},{9,8},{10,11... | collective-permute-start | bytes 1572872 | tf_op jit(solution)/shard_map/ppermute | solution.py:242
  60.1 15.7 %collective-permute-start.6 = (bf16[64,4096]{1,0:T(8,128)(2,1)}, bf16[64,4096]{1,0:T(8,128)(2,1)}, u32[]{:S(2)}, u32[]{:S(2)}) collective-permute-start(bf16[64,4096]{1,0:T(8,128)(2,1)} %get-tuple-element.62), channel_id=1, source_target_pairs={{0,16},{16,0},{32,48},{48,32},{1,17},{17,1},{33,49},{49,33},{2,18}... | collective-permute-start | bytes 1572872 | tf_op jit(solution)/shard_map/ppermute | solution.py:243
  61.5 13.2 %all-to-all-start.3 = ((bf16[16,32,128]{2,1,0:T(8,128)(2,1)}), bf16[16,32,128]{2,1,0:T(8,128)(2,1)S(1)}, u32[]{:S(2)}, u32[]{:S(2)}) async-start(bf16[16,32,128]{2,1,0:T(8,128)(2,1)} %add_convert_fusion), calls=%async_computation.3 | async-start | bytes 262144 | tf_op jit(solution)/shard_map/all_to_all | solution.py:200
  65.5 12.5 %copy-start.8 = (f32[128,1]{1,0:T(8,128)}, f32[128,1]{1,0:T(8,128)S(1)}, u32[]{:S(2)}) copy-start(f32[128,1]{1,0:T(8,128)S(1)} %multiply_rsqrt_fusion.scale) | copy-start | bytes 1540
  74.7 3.3 %copy-start.9 = (bf16[64,4096]{1,0:T(8,128)(2,1)}, bf16[64,4096]{1,0:T(8,128)(2,1)S(1)}, u32[]{:S(2)}) copy-start(bf16[64,4096]{1,0:T(8,128)(2,1)S(1)} %collective-permute-done.2.c4) | copy-start | bytes 1572868
  75.2 0.7 copy-start.12
  75.8 7.4 %collective-permute-start.7 = (bf16[64,4096]{1,0:T(8,128)(2,1)}, bf16[64,4096]{1,0:T(8,128)(2,1)}, u32[]{:S(2)}, u32[]{:S(2)}) collective-permute-start(bf16[64,4096]{1,0:T(8,128)(2,1)} %collective-permute-done.6.c3), channel_id=1, source_target_pairs={{0,1},{1,0},{2,3},{3,2},{4,5},{5,4},{6,7},{7,6},{8,9},{9,8},{10,11... | collective-permute-start | bytes 1572872 | tf_op jit(solution)/shard_map/ppermute | solution.py:256
  75.8 7.4 %collective-permute-start.3 = (bf16[128,128]{1,0:T(8,128)(2,1)S(1)}, bf16[128,128]{1,0:T(8,128)(2,1)S(1)}, u32[]{:S(2)}, u32[]{:S(2)}) collective-permute-start(bf16[128,128]{1,0:T(8,128)(2,1)S(1)} %get-tuple-element.58), channel_id=1, source_target_pairs={{0,1},{1,0},{2,3},{3,2},{4,5},{5,4},{6,7},{7,6},{8,9},{9,8},{10,11... | collective-permute-start | bytes 98312 | tf_op jit(solution)/shard_map/ppermute | solution.py:257
  76.3 6.9 %collective-permute-start.4 = (bf16[128,128]{1,0:T(8,128)(2,1)S(1)}, bf16[128,128]{1,0:T(8,128)(2,1)S(1)}, u32[]{:S(2)}, u32[]{:S(2)}) collective-permute-start(bf16[128,128]{1,0:T(8,128)(2,1)S(1)} %get-tuple-element.59), channel_id=1, source_target_pairs={{0,16},{16,0},{32,48},{48,32},{1,17},{17,1},{33,49},{49,33},{2,18}... | collective-permute-start | bytes 98312 | tf_op jit(solution)/shard_map/ppermute | solution.py:258
  76.5 6.7 %collective-permute-start.5 = (bf16[128,128]{1,0:T(8,128)(2,1)S(1)}, bf16[128,128]{1,0:T(8,128)(2,1)S(1)}, u32[]{:S(2)}, u32[]{:S(2)}) collective-permute-start(bf16[128,128]{1,0:T(8,128)(2,1)S(1)} %get-tuple-element.60), channel_id=1, source_target_pairs={{0,17},{1,16},{16,1},{17,0},{32,49},{33,48},{48,33},{49,32},{2,19}... | collective-permute-start | bytes 98312 | tf_op jit(solution)/shard_map/ppermute | solution.py:259
  78.0 8.8 %copy-start.1 = (bf16[128,4096]{1,0:T(8,128)(2,1)S(1)}, bf16[128,4096]{1,0:T(8,128)(2,1)}, u32[]{:S(2)}) copy-start(bf16[128,4096]{1,0:T(8,128)(2,1)} %c0.1) | copy-start | bytes 3145732
  83.2 12.8 %all-to-all-start.4 = ((bf16[16,32,128]{2,1,0:T(8,128)(2,1)}), bf16[16,32,128]{2,1,0:T(8,128)(2,1)S(1)}, u32[]{:S(2)}, u32[]{:S(2)}) async-start(bf16[16,32,128]{2,1,0:T(8,128)(2,1)} %bitcast.20), calls=%async_computation.4 | async-start | bytes 262144 | tf_op jit(solution)/shard_map/all_to_all | solution.py:200
  86.8 1.0 copy-start.10
  96.8 26.0 %all-to-all-start.5 = ((bf16[16,288,128]{2,1,0:T(8,128)(2,1)}), bf16[16,288,128]{2,1,0:T(8,128)(2,1)S(1)}, u32[]{:S(2)}, u32[]{:S(2)}) async-start(bf16[16,288,128]{2,1,0:T(8,128)(2,1)} %broadcast_dynamic-update-slice_fusion), calls=%async_computation.5 | async-start | bytes 2359296 | tf_op jit(solution)/shard_map/all_to_all | solution.py:200
  103.1 5.1 %copy-start.7 = (bf16[128,512]{1,0:T(8,128)(2,1)S(1)}, bf16[128,512]{1,0:T(8,128)(2,1)}, u32[]{:S(2)}) copy-start(bf16[128,512]{1,0:T(8,128)(2,1)} %q.4) | copy-start | bytes 393220
  103.1 5.1 %copy-start.11 = (bf16[128,512]{1,0:T(8,128)(2,1)S(1)}, bf16[128,512]{1,0:T(8,128)(2,1)}, u32[]{:S(2)}) copy-start(bf16[128,512]{1,0:T(8,128)(2,1)} %get-tuple-element.71.g) | copy-start | bytes 393220
Sparse Core Ops, SparseCore 0:
  24.6 44.5 all-gather.2

commit v3 on v2

v3 whole, which is shorter than its diff:
```python
import jax
import jax.numpy as jnp
from jax import lax
from jax.experimental import pallas as pl
from jax.experimental.pallas import tpu as pltpu
from jax.sharding import Mesh, PartitionSpec as P

HEADS = 4
HEAD = 128
TOKENS = 128
FEATURES = HEADS * HEAD
MODEL = 4096
GROUPS = 16
MEMBERS = 16
ROWS = MODEL // (GROUPS * MEMBERS)
SHARE = MODEL // GROUPS
STATE_ROWS = FEATURES // MEMBERS
CHUNKS = 4
LIMIT = 63_000_000
ROOM = 32_000_000
SLICE = HEAD // MEMBERS
FLIPS = (0, 2, 1, 3)
XY = ("x", "y")
ZC = ("z", "c")
BF16 = jnp.bfloat16
F32 = jnp.float32
NN = (((1,), (0,)), ((), ()))
NT = (((1,), (1,)), ((), ()))
TN = (((0,), (0,)), ((), ()))
VMEM = pl.BlockSpec(memory_space=pltpu.VMEM)
SMEM = pl.BlockSpec(memory_space=pltpu.SMEM)
HBM = pl.BlockSpec(memory_space=pltpu.HBM)


def mul(a, b, dims):
    return lax.dot_general(a, b, dims, preferred_element_type=F32)


def shape(dims, dtype):
    return jax.ShapeDtypeStruct(dims, dtype)


def call(kernel, ins, outs, args, flops, limit=LIMIT, **kw):
    out_bytes = sum(o.size * o.dtype.itemsize for o in outs)
    in_bytes = sum(a.size * a.dtype.itemsize for a in args)
    one = len(outs) == 1
    return pl.pallas_call(
        kernel,
        in_specs=ins,
        out_specs=VMEM if one else [VMEM] * len(outs),
        out_shape=outs[0] if one else outs,
        compiler_params=pltpu.CompilerParams(vmem_limit_bytes=limit),
        cost_estimate=pl.CostEstimate(
            flops=flops, bytes_accessed=in_bytes + out_bytes, transcendentals=0
        ),
        **kw,
    )(*args)


def head(ref, h):
    return ref[:, h * HEAD : (h + 1) * HEAD]


def state(ref, h):
    return ref[h * HEAD : (h + 1) * HEAD, :]


def scale_from(first):
    token = first + lax.broadcasted_iota(jnp.int32, (TOKENS, HEAD), 0)
    return lax.rsqrt((HEAD * (token + 1)).astype(F32))


def causal(x):
    row = lax.broadcasted_iota(jnp.int32, x.shape, 0)
    col = lax.broadcasted_iota(jnp.int32, x.shape, 1)
    return jnp.where(row >= col, x, 0.0).astype(BF16)


def keys_kernel(me, k, v, w, q, out, q0, q1, q2, q3):
    for h in range(HEADS):
        product = mul(head(k, h), head(v, h), TN).astype(BF16)
        for i in range(HEAD // STATE_ROWS):
            at = slice(i * STATE_ROWS, (i + 1) * STATE_ROWS)
            out[h * (HEAD // STATE_ROWS) + i, :STATE_ROWS, :] = product[at]
    for m in range(MEMBERS):
        out[m, STATE_ROWS:, :] = head(w, head_of(m))
    for flip, ref in zip(FLIPS, (q0, q1, q2, q3)):
        ref[...] = q[:, head_at(me[0] ^ flip)]


def head_of(m):
    return (m % 2) * 2 + (m % 4) // 2


def head_at(h):
    return pl.ds(pl.multiple_of(h * HEAD, HEAD), HEAD)


def before_kernel(first, inside, send):
    running = jnp.zeros((STATE_ROWS, HEAD), F32)
    rows = []
    for m in range(MEMBERS):
        inside[m] = running
        running = running + first[m, :STATE_ROWS, :].astype(F32)
        rows.append(first[m, STATE_ROWS:, :])
    packed = jnp.concatenate([running.astype(BF16)] + rows, axis=0)
    for j in range(GROUPS):
        send[j] = packed


def carry_kernel(group, second, inside, out):
    carried = jnp.zeros((STATE_ROWS, HEAD), F32)
    for j in range(GROUPS):
        piece = second[j, :STATE_ROWS, :].astype(F32)
        carried = carried + jnp.where(j < group[0], piece, 0.0)
    for m in range(MEMBERS):
        out[m] = (inside[m] + carried).astype(BF16)


def attend_kernel(me, base, q, k, v, key_state, out, a0, a1, a2, a3, by_head):
    scale = scale_from(base[0] + base[1] * TOKENS)
    for h in range(HEADS):
        qh = head(q, h)
        scores = causal(mul(qh, head(k, h), NT))
        total = mul(scores, head(v, h), NN) + mul(qh, state(key_state, h), NN)
        result = (total * scale).astype(BF16)
        out[:, h * HEAD : (h + 1) * HEAD] = result
        by_head[h] = result
    for flip, ref in zip(FLIPS, (a0, a1, a2, a3)):
        ref[...] = by_head[me[0] ^ flip]


def gradient_kernel(base, c0, c1, c2, c3, w, q0, q1, q2, q3, g0, g1, g2, g3, out, total):
    step = pl.program_id(0)
    left = jnp.concatenate([c[...] for c in (c0, c1, c2, c3)], axis=0)
    rows = [w[j, STATE_ROWS:, :] for j in range(GROUPS // CHUNKS)]
    term = mul(left, jnp.concatenate(rows, axis=0), NN)

    @pl.when(step == 0)
    def _():
        total[...] = term

    @pl.when(step > 0)
    def _():
        total[...] += term

    @pl.when(step == CHUNKS - 1)
    def _():
        sums = []
        for i, (q, g) in enumerate(zip((q0, q1, q2, q3), (g0, g1, g2, g3))):
            scale = scale_from(base[0] + (base[1] ^ i) * TOKENS)
            value = (total[i * TOKENS : (i + 1) * TOKENS] * scale).astype(BF16)
            g[...] = value
            sums.append(mul(q[...], value, TN))
        for m in range(MEMBERS):
            at = slice(m * SLICE, (m + 1) * SLICE)
            out[m] = jnp.concatenate([x[at] for x in sums], axis=0).astype(BF16)


def after_kernel(first, inside, total):
    pieces = [first[m].astype(F32) for m in range(MEMBERS)]
    running = jnp.zeros((STATE_ROWS, HEAD), F32)
    for block in reversed(range(MEMBERS)):
        quad, local = block // 4, block % 4
        inside[block] = running
        rows = []
        for h in range(HEADS):
            place = (h % 2) * 2 + h // 2
            at = (place ^ local) * SLICE
            rows.append(pieces[quad * 4 + place][at : at + SLICE])
        running = running + jnp.concatenate(rows, axis=0)
    total[...] = running.astype(BF16)


def mixed_kernel(me, att, w0, w1, w2, w3, out):
    left = jnp.concatenate([att[:, head_at(me[0] ^ flip)] for flip in FLIPS], axis=1)
    for j in range(GROUPS):
        right = jnp.concatenate([w[j, STATE_ROWS:, :] for w in (w0, w1, w2, w3)], axis=1)
        out[:, j * SHARE : (j + 1) * SHARE] = mul(left, right, NT).astype(BF16)


def weight_kernel(c0, c1, c2, c3, a0, a1, a2, a3, out):
    turned = jnp.concatenate([a[...].T for a in (a0, a1, a2, a3)], axis=1)
    for j in range(out.shape[0]):
        at = slice(j * SHARE, (j + 1) * SHARE)
        cots = jnp.concatenate([c[:, at] for c in (c0, c1, c2, c3)], axis=0)
        term = mul(turned, cots, NN).astype(BF16)
        for half in range(2):
            out[j, half * HEAD : (half + 1) * HEAD, :] = term[:, half * HEAD : (half + 1) * HEAD]
        out[j, SHARE:, :] = jnp.zeros((STATE_ROWS, HEAD), BF16)


def local_kernel(me, q, k, v, g0, g1, g2, g3, key_state, qg, kg, vg, by_head):
    for flip, ref in zip(FLIPS, (g0, g1, g2, g3)):
        by_head[me[0] ^ flip] = ref[...]
    for h in range(HEADS):
        at = slice(h * HEAD, (h + 1) * HEAD)
        qh, kh, vh, gh = head(q, h), head(k, h), head(v, h), by_head[h]
        scores = causal(mul(qh, kh, NT))
        grads = causal(mul(gh, vh, NT))
        qg[:, at] = (mul(grads, kh, NN) + mul(gh, state(key_state, h), NT)).astype(BF16)
        kg[:, at] = mul(grads, qh, TN)
        vg[:, at] = mul(scores, gh, TN)


def reduce_kernel(group, got, inside, out):
    after = jnp.zeros((STATE_ROWS, HEAD), F32)
    for j in range(GROUPS):
        piece = got[j, SHARE:, :].astype(F32)
        after = after + jnp.where(j > group[0], piece, 0.0)
    for m in range(MEMBERS):
        out[m, ROWS:, :] = (inside[m] + after).astype(BF16)
    per = HEAD // ROWS
    for half in range(2):
        total = None
        for j in range(GROUPS):
            piece = got[j, half * HEAD : (half + 1) * HEAD, :].astype(F32)
            total = piece if total is None else total + piece
        turned = total.T.astype(BF16)
        for m in range(per):
            out[half * per + m, :ROWS, :] = turned[m * ROWS : (m + 1) * ROWS]


def final_kernel(got, k, v, kg_local, vg_local, kg, vg, wg):
    states = [got[m, ROWS:, :].astype(F32) for m in range(MEMBERS)]
    for h in range(HEADS):
        at = slice(h * HEAD, (h + 1) * HEAD)
        rows = [x[h * SLICE : (h + 1) * SLICE] for x in states]
        grad_state = jnp.concatenate(rows, axis=0).astype(BF16)
        kg[:, at] = (kg_local[:, at] + mul(head(v, h), grad_state, NT)).astype(BF16)
        vg[:, at] = (vg_local[:, at] + mul(head(k, h), grad_state, NN)).astype(BF16)
        total = None
        for quad in range(MEMBERS // 4):
            piece = got[quad * 4 + (h % 2) * 2 + h // 2, :ROWS, :].astype(F32)
            total = piece if total is None else total + piece
        wg[:, at] = total


def exchange(value, axes):
    return lax.all_to_all(value, axes, 0, 0, tiled=True)


def body(queries, keys, values, out_weight, cotangent):
    group = lax.axis_index(XY).astype(jnp.int32)
    member = lax.axis_index(ZC)
    core = lax.axis_index("c")
    odd = lax.rem(lax.axis_index("z"), 2)
    me = (core * 2 + odd).astype(jnp.int32).reshape(1)
    group_id = group.reshape(1)

    base = jnp.stack([group * MEMBERS * TOKENS, member.astype(jnp.int32)])

    def to_core(x):
        return lax.ppermute(x, "c", [(0, 1), (1, 0)])

    def to_odd(x):
        return lax.ppermute(x, "z", [(i, i ^ 1) for i in range(8)])

    def to_both(x):
        return lax.ppermute(x, ZC, [(i, i ^ 3) for i in range(MEMBERS)])

    head_block = shape((TOKENS, HEAD), BF16)
    small = 2 * TOKENS * HEAD * FEATURES
    large = 2 * TOKENS * MODEL * FEATURES
    by_head = [pltpu.VMEM((HEADS, TOKENS, HEAD), BF16)]

    sent, q0, q1, q2, q3 = call(
        keys_kernel,
        [SMEM] + [VMEM] * 4,
        [shape((MEMBERS, STATE_ROWS + ROWS, HEAD), BF16)] + [head_block] * 4,
        (me, keys, values, out_weight, queries),
        small,
    )
    first = exchange(sent, ZC)
    cot_c = to_core(cotangent)
    q1, q2, q3 = to_core(q1), to_odd(q2), to_both(q3)
    inside, sent = call(
        before_kernel,
        [VMEM],
        [
            shape((MEMBERS, STATE_ROWS, HEAD), F32),
            shape((GROUPS, STATE_ROWS + SHARE, HEAD), BF16),
        ],
        (first,),
        small,
        limit=ROOM,
    )
    sent, cot_c, q1, q2, q3, late = lax.optimization_barrier((sent, cot_c, q1, q2, q3, cotangent))
    cot_z = to_odd(late)
    second = exchange(sent, XY)
    cot_zc = to_core(cot_z)
    states = call(
        carry_kernel,
        [SMEM, VMEM, VMEM],
        [shape((MEMBERS, STATE_ROWS, HEAD), BF16)],
        (group_id, second, inside),
        small,
        limit=ROOM,
    )
    third = exchange(states, ZC)
    key_state = third.reshape(FEATURES, HEAD)
    wide = pl.BlockSpec((TOKENS, MODEL // CHUNKS), lambda i: (0, i))
    whole = pl.BlockSpec((TOKENS, HEAD), lambda i: (0, 0))
    g0, g1, g2, g3, sent = pl.pallas_call(
        gradient_kernel,
        grid=(CHUNKS,),
        in_specs=[SMEM]
        + [wide] * 4
        + [pl.BlockSpec((GROUPS // CHUNKS, STATE_ROWS + SHARE, HEAD), lambda i: (i, 0, 0))]
        + [whole] * 4,
        out_specs=[whole] * 4
        + [pl.BlockSpec((MEMBERS, STATE_ROWS, HEAD), lambda i: (0, 0, 0))],
        out_shape=[head_block] * 4 + [shape((MEMBERS, STATE_ROWS, HEAD), BF16)],
        scratch_shapes=[pltpu.VMEM((4 * TOKENS, HEAD), F32)],
        compiler_params=pltpu.CompilerParams(vmem_limit_bytes=LIMIT),
        cost_estimate=pl.CostEstimate(flops=large, bytes_accessed=6 << 20, transcendentals=0),
    )(base, cotangent, cot_c, cot_z, cot_zc, second, q0, q1, q2, q3)
    key_state, sent, g0 = lax.optimization_barrier((key_state, sent, g0))
    attended, a0, a1, a2, a3 = call(
        attend_kernel,
        [SMEM] * 2 + [VMEM] * 4,
        [shape((TOKENS, FEATURES), BF16)] + [head_block] * 4,
        (me, base, queries, keys, values, key_state),
        3 * small,
        scratch_shapes=by_head,
    )
    a1, a2, a3 = to_core(a1), to_odd(a2), to_both(a3)
    g1, g2, g3 = to_core(g1), to_odd(g2), to_both(g3)
    fourth = exchange(sent, ZC)
    width = SHARE + STATE_ROWS
    terms = pl.pallas_call(
        weight_kernel,
        grid=(CHUNKS,),
        in_specs=[wide] * 4 + [whole] * 4,
        out_specs=pl.BlockSpec((GROUPS // CHUNKS, width, HEAD), lambda i: (i, 0, 0)),
        out_shape=shape((GROUPS, width, HEAD), BF16),
        compiler_params=pltpu.CompilerParams(vmem_limit_bytes=LIMIT),
        cost_estimate=pl.CostEstimate(flops=large, bytes_accessed=6 << 20, transcendentals=0),
    )(cotangent, cot_c, cot_z, cot_zc, a0, a1, a2, a3)
    fourth, terms, g1, g2, g3 = lax.optimization_barrier((fourth, terms, g1, g2, g3))
    inside, total = call(
        after_kernel,
        [VMEM],
        [shape((MEMBERS, STATE_ROWS, HEAD), F32), shape((STATE_ROWS, HEAD), BF16)],
        (fourth,),
        small,
        limit=ROOM,
    )
    terms = terms.at[:, SHARE:, :].set(total[None])
    got = exchange(terms, XY)

    w0, g0, attended = lax.optimization_barrier((second, g0, attended, total, a1, a2, a3))[:3]
    w1, w2 = to_core(w0), to_odd(w0)
    query_gradient, kg_local, vg_local = call(
        local_kernel,
        [SMEM] + [VMEM] * 8,
        [shape((TOKENS, FEATURES), BF16)] + [shape((TOKENS, FEATURES), F32)] * 2,
        (me, queries, keys, values, g0, g1, g2, g3, key_state),
        6 * small,
        scratch_shapes=by_head,
    )
    got = lax.optimization_barrier((got, query_gradient))[0]
    back = call(
        reduce_kernel,
        [SMEM, VMEM, VMEM],
        [shape((MEMBERS, ROWS + STATE_ROWS, HEAD), BF16)],
        (group_id, got, inside),
        small,
        limit=ROOM,
    )
    back, w2 = lax.optimization_barrier((back, w2))
    w3 = to_core(w2)
    last = exchange(back, ZC)
    mixed = call(
        mixed_kernel,
        [SMEM] + [VMEM] * 5,
        [shape((TOKENS, MODEL), BF16)],
        (me, attended, w0, w1, w2, w3),
        large,
    )
    last, mixed = lax.optimization_barrier((last, mixed))
    key_gradient, value_gradient, weight_grad = call(
        final_kernel,
        [VMEM] * 5,
        [shape((TOKENS, FEATURES), BF16)] * 2 + [shape((ROWS, FEATURES), F32)],
        (last, keys, values, kg_local, vg_local),
        2 * small,
        limit=ROOM,
    )
    return (mixed, query_gradient, key_gradient, value_gradient, weight_grad)


def solution(mesh):
    grid = Mesh(mesh.devices.reshape(4, 4, 8, 2), ("x", "y", "z", "c"))
    spec = P(("x", "y", "z", "c"), None)
    return jax.shard_map(
        body, mesh=grid, in_specs=(spec,) * 5, out_specs=(spec,) * 5, check_vma=False
    )
```

time: 147 us -> 131 us (0.89)
  blocking collectives: 15.4 us -> 0 us
  waiting for transfers between devices: 38.9 us -> 53.9 us
  between operations: 14.4 us -> 0.87 us
  other arithmetic: 9.11 us -> 0.58 us
  Pallas kernels: 18.5 us -> 25.6 us
  local copies, waits for them, and re-layouts: 10.6 us -> 4.2 us
  starting transfers between devices: 39.4 us -> 44.9 us
    ppermute x8 -> x15, waiting for transfers between devices: 0.02 us -> 23.5 us  [the longest x5 21.8 us: to_odd(): return lax.ppermute(x, 'z', [(i, i ^ 1) for i in range(8)])]
    all_to_all x1 -> x0, blocking collectives: 15.4 us -> none  [exchange(): return lax.all_to_all(value, axes, 0, 0, tiled=True)]
    all_to_all x6, waiting for transfers between devices: 38.9 us -> 30.5 us  [exchange(): return lax.all_to_all(value, axes, 0, 0, tiled=True)]
    ppermute x8 -> x15, starting transfers between devices: 5.84 us -> 12 us  [the longest x5 5.3 us: to_odd(): return lax.ppermute(x, 'z', [(i, i ^ 1) for i in range(8)])]
    unnamed x22 -> x0, other arithmetic: 6.14 us -> none
    pallas_call x1 -> x2, Pallas kernels: 4.21 us -> 9.91 us  [the longest x1 5.24 us: body(): pl.pallas_call(gradient_kernel, grid=(CHUNKS,), in_specs=[SMEM] + [wide]...]
    unnamed x35 -> x40, local copies, waits for them, and re-layouts: 6.66 us -> 3.5 us
    broadcast_in_dim x2 -> x0, local copies, waits for them, and re-layouts: 2.21 us -> none  [the longest x1 1.53 us: body(): jnp.broadcast_to(out_weight[None], (GROUPS, ROWS, FEATURES))]
  transfers between devices with their start and end apart: 15 -> 21, of which waited for: 5 -> 8; matrix products, arithmetic and copies ran while one was open for 9% -> 1% of each run, Pallas kernels for 12% -> 19%
where the time goes in v3:
time: 131 us; the launch traced here: 130 us
  waiting for transfers between devices  53.9 us (41%)
  starting transfers between devices  44.9 us (34%)
  Pallas kernels  25.6 us (20%)
  local copies, waits for them, and re-layouts  4.2 us (3%)
    all_to_all x6, starting transfers between devices, exchange(): return lax.all_to_all(value, axes, 0, 0, tiled=True)  32.8 us
    all_to_all x6, waiting for transfers between devices, exchange(): return lax.all_to_all(value, axes, 0, 0, tiled=True)  30.5 us
    ppermute x5, waiting for transfers between devices, to_odd(): return lax.ppermute(x, 'z', [(i, i ^ 1) for i in range(8)])  21.8 us
    pallas_call x9, Pallas kernels, call(): pl.pallas_call(kernel, in_specs=ins, out_specs=VMEM if one else [VMEM] *...  15.7 us
    ppermute x5, starting transfers between devices, to_odd(): return lax.ppermute(x, 'z', [(i, i ^ 1) for i in range(8)])  5.3 us
    ppermute x7, starting transfers between devices, to_core(): return lax.ppermute(x, 'c', [(0, 1), (1, 0)])  5.27 us
    pallas_call x1, Pallas kernels, body(): pl.pallas_call(gradient_kernel, grid=(CHUNKS,), in_specs=[SMEM] + [wide]...  5.24 us
    pallas_call x1, Pallas kernels, body(): pl.pallas_call(weight_kernel, grid=(CHUNKS,), in_specs=[wide] * 4 + [whol...  4.67 us
  transfers between devices with their start and end apart: 21, of which 8 were waited for; matrix products, arithmetic and copies ran while one was open for 1% of the time, Pallas kernels for 19%

profile of v3, /device:TPU:1, one launch (start us, length us, event | category | flops | bytes accessed | tf_op | source)
XLA Modules:
  0.0 130.0 jit_solution(3503123259710894978)
XLA Ops:
  0.6 3.3 %collective-permute-start = (bf16[128,4096]{1,0:T(8,128)(2,1)}, bf16[128,4096]{1,0:T(8,128)(2,1)S(1)}, u32[]{:S(2)}, u32[]{:S(2)}) collective-permute-start(bf16[128,4096]{1,0:T(8,128)(2,1)} %c0.3), channel_id=1, source_target_pairs={{0,1},{1,0},{2,3},{3,2},{4,5},{5,4},{6,7},{7,6},{8,9},{9,8},{10,11... | collective-permute-start | bytes 3145736 | tf_op jit(solution)/shard_map/ppermute | solution.py:254
  4.0 1.9 %shard_map.92 = (bf16[16,48,128]{2,1,0:T(8,128)(2,1)}, bf16[128,128]{1,0:T(8,128)(2,1)}, bf16[128,128]{1,0:T(8,128)(2,1)}, bf16[128,128]{1,0:T(8,128)(2,1)}, bf16[128,128]{1,0:T(8,128)(2,1)}) custom-call(s32[1]{0:T(128)} %bitcast.1.me, bf16[128,512]{1,0:T(8,128)(2,1)} %k.7, bf16[128,512]{1,0:T(8,128)(2,1)} %v.7, bf16[16,512]{1,0:T(8,128)(2,1)} %w.1, ...), custom_call_target="tpu_custom_call" | custom-call | flops 16777216 | bytes 737284 | tf_op jit(solution)/shard_map/pallas_call | solution.py:47
  5.9 6.9 %all-to-all-start = ((bf16[16,48,128]{2,1,0:T(8,128)(2,1)}), bf16[16,48,128]{2,1,0:T(8,128)(2,1)S(1)}, u32[]{:S(2)}, u32[]{:S(2)}) async-start(bf16[16,48,128]{2,1,0:T(8,128)(2,1)} %get-tuple-element.64), calls=%async_computation | async-start | bytes 393216 | tf_op jit(solution)/shard_map/all_to_all | solution.py:240
  12.8 0.2 collective-permute-start.1
  12.9 1.6 %collective-permute-start.2 = (bf16[128,128]{1,0:T(8,128)(2,1)}, bf16[128,128]{1,0:T(8,128)(2,1)S(1)}, u32[]{:S(2)}, u32[]{:S(2)}) collective-permute-start(bf16[128,128]{1,0:T(8,128)(2,1)} %get-tuple-element.67), channel_id=1, source_target_pairs={{0,2},{2,0},{4,6},{6,4},{8,10},{10,8},{12,14},{14,12},{1,3},{3,1},... | collective-permute-start | bytes 98312 | tf_op jit(solution)/shard_map/ppermute | solution.py:257
  14.5 0.4 collective-permute-start.3
  14.9 8.5 %all-to-all-done.first = bf16[16,48,128]{2,1,0:T(8,128)(2,1)S(1)} async-done(((bf16[16,48,128]{2,1,0:T(8,128)(2,1)}), bf16[16,48,128]{2,1,0:T(8,128)(2,1)S(1)}, u32[]{:S(2)}, u32[]{:S(2)}) %all-to-all-start) | async-done | bytes 196640 | tf_op jit(solution)/shard_map/all_to_all | solution.py:240
  23.4 1.2 shard_map.93
  24.7 0.0 copy-start.12
  24.7 0.1 collective-permute-start.4
  24.8 0.4 copy-done.11
  25.3 0.0 copy-done.12
  25.3 0.4 copy-done.6
  25.7 6.8 %all-to-all-start.1 = ((bf16[16,288,128]{2,1,0:T(8,128)(2,1)}), bf16[16,288,128]{2,1,0:T(8,128)(2,1)S(1)}, u32[]{:S(2)}, u32[]{:S(2)}) async-start(bf16[16,288,128]{2,1,0:T(8,128)(2,1)} %get-tuple-element.69), calls=%async_computation.1 | async-start | bytes 2359296 | tf_op jit(solution)/shard_map/all_to_all | solution.py:240
  32.5 17.6 %collective-permute-done.4.c2 = bf16[128,4096]{1,0:T(8,128)(2,1)S(1)} collective-permute-done((bf16[128,4096]{1,0:T(8,128)(2,1)}, bf16[128,4096]{1,0:T(8,128)(2,1)S(1)}, u32[]{:S(2)}, u32[]{:S(2)}) %collective-permute-start.4) | collective-permute-done | bytes 1048608 | tf_op jit(solution)/shard_map/ppermute | solution.py:257
  50.0 0.2 collective-permute-start.5
  50.2 1.6 %all-to-all-done.1.second.w.w0 = bf16[16,288,128]{2,1,0:T(8,128)(2,1)S(1)} async-done(((bf16[16,288,128]{2,1,0:T(8,128)(2,1)}), bf16[16,288,128]{2,1,0:T(8,128)(2,1)S(1)}, u32[]{:S(2)}, u32[]{:S(2)}) %all-to-all-start.1) | async-done | bytes 1179680 | tf_op jit(solution)/shard_map/all_to_all | solution.py:240
  51.9 0.8 shard_map.94
  52.6 4.2 %all-to-all-start.2 = ((bf16[16,32,128]{2,1,0:T(8,128)(2,1)}), bf16[16,32,128]{2,1,0:T(8,128)(2,1)S(1)}, u32[]{:S(2)}, u32[]{:S(2)}) async-start(bf16[16,32,128]{2,1,0:T(8,128)(2,1)} %shard_map.94), calls=%async_computation.2 | async-start | bytes 262144 | tf_op jit(solution)/shard_map/all_to_all | solution.py:240
  56.8 0.6 pad_add_fusion.base
  57.4 1.0 copy-done.8
  58.4 5.2 %shard_map.95 = (bf16[128,128]{1,0:T(8,128)(2,1)}, bf16[128,128]{1,0:T(8,128)(2,1)}, bf16[128,128]{1,0:T(8,128)(2,1)}, bf16[128,128]{1,0:T(8,128)(2,1)}, bf16[16,32,128]{2,1,0:T(8,128)(2,1)}) custom-call(s32[2]{0:T(128)} %pad_add_fusion.base, bf16[128,4096]{1,0:T(8,128)(2,1)} %c0.3, bf16[128,4096]{1,0:T(8,128)(2,1)} %copy-done.6, ...), custom_call_target="tpu_custom_call" | custom-call | flops 536870912 | bytes 6291456 | tf_op jit(solution)/shard_map/pallas_call | solution.py:304
  63.6 2.4 %all-to-all-done.2 = bf16[16,32,128]{2,1,0:T(8,128)(2,1)S(1)} async-done(((bf16[16,32,128]{2,1,0:T(8,128)(2,1)}), bf16[16,32,128]{2,1,0:T(8,128)(2,1)S(1)}, u32[]{:S(2)}, u32[]{:S(2)}) %all-to-all-start.2) | async-done | bytes 131104 | tf_op jit(solution)/shard_map/all_to_all | solution.py:240
  66.1 4.9 %all-to-all-start.3 = ((bf16[16,32,128]{2,1,0:T(8,128)(2,1)}), bf16[16,32,128]{2,1,0:T(8,128)(2,1)S(1)}, u32[]{:S(2)}, u32[]{:S(2)}) async-start(bf16[16,32,128]{2,1,0:T(8,128)(2,1)} %get-tuple-element.79), calls=%async_computation.3 | async-start | bytes 262144 | tf_op jit(solution)/shard_map/all_to_all | solution.py:240
  70.9 2.2 %shard_map.96 = (bf16[128,512]{1,0:T(8,128)(2,1)}, bf16[128,128]{1,0:T(8,128)(2,1)}, bf16[128,128]{1,0:T(8,128)(2,1)}, bf16[128,128]{1,0:T(8,128)(2,1)}, bf16[128,128]{1,0:T(8,128)(2,1)}) custom-call(s32[1]{0:T(128)} %bitcast.1.me, s32[2]{0:T(128)} %pad_add_fusion.base, bf16[128,512]{1,0:T(8,128)(2,1)} %q.5, bf16[128,512]{1,0:T(8,128)(2,1)} %k.7, ...), custom_call_target="tpu_custom_call" | custom-call | flops 50331648 | bytes 786444 | tf_op jit(solution)/shard_map/pallas_call | solution.py:47
  73.1 0.1 collective-permute-start.6
  73.2 1.6 %collective-permute-start.7 = (bf16[128,128]{1,0:T(8,128)(2,1)}, bf16[128,128]{1,0:T(8,128)(2,1)S(1)}, u32[]{:S(2)}, u32[]{:S(2)}) collective-permute-start(bf16[128,128]{1,0:T(8,128)(2,1)} %get-tuple-element.83), channel_id=1, source_target_pairs={{0,2},{2,0},{4,6},{6,4},{8,10},{10,8},{12,14},{14,12},{1,3},{3,1},... | collective-permute-start | bytes 98312 | tf_op jit(solution)/shard_map/ppermute | solution.py:257
  74.9 0.4 collective-permute-start.8
  75.3 0.1 collective-permute-start.9
  75.3 1.4 %collective-permute-start.10 = (bf16[128,128]{1,0:T(8,128)(2,1)}, bf16[128,128]{1,0:T(8,128)(2,1)S(1)}, u32[]{:S(2)}, u32[]{:S(2)}) collective-permute-start(bf16[128,128]{1,0:T(8,128)(2,1)} %get-tuple-element.86), channel_id=1, source_target_pairs={{0,2},{2,0},{4,6},{6,4},{8,10},{10,8},{12,14},{14,12},{1,3},{3,1},... | collective-permute-start | bytes 98312 | tf_op jit(solution)/shard_map/ppermute | solution.py:257
  76.8 0.7 collective-permute-start.11
  77.4 1.6 %collective-permute-done.8.a3 = bf16[128,128]{1,0:T(8,128)(2,1)S(1)} collective-permute-done((bf16[128,128]{1,0:T(8,128)(2,1)}, bf16[128,128]{1,0:T(8,128)(2,1)S(1)}, u32[]{:S(2)}, u32[]{:S(2)}) %collective-permute-start.8) | collective-permute-done | bytes 32800 | tf_op jit(solution)/shard_map/ppermute | solution.py:260
  79.1 0.6 copy-done.16
  79.7 4.7 %shard_map.97 = bf16[16,288,128]{2,1,0:T(8,128)(2,1)} custom-call(bf16[128,4096]{1,0:T(8,128)(2,1)} %c0.3, bf16[128,4096]{1,0:T(8,128)(2,1)} %copy-done.6, bf16[128,4096]{1,0:T(8,128)(2,1)} %copy-done.7, bf16[128,4096]{1,0:T(8,128)(2,1)} %copy-done.8, bf16[128,128]{1,0:T(8,128)(2,1)} %get-tuple-element.81.a0, bf16[128,128]{1,0:T(8,128)(2,1)} %copy-done.14, ...), custom_call_target="tpu_custom_call" | custom-call | flops 536870912 | bytes 6291456 | tf_op jit(solution)/shard_map/pallas_call | solution.py:331
  84.5 0.6 collective-permute-start.12
  85.1 0.7 broadcast_dynamic-update-slice_fusion
  85.8 4.5 %all-to-all-start.4 = ((bf16[16,288,128]{2,1,0:T(8,128)(2,1)}), bf16[16,288,128]{2,1,0:T(8,128)(2,1)S(1)}, u32[]{:S(2)}, u32[]{:S(2)}) async-start(bf16[16,288,128]{2,1,0:T(8,128)(2,1)} %broadcast_dynamic-update-slice_fusion), calls=%async_computation.4 | async-start | bytes 2359296 | tf_op jit(solution)/shard_map/all_to_all | solution.py:240
  90.2 0.7 collective-permute-start.13
  90.9 2.9 %shard_map.99 = (bf16[128,512]{1,0:T(8,128)(2,1)}, f32[128,512]{1,0:T(8,128)}, f32[128,512]{1,0:T(8,128)}) custom-call(s32[1]{0:T(128)} %bitcast.1.me, bf16[128,512]{1,0:T(8,128)(2,1)} %q.5, bf16[128,512]{1,0:T(8,128)(2,1)} %k.7, bf16[128,512]{1,0:T(8,128)(2,1)} %v.7, bf16[128,128]{1,0:T(8,128)(2,1)} %get-tuple-element.93.g0, bf16[128,128]{1,0:T(8,128)(2,1)} %copy-done.17, ...), custom_call_target="tpu_custom_call" | custom-call | flops 100663296 | bytes 1310724 | tf_op jit(solution)/shard_map/pallas_call | solution.py:47
  93.8 13.4 %all-to-all-done.4.got = bf16[16,288,128]{2,1,0:T(8,128)(2,1)S(1)} async-done(((bf16[16,288,128]{2,1,0:T(8,128)(2,1)}), bf16[16,288,128]{2,1,0:T(8,128)(2,1)S(1)}, u32[]{:S(2)}, u32[]{:S(2)}) %all-to-all-start.4) | async-done | bytes 1179680 | tf_op jit(solution)/shard_map/all_to_all | solution.py:240
  107.3 0.9 shard_map.100
  108.2 4.2 %collective-permute-done.12.w2 = bf16[16,288,128]{2,1,0:T(8,128)(2,1)} collective-permute-done((bf16[16,288,128]{2,1,0:T(8,128)(2,1)S(1)}, bf16[16,288,128]{2,1,0:T(8,128)(2,1)}, u32[]{:S(2)}, u32[]{:S(2)}) %collective-permute-start.12) | collective-permute-done | bytes 1179680 | tf_op jit(solution)/shard_map/ppermute | solution.py:257
  112.4 0.7 collective-permute-start.14
  113.0 5.7 %all-to-all-start.5 = ((bf16[16,48,128]{2,1,0:T(8,128)(2,1)}), bf16[16,48,128]{2,1,0:T(8,128)(2,1)S(1)}, u32[]{:S(2)}, u32[]{:S(2)}) async-start(bf16[16,48,128]{2,1,0:T(8,128)(2,1)} %shard_map.100), calls=%async_computation.5 | async-start | bytes 393216 | tf_op jit(solution)/shard_map/all_to_all | solution.py:240
  118.8 1.0 copy-done.9
  119.8 4.8 %shard_map.101 = bf16[128,4096]{1,0:T(8,128)(2,1)} custom-call(s32[1]{0:T(128)} %bitcast.1.me, bf16[128,512]{1,0:T(8,128)(2,1)} %get-tuple-element.102.att, bf16[16,288,128]{2,1,0:T(8,128)(2,1)} %copy-done, bf16[16,288,128]{2,1,0:T(8,128)(2,1)} %collective-permute-done.13.w1, bf16[16,288,128]{2,1,0:T(8,128)(2,1)} %collective-permute-done.12.w2, ...), custom_call_target="tpu_custom_call" | custom-call | flops 536870912 | bytes 5898244 | tf_op jit(solution)/shard_map/pallas_call | solution.py:47
  124.6 4.5 %all-to-all-done.5.got = bf16[16,48,128]{2,1,0:T(8,128)(2,1)S(1)} async-done(((bf16[16,48,128]{2,1,0:T(8,128)(2,1)}), bf16[16,48,128]{2,1,0:T(8,128)(2,1)S(1)}, u32[]{:S(2)}, u32[]{:S(2)}) %all-to-all-start.5) | async-done | bytes 196640 | tf_op jit(solution)/shard_map/all_to_all | solution.py:240
  129.1 1.0 shard_map.102
  (47 shorter events, 0.1 us)
Async XLA Ops:
  0.6 24.1 %collective-permute-start = (bf16[128,4096]{1,0:T(8,128)(2,1)}, bf16[128,4096]{1,0:T(8,128)(2,1)S(1)}, u32[]{:S(2)}, u32[]{:S(2)}) collective-permute-start(bf16[128,4096]{1,0:T(8,128)(2,1)} %c0.3), channel_id=1, source_target_pairs={{0,1},{1,0},{2,3},{3,2},{4,5},{5,4},{6,7},{7,6},{8,9},{9,8},{10,11... | collective-permute-start | bytes 3145736 | tf_op jit(solution)/shard_map/ppermute | solution.py:254
  5.9 17.5 %all-to-all-start = ((bf16[16,48,128]{2,1,0:T(8,128)(2,1)}), bf16[16,48,128]{2,1,0:T(8,128)(2,1)S(1)}, u32[]{:S(2)}, u32[]{:S(2)}) async-start(bf16[16,48,128]{2,1,0:T(8,128)(2,1)} %get-tuple-element.64), calls=%async_computation | async-start | bytes 393216 | tf_op jit(solution)/shard_map/all_to_all | solution.py:240
  12.8 11.9 %collective-permute-start.1 = (bf16[128,128]{1,0:T(8,128)(2,1)}, bf16[128,128]{1,0:T(8,128)(2,1)S(1)}, u32[]{:S(2)}, u32[]{:S(2)}) collective-permute-start(bf16[128,128]{1,0:T(8,128)(2,1)} %get-tuple-element.66), channel_id=1, source_target_pairs={{0,1},{1,0},{2,3},{3,2},{4,5},{5,4},{6,7},{7,6},{8,9},{9,8},{10,11... | collective-permute-start | bytes 98312 | tf_op jit(solution)/shard_map/ppermute | solution.py:254
  12.9 11.7 %collective-permute-start.2 = (bf16[128,128]{1,0:T(8,128)(2,1)}, bf16[128,128]{1,0:T(8,128)(2,1)S(1)}, u32[]{:S(2)}, u32[]{:S(2)}) collective-permute-start(bf16[128,128]{1,0:T(8,128)(2,1)} %get-tuple-element.67), channel_id=1, source_target_pairs={{0,2},{2,0},{4,6},{6,4},{8,10},{10,8},{12,14},{14,12},{1,3},{3,1},... | collective-permute-start | bytes 98312 | tf_op jit(solution)/shard_map/ppermute | solution.py:257
  14.5 10.2 %collective-permute-start.3 = (bf16[128,128]{1,0:T(8,128)(2,1)}, bf16[128,128]{1,0:T(8,128)(2,1)S(1)}, u32[]{:S(2)}, u32[]{:S(2)}) collective-permute-start(bf16[128,128]{1,0:T(8,128)(2,1)} %get-tuple-element.68), channel_id=1, source_target_pairs={{0,3},{1,2},{2,1},{3,0},{4,7},{5,6},{6,5},{7,4},{8,11},{9,10},{10,... | collective-permute-start | bytes 98312 | tf_op jit(solution)/shard_map/ppermute | solution.py:260
  24.7 0.6 copy-start.11
  24.7 0.6 copy-start.12
  24.7 0.6 copy-start.13
  24.7 1.0 copy-start.6
  24.7 25.3 %collective-permute-start.4 = (bf16[128,4096]{1,0:T(8,128)(2,1)}, bf16[128,4096]{1,0:T(8,128)(2,1)S(1)}, u32[]{:S(2)}, u32[]{:S(2)}) collective-permute-start(bf16[128,4096]{1,0:T(8,128)(2,1)} %c0.3), channel_id=1, source_target_pairs={{0,2},{2,0},{4,6},{6,4},{8,10},{10,8},{12,14},{14,12},{1,3},{3,1},... | collective-permute-start | bytes 3145736 | tf_op jit(solution)/shard_map/ppermute | solution.py:257
  25.7 26.2 %all-to-all-start.1 = ((bf16[16,288,128]{2,1,0:T(8,128)(2,1)}), bf16[16,288,128]{2,1,0:T(8,128)(2,1)S(1)}, u32[]{:S(2)}, u32[]{:S(2)}) async-start(bf16[16,288,128]{2,1,0:T(8,128)(2,1)} %get-tuple-element.69), calls=%async_computation.1 | async-start | bytes 2359296 | tf_op jit(solution)/shard_map/all_to_all | solution.py:240
  50.0 7.4 %copy-start.7 = (bf16[128,4096]{1,0:T(8,128)(2,1)}, bf16[128,4096]{1,0:T(8,128)(2,1)S(1)}, u32[]{:S(2)}) copy-start(bf16[128,4096]{1,0:T(8,128)(2,1)S(1)} %collective-permute-done.4.c2) | copy-start | bytes 3145732
  50.0 7.4 %collective-permute-start.5 = (bf16[128,4096]{1,0:T(8,128)(2,1)S(1)}, bf16[128,4096]{1,0:T(8,128)(2,1)S(1)}, u32[]{:S(2)}, u32[]{:S(2)}) collective-permute-start(bf16[128,4096]{1,0:T(8,128)(2,1)S(1)} %collective-permute-done.4.c2), channel_id=1, source_target_pairs={{0,1},{1,0},{2,3},{3,2},{4,5},{5,4},{6,7},{7,6},{8,9},{9,8},{10,11... | collective-permute-start | bytes 3145736 | tf_op jit(solution)/shard_map/ppermute | solution.py:254
  51.9 5.5 %copy-start = (bf16[16,288,128]{2,1,0:T(8,128)(2,1)}, bf16[16,288,128]{2,1,0:T(8,128)(2,1)S(1)}, u32[]{:S(2)}) copy-start(bf16[16,288,128]{2,1,0:T(8,128)(2,1)S(1)} %all-to-all-done.1.second.w.w0) | copy-start | bytes 3538948
  52.6 13.4 %all-to-all-start.2 = ((bf16[16,32,128]{2,1,0:T(8,128)(2,1)}), bf16[16,32,128]{2,1,0:T(8,128)(2,1)S(1)}, u32[]{:S(2)}, u32[]{:S(2)}) async-start(bf16[16,32,128]{2,1,0:T(8,128)(2,1)} %shard_map.94), calls=%async_computation.2 | async-start | bytes 262144 | tf_op jit(solution)/shard_map/all_to_all | solution.py:240
  57.4 1.0 copy-start.8
  66.1 4.9 %copy-start.10 = (bf16[16,32,128]{2,1,0:T(8,128)(2,1)}, bf16[16,32,128]{2,1,0:T(8,128)(2,1)S(1)}, u32[]{:S(2)}) copy-start(bf16[16,32,128]{2,1,0:T(8,128)(2,1)S(1)} %all-to-all-done.2) | copy-start | bytes 393220
  66.1 18.4 %all-to-all-start.3 = ((bf16[16,32,128]{2,1,0:T(8,128)(2,1)}), bf16[16,32,128]{2,1,0:T(8,128)(2,1)S(1)}, u32[]{:S(2)}, u32[]{:S(2)}) async-start(bf16[16,32,128]{2,1,0:T(8,128)(2,1)} %get-tuple-element.79), calls=%async_computation.3 | async-start | bytes 262144 | tf_op jit(solution)/shard_map/all_to_all | solution.py:240
  73.1 3.6 %collective-permute-start.6 = (bf16[128,128]{1,0:T(8,128)(2,1)}, bf16[128,128]{1,0:T(8,128)(2,1)S(1)}, u32[]{:S(2)}, u32[]{:S(2)}) collective-permute-start(bf16[128,128]{1,0:T(8,128)(2,1)} %get-tuple-element.82), channel_id=1, source_target_pairs={{0,1},{1,0},{2,3},{3,2},{4,5},{5,4},{6,7},{7,6},{8,9},{9,8},{10,11... | collective-permute-start | bytes 98312 | tf_op jit(solution)/shard_map/ppermute | solution.py:254
  73.2 4.2 %collective-permute-start.7 = (bf16[128,128]{1,0:T(8,128)(2,1)}, bf16[128,128]{1,0:T(8,128)(2,1)S(1)}, u32[]{:S(2)}, u32[]{:S(2)}) collective-permute-start(bf16[128,128]{1,0:T(8,128)(2,1)} %get-tuple-element.83), channel_id=1, source_target_pairs={{0,2},{2,0},{4,6},{6,4},{8,10},{10,8},{12,14},{14,12},{1,3},{3,1},... | collective-permute-start | bytes 98312 | tf_op jit(solution)/shard_map/ppermute | solution.py:257
  74.9 4.2 %collective-permute-start.8 = (bf16[128,128]{1,0:T(8,128)(2,1)}, bf16[128,128]{1,0:T(8,128)(2,1)S(1)}, u32[]{:S(2)}, u32[]{:S(2)}) collective-permute-start(bf16[128,128]{1,0:T(8,128)(2,1)} %get-tuple-element.84), channel_id=1, source_target_pairs={{0,3},{1,2},{2,1},{3,0},{4,7},{5,6},{6,5},{7,4},{8,11},{9,10},{10,... | collective-permute-start | bytes 98312 | tf_op jit(solution)/shard_map/ppermute | solution.py:260
  75.3 9.1 %collective-permute-start.9 = (bf16[128,128]{1,0:T(8,128)(2,1)}, bf16[128,128]{1,0:T(8,128)(2,1)S(1)}, u32[]{:S(2)}, u32[]{:S(2)}) collective-permute-start(bf16[128,128]{1,0:T(8,128)(2,1)} %get-tuple-element.85), channel_id=1, source_target_pairs={{0,1},{1,0},{2,3},{3,2},{4,5},{5,4},{6,7},{7,6},{8,9},{9,8},{10,11... | collective-permute-start | bytes 98312 | tf_op jit(solution)/shard_map/ppermute | solution.py:254
  75.3 9.0 %collective-permute-start.10 = (bf16[128,128]{1,0:T(8,128)(2,1)}, bf16[128,128]{1,0:T(8,128)(2,1)S(1)}, u32[]{:S(2)}, u32[]{:S(2)}) collective-permute-start(bf16[128,128]{1,0:T(8,128)(2,1)} %get-tuple-element.86), channel_id=1, source_target_pairs={{0,2},{2,0},{4,6},{6,4},{8,10},{10,8},{12,14},{14,12},{1,3},{3,1},... | collective-permute-start | bytes 98312 | tf_op jit(solution)/shard_map/ppermute | solution.py:257
  76.7 2.3 %copy-start.14 = (bf16[128,128]{1,0:T(8,128)(2,1)}, bf16[128,128]{1,0:T(8,128)(2,1)S(1)}, u32[]{:S(2)}) copy-start(bf16[128,128]{1,0:T(8,128)(2,1)S(1)} %collective-permute-done.6.a1) | copy-start | bytes 98308
  76.8 7.6 %collective-permute-start.11 = (bf16[128,128]{1,0:T(8,128)(2,1)}, bf16[128,128]{1,0:T(8,128)(2,1)S(1)}, u32[]{:S(2)}, u32[]{:S(2)}) collective-permute-start(bf16[128,128]{1,0:T(8,128)(2,1)} %get-tuple-element.87), channel_id=1, source_target_pairs={{0,3},{1,2},{2,1},{3,0},{4,7},{5,6},{6,5},{7,4},{8,11},{9,10},{10,... | collective-permute-start | bytes 98312 | tf_op jit(solution)/shard_map/ppermute | solution.py:260
  77.4 1.7 %copy-start.15 = (bf16[128,128]{1,0:T(8,128)(2,1)}, bf16[128,128]{1,0:T(8,128)(2,1)S(1)}, u32[]{:S(2)}) copy-start(bf16[128,128]{1,0:T(8,128)(2,1)S(1)} %collective-permute-done.7.a2) | copy-start | bytes 98308
  79.1 0.6 copy-start.16
  79.7 4.8 %copy-start.1 = (bf16[16,288,128]{2,1,0:T(8,128)(2,1)S(1)}, bf16[16,288,128]{2,1,0:T(8,128)(2,1)}, u32[]{:S(2)}) copy-start(bf16[16,288,128]{2,1,0:T(8,128)(2,1)} %copy-done) | copy-start | bytes 3538948
  84.4 1.4 %copy-start.17 = (bf16[128,128]{1,0:T(8,128)(2,1)}, bf16[128,128]{1,0:T(8,128)(2,1)S(1)}, u32[]{:S(2)}) copy-start(bf16[128,128]{1,0:T(8,128)(2,1)S(1)} %collective-permute-done.9.g1) | copy-start | bytes 98308
  84.4 1.4 %copy-start.18 = (bf16[128,128]{1,0:T(8,128)(2,1)}, bf16[128,128]{1,0:T(8,128)(2,1)S(1)}, u32[]{:S(2)}) copy-start(bf16[128,128]{1,0:T(8,128)(2,1)S(1)} %collective-permute-done.10.g2) | copy-start | bytes 98308
  84.4 1.4 %copy-start.19 = (bf16[128,128]{1,0:T(8,128)(2,1)}, bf16[128,128]{1,0:T(8,128)(2,1)S(1)}, u32[]{:S(2)}) copy-start(bf16[128,128]{1,0:T(8,128)(2,1)S(1)} %collective-permute-done.11.g3) | copy-start | bytes 98308
  84.5 27.9 %collective-permute-start.12 = (bf16[16,288,128]{2,1,0:T(8,128)(2,1)S(1)}, bf16[16,288,128]{2,1,0:T(8,128)(2,1)}, u32[]{:S(2)}, u32[]{:S(2)}) collective-permute-start(bf16[16,288,128]{2,1,0:T(8,128)(2,1)S(1)} %copy-done.1), channel_id=1, source_target_pairs={{0,2},{2,0},{4,6},{6,4},{8,10},{10,8},{12,14},{14,12},{1,3},{3,1},... | collective-permute-start | bytes 3538952 | tf_op jit(solution)/shard_map/ppermute | solution.py:257
  85.8 21.5 %all-to-all-start.4 = ((bf16[16,288,128]{2,1,0:T(8,128)(2,1)}), bf16[16,288,128]{2,1,0:T(8,128)(2,1)S(1)}, u32[]{:S(2)}, u32[]{:S(2)}) async-start(bf16[16,288,128]{2,1,0:T(8,128)(2,1)} %broadcast_dynamic-update-slice_fusion), calls=%async_computation.4 | async-start | bytes 2359296 | tf_op jit(solution)/shard_map/all_to_all | solution.py:240
  90.2 28.5 %collective-permute-start.13 = (bf16[16,288,128]{2,1,0:T(8,128)(2,1)S(1)}, bf16[16,288,128]{2,1,0:T(8,128)(2,1)}, u32[]{:S(2)}, u32[]{:S(2)}) collective-permute-start(bf16[16,288,128]{2,1,0:T(8,128)(2,1)S(1)} %copy-done.1), channel_id=1, source_target_pairs={{0,1},{1,0},{2,3},{3,2},{4,5},{5,4},{6,7},{7,6},{8,9},{9,8},{10,11... | collective-permute-start | bytes 3538952 | tf_op jit(solution)/shard_map/ppermute | solution.py:254
  112.4 6.4 %collective-permute-start.14 = (bf16[16,288,128]{2,1,0:T(8,128)(2,1)}, bf16[16,288,128]{2,1,0:T(8,128)(2,1)S(1)}, u32[]{:S(2)}, u32[]{:S(2)}) collective-permute-start(bf16[16,288,128]{2,1,0:T(8,128)(2,1)} %collective-permute-done.12.w2), channel_id=1, source_target_pairs={{0,1},{1,0},{2,3},{3,2},{4,5},{5,4},{6,7},{7,6},{8,9},{9,8},{10,11... | collective-permute-start | bytes 3538952 | tf_op jit(solution)/shard_map/ppermute | solution.py:254
  113.0 16.0 %all-to-all-start.5 = ((bf16[16,48,128]{2,1,0:T(8,128)(2,1)}), bf16[16,48,128]{2,1,0:T(8,128)(2,1)S(1)}, u32[]{:S(2)}, u32[]{:S(2)}) async-start(bf16[16,48,128]{2,1,0:T(8,128)(2,1)} %shard_map.100), calls=%async_computation.5 | async-start | bytes 393216 | tf_op jit(solution)/shard_map/all_to_all | solution.py:240
  118.7 10.3 %copy-start.2 = (bf16[128,512]{1,0:T(8,128)(2,1)S(1)}, bf16[128,512]{1,0:T(8,128)(2,1)}, u32[]{:S(2)}) copy-start(bf16[128,512]{1,0:T(8,128)(2,1)} %k.7) | copy-start | bytes 393220
  118.7 10.3 %copy-start.3 = (bf16[128,512]{1,0:T(8,128)(2,1)S(1)}, bf16[128,512]{1,0:T(8,128)(2,1)}, u32[]{:S(2)}) copy-start(bf16[128,512]{1,0:T(8,128)(2,1)} %v.7) | copy-start | bytes 393220
  118.7 10.3 %copy-start.4 = (f32[128,512]{1,0:T(8,128)S(1)}, f32[128,512]{1,0:T(8,128)}, u32[]{:S(2)}) copy-start(f32[128,512]{1,0:T(8,128)} %get-tuple-element.106.kg_local) | copy-start | bytes 786436
  118.8 10.3 %copy-start.5 = (f32[128,512]{1,0:T(8,128)S(1)}, f32[128,512]{1,0:T(8,128)}, u32[]{:S(2)}) copy-start(f32[128,512]{1,0:T(8,128)} %get-tuple-element.107.vg_local) | copy-start | bytes 786436
  118.8 1.0 copy-start.9

commit v4 on v3

v4 whole, which is shorter than its diff:
```python
import jax
import jax.numpy as jnp
from jax import lax
from jax.experimental import pallas as pl
from jax.experimental.pallas import tpu as pltpu
from jax.sharding import Mesh, PartitionSpec as P

HEADS = 4
HEAD = 128
TOKENS = 128
FEATURES = HEADS * HEAD
MODEL = 4096
GROUPS = 16
MEMBERS = 16
ROWS = MODEL // (GROUPS * MEMBERS)
SHARE = MODEL // GROUPS
STATE_ROWS = FEATURES // MEMBERS
CHUNKS = 4
LIMIT = 63_000_000
SOME = 60_000_000
ROOM = 32_000_000
SLICE = HEAD // MEMBERS
FLIPS = (0, 2, 1, 3)
XY = ("x", "y")
ZC = ("z", "c")
BF16 = jnp.bfloat16
F32 = jnp.float32
NN = (((1,), (0,)), ((), ()))
NT = (((1,), (1,)), ((), ()))
TN = (((0,), (0,)), ((), ()))
VMEM = pl.BlockSpec(memory_space=pltpu.VMEM)
SMEM = pl.BlockSpec(memory_space=pltpu.SMEM)
HBM = pl.BlockSpec(memory_space=pl.ANY)


def mul(a, b, dims):
    return lax.dot_general(a, b, dims, preferred_element_type=F32)


def shape(dims, dtype):
    return jax.ShapeDtypeStruct(dims, dtype)


def call(kernel, ins, outs, args, flops, limit=LIMIT, **kw):
    out_bytes = sum(o.size * o.dtype.itemsize for o in outs)
    in_bytes = sum(a.size * a.dtype.itemsize for a in args)
    one = len(outs) == 1
    return pl.pallas_call(
        kernel,
        in_specs=ins,
        out_specs=VMEM if one else [VMEM] * len(outs),
        out_shape=outs[0] if one else outs,
        compiler_params=pltpu.CompilerParams(vmem_limit_bytes=limit),
        cost_estimate=pl.CostEstimate(
            flops=flops, bytes_accessed=in_bytes + out_bytes, transcendentals=0
        ),
        **kw,
    )(*args)


def head(ref, h):
    return ref[:, h * HEAD : (h + 1) * HEAD]


def scale_from(first):
    token = first + lax.broadcasted_iota(jnp.int32, (TOKENS, HEAD), 0)
    return lax.rsqrt((HEAD * (token + 1)).astype(F32))


def causal(x):
    row = lax.broadcasted_iota(jnp.int32, x.shape, 0)
    col = lax.broadcasted_iota(jnp.int32, x.shape, 1)
    return jnp.where(row >= col, x, 0.0).astype(BF16)


def keys_kernel(me, k, v, w, q, out, x0, x1, x2, x3):
    products = [mul(head(k, h), head(v, h), TN) for h in range(HEADS)]
    for m in range(MEMBERS):
        rows = [x[m * SLICE : (m + 1) * SLICE] for x in products]
        out[m, :STATE_ROWS, :] = jnp.concatenate(rows, axis=0).astype(BF16)
        out[m, STATE_ROWS:, :] = head(w, head_of(m))
    for flip, ref in zip(FLIPS, (x0, x1, x2, x3)):
        at = head_at(me[0] ^ flip)
        for i, x in enumerate((q, k, v)):
            ref[i * TOKENS : (i + 1) * TOKENS, :] = x[:, at]


def head_of(m):
    return (m % 2) * 2 + (m % 4) // 2


def head_at(h):
    return pl.ds(pl.multiple_of(h * HEAD, HEAD), HEAD)


def before_kernel(first, inside, send):
    running = jnp.zeros((STATE_ROWS, HEAD), F32)
    rows = []
    for m in range(MEMBERS):
        inside[m] = running
        running = running + first[m, :STATE_ROWS, :].astype(F32)
        rows.append(first[m, STATE_ROWS:, :])
    packed = jnp.concatenate([running.astype(BF16)] + rows, axis=0)
    for j in range(GROUPS):
        send[j] = packed


def carry_kernel(group, second, inside, out):
    carried = jnp.zeros((STATE_ROWS, HEAD), F32)
    for j in range(GROUPS):
        piece = second[j, :STATE_ROWS, :].astype(F32)
        carried = carried + jnp.where(j < group[0], piece, 0.0)
    states = [inside[m] + carried for m in range(MEMBERS)]
    for m in range(MEMBERS):
        at = head_of(m) * SLICE
        rows = [states[m ^ k][at : at + SLICE] for k in range(4)]
        out[m] = jnp.concatenate(rows, axis=0).astype(BF16)


def attend_kernel(
    base, place, x0, x1, x2, x3, got, g1, g2, g3, a0, a1, a2, a3, s0, p1, p2, p3
):
    slices = [got[m].astype(F32) for m in range(MEMBERS)]
    for i, (x, a) in enumerate(zip((x0, x1, x2, x3), (a0, a1, a2, a3))):
        rows = [piece[i * SLICE : (i + 1) * SLICE] for piece in slices]
        key_state = jnp.concatenate(rows, axis=0).astype(BF16)
        q, k, v = (x[j * TOKENS : (j + 1) * TOKENS, :] for j in range(3))
        scores = causal(mul(q, k, NT))
        total = mul(scores, v, NN) + mul(q, key_state, NN)
        result = (total * scale_from(base[0] + (place[0] ^ i) * TOKENS)).astype(BF16)
        a[...] = result
        if i == 0:
            s0[...] = key_state
        else:
            pair, g = ((p1, g1), (p2, g2), (p3, g3))[i - 1]
            pair[:TOKENS] = result
            pair[TOKENS : 2 * TOKENS] = g[...]
            pair[2 * TOKENS :] = key_state


def gradient_kernel(
    base, place, c0, c1, c2, c3, w, x0, x1, x2, x3, g0, g1, g2, g3, out, cots, held, sems
):
    copies = [
        pltpu.make_async_copy(c, cots.at[i], sems.at[i]) for i, c in enumerate((c0, c1, c2, c3))
    ]
    weight_copy = pltpu.make_async_copy(w, held, sems.at[4])
    weight_copy.start()
    for copy in copies:
        copy.start()
    weight_copy.wait()
    right = held[:, STATE_ROWS:, :].reshape(MODEL, HEAD)
    sums = []
    for i, (x, g) in enumerate(zip((x0, x1, x2, x3), (g0, g1, g2, g3))):
        copies[i].wait()
        scale = scale_from(base[0] + (place[0] ^ i) * TOKENS)
        total = mul(cots[i], right, NN)
        value = (total * scale).astype(BF16)
        g[...] = value
        sums.append(mul(x[:TOKENS, :], value, TN))
    for m in range(MEMBERS):
        at = slice(m * SLICE, (m + 1) * SLICE)
        out[m] = jnp.concatenate([x[at] for x in sums], axis=0).astype(BF16)


def after_kernel(first, inside, total):
    pieces = [first[m].astype(F32) for m in range(MEMBERS)]
    running = jnp.zeros((STATE_ROWS, HEAD), F32)
    for block in reversed(range(MEMBERS)):
        quad, local = block // 4, block % 4
        inside[block] = running
        rows = []
        for h in range(HEADS):
            place = (h % 2) * 2 + h // 2
            at = (place ^ local) * SLICE
            rows.append(pieces[quad * 4 + place][at : at + SLICE])
        running = running + jnp.concatenate(rows, axis=0)
    total[...] = running.astype(BF16)


def mixed_kernel(a0, p1, p2, p3, *refs):
    *parts, out = refs
    left = jnp.concatenate([a0[...]] + [p[:TOKENS] for p in (p1, p2, p3)], axis=1)
    for j in range(GROUPS):
        half, at = divmod(j, GROUPS // 2)
        right = jnp.concatenate([w[at] for w in parts[half::2]], axis=1)
        out[:, j * SHARE : (j + 1) * SHARE] = mul(left, right, NT).astype(BF16)


def weight_kernel(c0, c1, c2, c3, a0, a1, a2, a3, out, cots, sems):
    width = MODEL // CHUNKS
    copies = []
    for step in range(CHUNKS):
        at = pl.ds(step * width, width)
        copies.append(
            [
                pltpu.make_async_copy(c.at[:, at], cots.at[i, :, at], sems.at[step, i])
                for i, c in enumerate((c0, c1, c2, c3))
            ]
        )
    for group in copies:
        for copy in group:
            copy.start()
    turned = jnp.concatenate([a[...].T for a in (a0, a1, a2, a3)], axis=1)
    for j in range(GROUPS):
        if j % (GROUPS // CHUNKS) == 0:
            for copy in copies[j // (GROUPS // CHUNKS)]:
                copy.wait()
        at = slice(j * SHARE, (j + 1) * SHARE)
        right = cots[:, :, at].reshape(4 * TOKENS, SHARE)
        term = mul(turned, right, NN).astype(BF16)
        for half in range(2):
            out[j, half * HEAD : (half + 1) * HEAD, :] = term[:, half * HEAD : (half + 1) * HEAD]
        out[j, SHARE:, :] = jnp.zeros((STATE_ROWS, HEAD), BF16)


def local_kernel(me, q, k, v, g0, s0, p1, p2, p3, qg, kg, vg, by_head):
    by_head[me[0], :TOKENS] = g0[...]
    by_head[me[0], TOKENS:] = s0[...]
    for flip, pair in zip(FLIPS[1:], (p1, p2, p3)):
        by_head[me[0] ^ flip] = pair[TOKENS:]
    for h in range(HEADS):
        at = slice(h * HEAD, (h + 1) * HEAD)
        qh, kh, vh, gh = head(q, h), head(k, h), head(v, h), by_head[h, :TOKENS]
        scores = causal(mul(qh, kh, NT))
        grads = causal(mul(gh, vh, NT))
        qg[:, at] = (mul(grads, kh, NN) + mul(gh, by_head[h, TOKENS:], NT)).astype(BF16)
        kg[:, at] = mul(grads, qh, TN)
        vg[:, at] = mul(scores, gh, TN)


def reduce_kernel(group, got, inside, out):
    after = jnp.zeros((STATE_ROWS, HEAD), F32)
    for j in range(GROUPS):
        piece = got[j, SHARE:, :].astype(F32)
        after = after + jnp.where(j > group[0], piece, 0.0)
    for m in range(MEMBERS):
        out[m, ROWS:, :] = (inside[m] + after).astype(BF16)
    per = HEAD // ROWS
    for half in range(2):
        total = None
        for j in range(GROUPS):
            piece = got[j, half * HEAD : (half + 1) * HEAD, :].astype(F32)
            total = piece if total is None else total + piece
        turned = total.T.astype(BF16)
        for m in range(per):
            out[half * per + m, :ROWS, :] = turned[m * ROWS : (m + 1) * ROWS]


def final_kernel(got, k, v, kg_local, vg_local, kg, vg, wg):
    states = [got[m, ROWS:, :].astype(F32) for m in range(MEMBERS)]
    for h in range(HEADS):
        at = slice(h * HEAD, (h + 1) * HEAD)
        rows = [x[h * SLICE : (h + 1) * SLICE] for x in states]
        grad_state = jnp.concatenate(rows, axis=0).astype(BF16)
        kg[:, at] = (kg_local[:, at] + mul(head(v, h), grad_state, NT)).astype(BF16)
        vg[:, at] = (vg_local[:, at] + mul(head(k, h), grad_state, NN)).astype(BF16)
        total = None
        for quad in range(MEMBERS // 4):
            piece = got[quad * 4 + (h % 2) * 2 + h // 2, :ROWS, :].astype(F32)
            total = piece if total is None else total + piece
        wg[:, at] = total


def exchange(value, axes):
    return lax.all_to_all(value, axes, 0, 0, tiled=True)


def body(queries, keys, values, out_weight, cotangent):
    group = lax.axis_index(XY).astype(jnp.int32)
    member = lax.axis_index(ZC)
    core = lax.axis_index("c")
    odd = lax.rem(lax.axis_index("z"), 2)
    me = (core * 2 + odd).astype(jnp.int32).reshape(1)
    group_id = group.reshape(1)

    base = (group * MEMBERS * TOKENS).reshape(1)
    place = member.astype(jnp.int32).reshape(1)

    def to_core(x):
        return lax.ppermute(x, "c", [(0, 1), (1, 0)])

    def to_odd(x):
        return lax.ppermute(x, "z", [(i, i ^ 1) for i in range(8)])

    def to_both(x):
        return lax.ppermute(x, ZC, [(i, i ^ 3) for i in range(MEMBERS)])

    head_block = shape((TOKENS, HEAD), BF16)
    small = 2 * TOKENS * HEAD * FEATURES
    large = 2 * TOKENS * MODEL * FEATURES
    triple = shape((3 * TOKENS, HEAD), BF16)

    sent, x0, x1, x2, x3 = call(
        keys_kernel,
        [SMEM] + [VMEM] * 4,
        [shape((MEMBERS, STATE_ROWS + ROWS, HEAD), BF16)] + [triple] * 4,
        (me, keys, values, out_weight, queries),
        small,
    )
    first = exchange(sent, ZC)
    cot_c = to_core(cotangent)
    x1, x2, x3 = to_core(x1), to_odd(x2), to_both(x3)
    inside, sent = call(
        before_kernel,
        [VMEM],
        [
            shape((MEMBERS, STATE_ROWS, HEAD), F32),
            shape((GROUPS, STATE_ROWS + SHARE, HEAD), BF16),
        ],
        (first,),
        small,
        limit=ROOM,
    )
    sent, cot_c, x1, x2, x3, late = lax.optimization_barrier((sent, cot_c, x1, x2, x3, cotangent))
    cot_z = to_odd(late)
    second = exchange(sent, XY)
    cot_zc = to_core(cot_z)
    states = call(
        carry_kernel,
        [SMEM, VMEM, VMEM],
        [shape((MEMBERS, STATE_ROWS, HEAD), BF16)],
        (group_id, second, inside),
        small,
        limit=ROOM,
    )
    third = exchange(states, ZC)
    g0, g1, g2, g3, sent = call(
        gradient_kernel,
        [SMEM] * 2 + [HBM] * 5 + [VMEM] * 4,
        [head_block] * 4
        + [shape((MEMBERS, STATE_ROWS, HEAD), BF16)],
        (base, place, cotangent, cot_c, cot_z, cot_zc, second, x0, x1, x2, x3),
        large,
        scratch_shapes=[
            pltpu.VMEM((4, TOKENS, MODEL), BF16),
            pltpu.VMEM((GROUPS, STATE_ROWS + SHARE, HEAD), BF16),
            pltpu.SemaphoreType.DMA((5,)),
        ],
    )
    third, sent, g0 = lax.optimization_barrier((third, sent, g0))
    a0, a1, a2, a3, s0, p1, p2, p3 = call(
        attend_kernel,
        [SMEM] * 2 + [VMEM] * 8,
        [head_block] * 5 + [triple] * 3,
        (base, place, x0, x1, x2, x3, third, g1, g2, g3),
        3 * small,
    )
    fourth = exchange(sent, ZC)
    width = SHARE + STATE_ROWS
    terms = call(
        weight_kernel,
        [HBM] * 4 + [VMEM] * 4,
        [shape((GROUPS, width, HEAD), BF16)],
        (cotangent, cot_c, cot_z, cot_zc, a0, a1, a2, a3),
        large,
        limit=SOME,
        scratch_shapes=[
            pltpu.VMEM((4, TOKENS, MODEL), BF16),
            pltpu.SemaphoreType.DMA((CHUNKS, 4)),
        ],
    )
    fourth, terms = lax.optimization_barrier((fourth, terms))
    inside, total = call(
        after_kernel,
        [VMEM],
        [shape((MEMBERS, STATE_ROWS, HEAD), F32), shape((STATE_ROWS, HEAD), BF16)],
        (fourth,),
        small,
        limit=ROOM,
    )
    terms = terms.at[:, SHARE:, :].set(total[None])
    got = exchange(terms, XY)

    p1, p2, p3, weight, _ = lax.optimization_barrier((p1, p2, p3, second, total))
    w0 = [weight[: GROUPS // 2, STATE_ROWS:], weight[GROUPS // 2 :, STATE_ROWS:]]
    p1, p2, p3 = to_core(p1), to_odd(p2), to_both(p3)
    w1 = [to_core(w) for w in w0]
    ring = [(i, (i + 1) % 8) for i in range(8)]
    w2 = [lax.ppermute(w0[0], "z", ring), lax.ppermute(w0[1], "z", [(j, i) for i, j in ring])]
    got, w1 = lax.optimization_barrier((got, w1))
    back = call(
        reduce_kernel,
        [SMEM, VMEM, VMEM],
        [shape((MEMBERS, ROWS + STATE_ROWS, HEAD), BF16)],
        (group_id, got, inside),
        small,
        limit=ROOM,
    )
    back, w2, p1, p2, p3 = lax.optimization_barrier((back, w2, p1, p2, p3))
    w3 = [to_core(w) for w in w2]
    last = exchange(back, ZC)
    mixed = call(
        mixed_kernel,
        [VMEM] * 12,
        [shape((TOKENS, MODEL), BF16)],
        (a0, p1, p2, p3, *w0, *w1, *w2, *w3),
        large,
    )
    query_gradient, kg_local, vg_local = call(
        local_kernel,
        [SMEM] + [VMEM] * 8,
        [shape((TOKENS, FEATURES), BF16)] + [shape((TOKENS, FEATURES), F32)] * 2,
        (me, queries, keys, values, g0, s0, p1, p2, p3),
        6 * small,
        scratch_shapes=[pltpu.VMEM((HEADS, 2 * TOKENS, HEAD), BF16)],
    )
    last, mixed, kg_local = lax.optimization_barrier((last, mixed, kg_local))
    key_gradient, value_gradient, weight_grad = call(
        final_kernel,
        [VMEM] * 5,
        [shape((TOKENS, FEATURES), BF16)] * 2 + [shape((ROWS, FEATURES), F32)],
        (last, keys, values, kg_local, vg_local),
        2 * small,
        limit=ROOM,
    )
    return (mixed, query_gradient, key_gradient, value_gradient, weight_grad)


def solution(mesh):
    grid = Mesh(mesh.devices.reshape(4, 4, 8, 2), ("x", "y", "z", "c"))
    spec = P(("x", "y", "z", "c"), None)
    return jax.shard_map(
        body, mesh=grid, in_specs=(spec,) * 5, out_specs=(spec,) * 5, check_vma=False
    )
```

time: 131 us -> 125 us (0.954)
  waiting for transfers between devices: 53.9 us -> 49.6 us
    pallas_call x9 -> x11, Pallas kernels: 15.7 us -> 25.8 us  [call(): pl.pallas_call(kernel, in_specs=ins, out_specs=VMEM if one else [VMEM] *...]
    pallas_call x2 -> x0, Pallas kernels: 9.91 us -> none  [the longest x1 5.24 us: body(): pl.pallas_call(gradient_kernel, grid=(CHUNKS,), in_specs=[SMEM] + [wide]...]
    ppermute x5 -> x3, waiting for transfers between devices: 21.8 us -> 17.5 us  [to_odd(): return lax.ppermute(x, 'z', [(i, i ^ 1) for i in range(8)])]
    ppermute x5 -> x3, starting transfers between devices: 5.3 us -> 1.89 us  [to_odd(): return lax.ppermute(x, 'z', [(i, i ^ 1) for i in range(8)])]
    ppermute x3 -> x2, waiting for transfers between devices: 1.66 us -> 0.01 us  [to_both(): return lax.ppermute(x, ZC, [(i, i ^ 3) for i in range(MEMBERS)])]
    unnamed x40 -> x42, local copies, waits for them, and re-layouts: 3.5 us -> 1.92 us
    ppermute x0 -> x2, starting transfers between devices: none -> 1.47 us  [the longest x1 1.17 us: body(): lax.ppermute(w0[0], 'z', ring)]
    all_to_all x6, waiting for transfers between devices: 30.5 us -> 31.9 us  [exchange(): return lax.all_to_all(value, axes, 0, 0, tiled=True)]
  transfers between devices with their start and end apart: 21 -> 21, of which waited for: 8 -> 8; matrix products, arithmetic and copies ran while one was open for 1% -> 1% of each run, Pallas kernels for 19% -> 20%
where the time goes in v4:
time: 125 us; the launch traced here: 124 us
  waiting for transfers between devices  49.6 us (40%)
  starting transfers between devices  44.6 us (36%)
  Pallas kernels  25.8 us (21%)
  local copies, waits for them, and re-layouts  3.53 us (3%)
    all_to_all x6, starting transfers between devices, exchange(): return lax.all_to_all(value, axes, 0, 0, tiled=True)  33 us
    all_to_all x6, waiting for transfers between devices, exchange(): return lax.all_to_all(value, axes, 0, 0, tiled=True)  31.9 us
    pallas_call x11, Pallas kernels, call(): pl.pallas_call(kernel, in_specs=ins, out_specs=VMEM if one else [VMEM] *...  25.8 us
    ppermute x3, waiting for transfers between devices, to_odd(): return lax.ppermute(x, 'z', [(i, i ^ 1) for i in range(8)])  17.5 us
    ppermute x8, starting transfers between devices, to_core(): return lax.ppermute(x, 'c', [(0, 1), (1, 0)])  6.06 us
  transfers between devices with their start and end apart: 21, of which 8 were waited for; matrix products, arithmetic and copies ran while one was open for 1% of the time, Pallas kernels for 20%

profile of v4, /device:TPU:1, one launch (start us, length us, event | category | flops | bytes accessed | tf_op | source)
XLA Modules:
  0.0 124.5 jit_solution(4339208000686808268)
XLA Ops:
  0.6 3.3 %collective-permute-start = (bf16[128,4096]{1,0:T(8,128)(2,1)}, bf16[128,4096]{1,0:T(8,128)(2,1)S(1)}, u32[]{:S(2)}, u32[]{:S(2)}) collective-permute-start(bf16[128,4096]{1,0:T(8,128)(2,1)} %c0.3), channel_id=1, source_target_pairs={{0,1},{1,0},{2,3},{3,2},{4,5},{5,4},{6,7},{7,6},{8,9},{9,8},{10,11... | collective-permute-start | bytes 3145736 | tf_op jit(solution)/shard_map/ppermute | solution.py:281
  4.0 1.9 %shard_map.92 = (bf16[16,48,128]{2,1,0:T(8,128)(2,1)}, bf16[384,128]{1,0:T(8,128)(2,1)}, bf16[384,128]{1,0:T(8,128)(2,1)}, bf16[384,128]{1,0:T(8,128)(2,1)}, bf16[384,128]{1,0:T(8,128)(2,1)}) custom-call(s32[1]{0:T(128)} %bitcast.1.me, bf16[128,512]{1,0:T(8,128)(2,1)} %k.5, bf16[128,512]{1,0:T(8,128)(2,1)} %v.5, bf16[16,512]{1,0:T(8,128)(2,1)} %w.1, ...), custom_call_target="tpu_custom_call" | custom-call | flops 16777216 | bytes 999428 | tf_op jit(solution)/shard_map/pallas_call | solution.py:48
  5.9 6.9 %all-to-all-start = ((bf16[16,48,128]{2,1,0:T(8,128)(2,1)}), bf16[16,48,128]{2,1,0:T(8,128)(2,1)S(1)}, u32[]{:S(2)}, u32[]{:S(2)}) async-start(bf16[16,48,128]{2,1,0:T(8,128)(2,1)} %get-tuple-element.72), calls=%async_computation | async-start | bytes 393216 | tf_op jit(solution)/shard_map/all_to_all | solution.py:266
  12.8 0.2 collective-permute-start.1
  12.9 1.6 %collective-permute-start.2 = (bf16[384,128]{1,0:T(8,128)(2,1)}, bf16[384,128]{1,0:T(8,128)(2,1)S(1)}, u32[]{:S(2)}, u32[]{:S(2)}) collective-permute-start(bf16[384,128]{1,0:T(8,128)(2,1)} %get-tuple-element.75), channel_id=1, source_target_pairs={{0,2},{2,0},{4,6},{6,4},{8,10},{10,8},{12,14},{14,12},{1,3},{3,1},... | collective-permute-start | bytes 294920 | tf_op jit(solution)/shard_map/ppermute | solution.py:284
  14.5 0.4 collective-permute-start.3
  14.9 8.5 %all-to-all-done.first = bf16[16,48,128]{2,1,0:T(8,128)(2,1)S(1)} async-done(((bf16[16,48,128]{2,1,0:T(8,128)(2,1)}), bf16[16,48,128]{2,1,0:T(8,128)(2,1)S(1)}, u32[]{:S(2)}, u32[]{:S(2)}) %all-to-all-start) | async-done | bytes 196640 | tf_op jit(solution)/shard_map/all_to_all | solution.py:266
  23.4 1.2 shard_map.93
  24.7 0.0 copy-start.6
  24.7 0.1 collective-permute-start.4
  24.8 0.5 copy-done.13
  25.3 0.1 copy-done.14
  25.4 0.1 copy-done.15
  25.4 0.3 copy-done.6
  25.7 6.8 %all-to-all-start.1 = ((bf16[16,288,128]{2,1,0:T(8,128)(2,1)}), bf16[16,288,128]{2,1,0:T(8,128)(2,1)S(1)}, u32[]{:S(2)}, u32[]{:S(2)}) async-start(bf16[16,288,128]{2,1,0:T(8,128)(2,1)} %get-tuple-element.77), calls=%async_computation.1 | async-start | bytes 2359296 | tf_op jit(solution)/shard_map/all_to_all | solution.py:266
  32.5 17.5 %collective-permute-done.4.c2 = bf16[128,4096]{1,0:T(8,128)(2,1)S(1)} collective-permute-done((bf16[128,4096]{1,0:T(8,128)(2,1)}, bf16[128,4096]{1,0:T(8,128)(2,1)S(1)}, u32[]{:S(2)}, u32[]{:S(2)}) %collective-permute-start.4) | collective-permute-done | bytes 1048608 | tf_op jit(solution)/shard_map/ppermute | solution.py:284
  50.0 0.2 collective-permute-start.5
  50.2 1.7 %all-to-all-done.1.second.w = bf16[16,288,128]{2,1,0:T(8,128)(2,1)S(1)} async-done(((bf16[16,288,128]{2,1,0:T(8,128)(2,1)}), bf16[16,288,128]{2,1,0:T(8,128)(2,1)S(1)}, u32[]{:S(2)}, u32[]{:S(2)}) %all-to-all-start.1) | async-done | bytes 1179680 | tf_op jit(solution)/shard_map/all_to_all | solution.py:266
  51.9 0.8 shard_map.94
  52.7 5.9 %all-to-all-start.2 = ((bf16[16,32,128]{2,1,0:T(8,128)(2,1)}), bf16[16,32,128]{2,1,0:T(8,128)(2,1)S(1)}, u32[]{:S(2)}, u32[]{:S(2)}) async-start(bf16[16,32,128]{2,1,0:T(8,128)(2,1)} %shard_map.94), calls=%async_computation.2 | async-start | bytes 262144 | tf_op jit(solution)/shard_map/all_to_all | solution.py:266
  58.6 0.9 copy-done.8
  59.6 5.5 %shard_map.95 = (bf16[128,128]{1,0:T(8,128)(2,1)}, bf16[128,128]{1,0:T(8,128)(2,1)}, bf16[128,128]{1,0:T(8,128)(2,1)}, bf16[128,128]{1,0:T(8,128)(2,1)}, bf16[16,32,128]{2,1,0:T(8,128)(2,1)}) custom-call(s32[1]{0:T(128)} %bitcast.2.base, s32[1]{0:T(128)} %bitcast.3.place, bf16[128,4096]{1,0:T(8,128)(2,1)} %c0.3, bf16[128,4096]{1,0:T(8,128)(2,1)} %copy-done.6, ...), custom_call_target="tpu_custom_call" | custom-call | flops 536870912 | bytes 6029320 | tf_op jit(solution)/shard_map/pallas_call | solution.py:48
  65.1 2.6 %all-to-all-done.2.got = bf16[16,32,128]{2,1,0:T(8,128)(2,1)S(1)} async-done(((bf16[16,32,128]{2,1,0:T(8,128)(2,1)}), bf16[16,32,128]{2,1,0:T(8,128)(2,1)S(1)}, u32[]{:S(2)}, u32[]{:S(2)}) %all-to-all-start.2) | async-done | bytes 131104 | tf_op jit(solution)/shard_map/all_to_all | solution.py:266
  67.8 4.6 %all-to-all-start.3 = ((bf16[16,32,128]{2,1,0:T(8,128)(2,1)}), bf16[16,32,128]{2,1,0:T(8,128)(2,1)S(1)}, u32[]{:S(2)}, u32[]{:S(2)}) async-start(bf16[16,32,128]{2,1,0:T(8,128)(2,1)} %get-tuple-element.87), calls=%async_computation.3 | async-start | bytes 262144 | tf_op jit(solution)/shard_map/all_to_all | solution.py:266
  72.4 2.2 %shard_map.96 = (bf16[128,128]{1,0:T(8,128)(2,1)}, bf16[128,128]{1,0:T(8,128)(2,1)}, bf16[128,128]{1,0:T(8,128)(2,1)}, bf16[128,128]{1,0:T(8,128)(2,1)}, bf16[12...) custom-call(s32[1]{0:T(128)} %bitcast.2.base, ...), custom_call_target="tpu_custom_call" | custom-call | flops 50331648 | bytes 1081352 | tf_op jit(solution)/shard_map/pallas_call | solution.py:48
  74.6 4.4 %shard_map.97 = bf16[16,288,128]{2,1,0:T(8,128)(2,1)} custom-call(bf16[128,4096]{1,0:T(8,128)(2,1)} %c0.3, bf16[128,4096]{1,0:T(8,128)(2,1)} %copy-done.6, bf16[128,4096]{1,0:T(8,128)(2,1)} %copy-done.7, bf16[128,4096]{1,0:T(8,128)(2,1)} %copy-done.8, bf16[128,128]{1,0:T(8,128)(2,1)} %get-tuple-element.92.a0, bf16[128,128]{1,0:T(8,128)(2,1)} %get-tuple-element.93.a1, ...), custom_call_target="tpu_custom_call" | custom-call | flops 536870912 | bytes 5505024 | tf_op jit(solution)/shard_map/pallas_call | solution.py:48
  79.1 2.5 %all-to-all-done.3.first = bf16[16,32,128]{2,1,0:T(8,128)(2,1)S(1)} async-done(((bf16[16,32,128]{2,1,0:T(8,128)(2,1)}), bf16[16,32,128]{2,1,0:T(8,128)(2,1)S(1)}, u32[]{:S(2)}, u32[]{:S(2)}) %all-to-all-start.3) | async-done | bytes 131104 | tf_op jit(solution)/shard_map/all_to_all | solution.py:266
  81.6 0.7 broadcast_dynamic-update-slice_fusion
  82.3 4.7 %all-to-all-start.4 = ((bf16[16,288,128]{2,1,0:T(8,128)(2,1)}), bf16[16,288,128]{2,1,0:T(8,128)(2,1)S(1)}, u32[]{:S(2)}, u32[]{:S(2)}) async-start(bf16[16,288,128]{2,1,0:T(8,128)(2,1)} %broadcast_dynamic-update-slice_fusion), calls=%async_computation.4 | async-start | bytes 2359296 | tf_op jit(solution)/shard_map/all_to_all | solution.py:266
  87.0 0.9 fusion
  87.9 0.5 collective-permute-start.6
  88.4 0.3 collective-permute-start.9
  88.7 1.2 collective-permute-start.8
  89.9 0.6 collective-permute-start.10
  90.4 0.1 collective-permute-done.7.refs_3_
  90.5 0.2 collective-permute-start.11
  90.7 0.0 collective-permute-done.6.refs_2_
  90.8 1.8 %collective-permute-start.12 = (bf16[384,128]{1,0:T(8,128)(2,1)S(1)}, bf16[384,128]{1,0:T(8,128)(2,1)S(1)}, u32[]{:S(2)}, u32[]{:S(2)}) collective-permute-start(bf16[384,128]{1,0:T(8,128)(2,1)S(1)} %copy-done.19), channel_id=1, source_target_pairs={{0,3},{1,2},{2,1},{3,0},{4,7},{5,6},{6,5},{7,4},{8,11},{9,10},{10,... | collective-permute-start | bytes 294920 | tf_op jit(solution)/shard_map/ppermute | solution.py:287
  92.6 14.2 %all-to-all-done.4.got = bf16[16,288,128]{2,1,0:T(8,128)(2,1)S(1)} async-done(((bf16[16,288,128]{2,1,0:T(8,128)(2,1)}), bf16[16,288,128]{2,1,0:T(8,128)(2,1)S(1)}, u32[]{:S(2)}, u32[]{:S(2)}) %all-to-all-start.4) | async-done | bytes 1179680 | tf_op jit(solution)/shard_map/all_to_all | solution.py:266
  106.7 0.9 shard_map.99
  107.6 0.0 copy-start.17
  107.7 1.2 collective-permute-start.13
  108.9 0.1 collective-permute-start.14
  109.0 4.2 %all-to-all-start.5 = ((bf16[16,48,128]{2,1,0:T(8,128)(2,1)}), bf16[16,48,128]{2,1,0:T(8,128)(2,1)S(1)}, u32[]{:S(2)}, u32[]{:S(2)}) async-start(bf16[16,48,128]{2,1,0:T(8,128)(2,1)} %shard_map.99), calls=%async_computation.5 | async-start | bytes 393216 | tf_op jit(solution)/shard_map/all_to_all | solution.py:266
  113.2 2.9 %shard_map.101 = (bf16[128,512]{1,0:T(8,128)(2,1)}, f32[128,512]{1,0:T(8,128)}, f32[128,512]{1,0:T(8,128)}) custom-call(s32[1]{0:T(128)} %bitcast.1.me, bf16[128,512]{1,0:T(8,128)(2,1)} %q.3, bf16[128,512]{1,0:T(8,128)(2,1)} %k.5, bf16[128,512]{1,0:T(8,128)(2,1)} %v.5, bf16[128,128]{1,0:T(8,128)(2,1)} %get-tuple-element.116.g0, ...), custom_call_target="tpu_custom_call" | custom-call | flops 100663296 | bytes 1409028 | tf_op jit(solution)/shard_map/pallas_call | solution.py:48
  116.2 4.8 %shard_map.100 = bf16[128,4096]{1,0:T(8,128)(2,1)} custom-call(bf16[128,128]{1,0:T(8,128)(2,1)} %get-tuple-element.92.a0, bf16[384,128]{1,0:T(8,128)(2,1)} %copy-done.16, bf16[384,128]{1,0:T(8,128)(2,1)} %copy-done.17, bf16[384,128]{1,0:T(8,128)(2,1)} %copy-done.18, bf16[8,256,128]{2,1,0:T(8,128)(2,1)} %get-tuple-element.128.refs_0_, ...), custom_call_target="tpu_custom_call" | custom-call | flops 536870912 | bytes 5570560 | tf_op jit(solution)/shard_map/pallas_call | solution.py:48
  121.0 2.5 %all-to-all-done.5.got = bf16[16,48,128]{2,1,0:T(8,128)(2,1)S(1)} async-done(((bf16[16,48,128]{2,1,0:T(8,128)(2,1)}), bf16[16,48,128]{2,1,0:T(8,128)(2,1)S(1)}, u32[]{:S(2)}, u32[]{:S(2)}) %all-to-all-start.5) | async-done | bytes 196640 | tf_op jit(solution)/shard_map/all_to_all | solution.py:266
  123.5 1.0 shard_map.102
  (49 shorter events, 0.1 us)
Async XLA Ops:
  0.6 24.1 %collective-permute-start = (bf16[128,4096]{1,0:T(8,128)(2,1)}, bf16[128,4096]{1,0:T(8,128)(2,1)S(1)}, u32[]{:S(2)}, u32[]{:S(2)}) collective-permute-start(bf16[128,4096]{1,0:T(8,128)(2,1)} %c0.3), channel_id=1, source_target_pairs={{0,1},{1,0},{2,3},{3,2},{4,5},{5,4},{6,7},{7,6},{8,9},{9,8},{10,11... | collective-permute-start | bytes 3145736 | tf_op jit(solution)/shard_map/ppermute | solution.py:281
  5.9 17.5 %all-to-all-start = ((bf16[16,48,128]{2,1,0:T(8,128)(2,1)}), bf16[16,48,128]{2,1,0:T(8,128)(2,1)S(1)}, u32[]{:S(2)}, u32[]{:S(2)}) async-start(bf16[16,48,128]{2,1,0:T(8,128)(2,1)} %get-tuple-element.72), calls=%async_computation | async-start | bytes 393216 | tf_op jit(solution)/shard_map/all_to_all | solution.py:266
  12.8 11.9 %collective-permute-start.1 = (bf16[384,128]{1,0:T(8,128)(2,1)}, bf16[384,128]{1,0:T(8,128)(2,1)S(1)}, u32[]{:S(2)}, u32[]{:S(2)}) collective-permute-start(bf16[384,128]{1,0:T(8,128)(2,1)} %get-tuple-element.74), channel_id=1, source_target_pairs={{0,1},{1,0},{2,3},{3,2},{4,5},{5,4},{6,7},{7,6},{8,9},{9,8},{10,11... | collective-permute-start | bytes 294920 | tf_op jit(solution)/shard_map/ppermute | solution.py:281
  12.9 11.7 %collective-permute-start.2 = (bf16[384,128]{1,0:T(8,128)(2,1)}, bf16[384,128]{1,0:T(8,128)(2,1)S(1)}, u32[]{:S(2)}, u32[]{:S(2)}) collective-permute-start(bf16[384,128]{1,0:T(8,128)(2,1)} %get-tuple-element.75), channel_id=1, source_target_pairs={{0,2},{2,0},{4,6},{6,4},{8,10},{10,8},{12,14},{14,12},{1,3},{3,1},... | collective-permute-start | bytes 294920 | tf_op jit(solution)/shard_map/ppermute | solution.py:284
  14.5 10.2 %collective-permute-start.3 = (bf16[384,128]{1,0:T(8,128)(2,1)}, bf16[384,128]{1,0:T(8,128)(2,1)S(1)}, u32[]{:S(2)}, u32[]{:S(2)}) collective-permute-start(bf16[384,128]{1,0:T(8,128)(2,1)} %get-tuple-element.76), channel_id=1, source_target_pairs={{0,3},{1,2},{2,1},{3,0},{4,7},{5,6},{6,5},{7,4},{8,11},{9,10},{10,... | collective-permute-start | bytes 294920 | tf_op jit(solution)/shard_map/ppermute | solution.py:287
  24.7 0.6 copy-start.13
  24.7 0.7 copy-start.14
  24.7 0.7 copy-start.15
  24.7 1.0 copy-start.6
  24.7 25.3 %collective-permute-start.4 = (bf16[128,4096]{1,0:T(8,128)(2,1)}, bf16[128,4096]{1,0:T(8,128)(2,1)S(1)}, u32[]{:S(2)}, u32[]{:S(2)}) collective-permute-start(bf16[128,4096]{1,0:T(8,128)(2,1)} %c0.3), channel_id=1, source_target_pairs={{0,2},{2,0},{4,6},{6,4},{8,10},{10,8},{12,14},{14,12},{1,3},{3,1},... | collective-permute-start | bytes 3145736 | tf_op jit(solution)/shard_map/ppermute | solution.py:284
  25.7 26.2 %all-to-all-start.1 = ((bf16[16,288,128]{2,1,0:T(8,128)(2,1)}), bf16[16,288,128]{2,1,0:T(8,128)(2,1)S(1)}, u32[]{:S(2)}, u32[]{:S(2)}) async-start(bf16[16,288,128]{2,1,0:T(8,128)(2,1)} %get-tuple-element.77), calls=%async_computation.1 | async-start | bytes 2359296 | tf_op jit(solution)/shard_map/all_to_all | solution.py:266
  50.0 8.6 %copy-start.7 = (bf16[128,4096]{1,0:T(8,128)(2,1)}, bf16[128,4096]{1,0:T(8,128)(2,1)S(1)}, u32[]{:S(2)}) copy-start(bf16[128,4096]{1,0:T(8,128)(2,1)S(1)} %collective-permute-done.4.c2) | copy-start | bytes 3145732
  50.0 8.6 %collective-permute-start.5 = (bf16[128,4096]{1,0:T(8,128)(2,1)S(1)}, bf16[128,4096]{1,0:T(8,128)(2,1)S(1)}, u32[]{:S(2)}, u32[]{:S(2)}) collective-permute-start(bf16[128,4096]{1,0:T(8,128)(2,1)S(1)} %collective-permute-done.4.c2), channel_id=1, source_target_pairs={{0,1},{1,0},{2,3},{3,2},{4,5},{5,4},{6,7},{7,6},{8,9},{9,8},{10,11... | collective-permute-start | bytes 3145736 | tf_op jit(solution)/shard_map/ppermute | solution.py:281
  51.9 6.7 %copy-start = (bf16[16,288,128]{2,1,0:T(8,128)(2,1)}, bf16[16,288,128]{2,1,0:T(8,128)(2,1)S(1)}, u32[]{:S(2)}) copy-start(bf16[16,288,128]{2,1,0:T(8,128)(2,1)S(1)} %all-to-all-done.1.second.w) | copy-start | bytes 3538948
  52.7 15.1 %all-to-all-start.2 = ((bf16[16,32,128]{2,1,0:T(8,128)(2,1)}), bf16[16,32,128]{2,1,0:T(8,128)(2,1)S(1)}, u32[]{:S(2)}, u32[]{:S(2)}) async-start(bf16[16,32,128]{2,1,0:T(8,128)(2,1)} %shard_map.94), calls=%async_computation.2 | async-start | bytes 262144 | tf_op jit(solution)/shard_map/all_to_all | solution.py:266
  58.6 1.0 copy-start.8
  67.8 4.6 %copy-start.10 = (bf16[16,32,128]{2,1,0:T(8,128)(2,1)}, bf16[16,32,128]{2,1,0:T(8,128)(2,1)S(1)}, u32[]{:S(2)}) copy-start(bf16[16,32,128]{2,1,0:T(8,128)(2,1)S(1)} %all-to-all-done.2.got) | copy-start | bytes 393220
  67.8 13.8 %all-to-all-start.3 = ((bf16[16,32,128]{2,1,0:T(8,128)(2,1)}), bf16[16,32,128]{2,1,0:T(8,128)(2,1)S(1)}, u32[]{:S(2)}, u32[]{:S(2)}) async-start(bf16[16,32,128]{2,1,0:T(8,128)(2,1)} %get-tuple-element.87), calls=%async_computation.3 | async-start | bytes 262144 | tf_op jit(solution)/shard_map/all_to_all | solution.py:266
  82.3 4.7 %copy-start.1 = (bf16[16,288,128]{2,1,0:T(8,128)(2,1)S(1)}, bf16[16,288,128]{2,1,0:T(8,128)(2,1)}, u32[]{:S(2)}) copy-start(bf16[16,288,128]{2,1,0:T(8,128)(2,1)} %copy-done) | copy-start | bytes 3538948
  82.3 24.5 %all-to-all-start.4 = ((bf16[16,288,128]{2,1,0:T(8,128)(2,1)}), bf16[16,288,128]{2,1,0:T(8,128)(2,1)S(1)}, u32[]{:S(2)}, u32[]{:S(2)}) async-start(bf16[16,288,128]{2,1,0:T(8,128)(2,1)} %broadcast_dynamic-update-slice_fusion), calls=%async_computation.4 | async-start | bytes 2359296 | tf_op jit(solution)/shard_map/all_to_all | solution.py:266
  86.9 3.6 %copy-start.20 = (bf16[384,128]{1,0:T(8,128)(2,1)S(1)}, bf16[384,128]{1,0:T(8,128)(2,1)}, u32[]{:S(2)}) copy-start(bf16[384,128]{1,0:T(8,128)(2,1)} %get-tuple-element.106) | copy-start | bytes 294916
  86.9 3.8 %copy-start.19 = (bf16[384,128]{1,0:T(8,128)(2,1)S(1)}, bf16[384,128]{1,0:T(8,128)(2,1)}, u32[]{:S(2)}) copy-start(bf16[384,128]{1,0:T(8,128)(2,1)} %get-tuple-element.107) | copy-start | bytes 294916
  87.9 28.3 %copy-start.9 = (bf16[8,256,128]{2,1,0:T(8,128)(2,1)}, bf16[8,256,128]{2,1,0:T(8,128)(2,1)S(1)}, u32[]{:S(2)}) copy-start(bf16[8,256,128]{2,1,0:T(8,128)(2,1)S(1)} %get-tuple-element.127.refs_1_) | copy-start | bytes 1572868
  87.9 2.6 %collective-permute-start.7 = (bf16[8,256,128]{2,1,0:T(8,128)(2,1)S(1)}, bf16[8,256,128]{2,1,0:T(8,128)(2,1)S(1)}, u32[]{:S(2)}, u32[]{:S(2)}) collective-permute-start(bf16[8,256,128]{2,1,0:T(8,128)(2,1)S(1)} %get-tuple-element.127.refs_1_), channel_id=1, source_target_pairs={{0,1},{1,0},{2,3},{3,2},{4,5},{5,4},{6,7},{7,6},{8,9},{9,8},{10,11... | collective-permute-start | bytes 1572872 | tf_op jit(solution)/shard_map/ppermute | solution.py:281
  87.9 2.9 %collective-permute-start.6 = (bf16[8,256,128]{2,1,0:T(8,128)(2,1)}, bf16[8,256,128]{2,1,0:T(8,128)(2,1)S(1)}, u32[]{:S(2)}, u32[]{:S(2)}) collective-permute-start(bf16[8,256,128]{2,1,0:T(8,128)(2,1)} %get-tuple-element.128.refs_0_), channel_id=1, source_target_pairs={{0,1},{1,0},{2,3},{3,2},{4,5},{5,4},{6,7},{7,6},{8,9},{9,8},{10,11... | collective-permute-start | bytes 1572872 | tf_op jit(solution)/shard_map/ppermute | solution.py:281
  88.4 19.3 %collective-permute-start.9 = (bf16[8,256,128]{2,1,0:T(8,128)(2,1)S(1)}, bf16[8,256,128]{2,1,0:T(8,128)(2,1)}, u32[]{:S(2)}, u32[]{:S(2)}) collective-permute-start(bf16[8,256,128]{2,1,0:T(8,128)(2,1)S(1)} %get-tuple-element.127.refs_1_), channel_id=1, source_target_pairs={{2,0},{4,2},{6,4},{8,6},{10,8},{12,10},{14,12},{0,14},{3,1},{5,3},... | collective-permute-start | bytes 1572872 | tf_op jit(solution)/shard_map/ppermute | solution.py:380
  88.7 19.0 %collective-permute-start.8 = (bf16[8,256,128]{2,1,0:T(8,128)(2,1)}, bf16[8,256,128]{2,1,0:T(8,128)(2,1)}, u32[]{:S(2)}, u32[]{:S(2)}) collective-permute-start(bf16[8,256,128]{2,1,0:T(8,128)(2,1)} %get-tuple-element.128.refs_0_), channel_id=1, source_target_pairs={{0,2},{2,4},{4,6},{6,8},{8,10},{10,12},{12,14},{14,0},{1,3},{3,5},... | collective-permute-start | bytes 1572872 | tf_op jit(solution)/shard_map/ppermute | solution.py:380
  89.9 17.8 %collective-permute-start.10 = (bf16[384,128]{1,0:T(8,128)(2,1)}, bf16[384,128]{1,0:T(8,128)(2,1)S(1)}, u32[]{:S(2)}, u32[]{:S(2)}) collective-permute-start(bf16[384,128]{1,0:T(8,128)(2,1)} %get-tuple-element.105), channel_id=1, source_target_pairs={{0,1},{1,0},{2,3},{3,2},{4,5},{5,4},{6,7},{7,6},{8,9},{9,8},{10,11... | collective-permute-start | bytes 294920 | tf_op jit(solution)/shard_map/ppermute | solution.py:281
  90.5 25.7 %copy-start.11 = (bf16[8,256,128]{2,1,0:T(8,128)(2,1)}, bf16[8,256,128]{2,1,0:T(8,128)(2,1)S(1)}, u32[]{:S(2)}) copy-start(bf16[8,256,128]{2,1,0:T(8,128)(2,1)S(1)} %collective-permute-done.7.refs_3_) | copy-start | bytes 1572868
  90.5 17.1 %collective-permute-start.11 = (bf16[384,128]{1,0:T(8,128)(2,1)S(1)}, bf16[384,128]{1,0:T(8,128)(2,1)S(1)}, u32[]{:S(2)}, u32[]{:S(2)}) collective-permute-start(bf16[384,128]{1,0:T(8,128)(2,1)S(1)} %copy-done.20), channel_id=1, source_target_pairs={{0,2},{2,0},{4,6},{6,4},{8,10},{10,8},{12,14},{14,12},{1,3},{3,1},... | collective-permute-start | bytes 294920 | tf_op jit(solution)/shard_map/ppermute | solution.py:284
  90.8 25.4 %copy-start.12 = (bf16[8,256,128]{2,1,0:T(8,128)(2,1)}, bf16[8,256,128]{2,1,0:T(8,128)(2,1)S(1)}, u32[]{:S(2)}) copy-start(bf16[8,256,128]{2,1,0:T(8,128)(2,1)S(1)} %collective-permute-done.6.refs_2_) | copy-start | bytes 1572868
  90.8 16.9 %collective-permute-start.12 = (bf16[384,128]{1,0:T(8,128)(2,1)S(1)}, bf16[384,128]{1,0:T(8,128)(2,1)S(1)}, u32[]{:S(2)}, u32[]{:S(2)}) collective-permute-start(bf16[384,128]{1,0:T(8,128)(2,1)S(1)} %copy-done.19), channel_id=1, source_target_pairs={{0,3},{1,2},{2,1},{3,0},{4,7},{5,6},{6,5},{7,4},{8,11},{9,10},{10,... | collective-permute-start | bytes 294920 | tf_op jit(solution)/shard_map/ppermute | solution.py:287
  107.6 5.6 %copy-start.16 = (bf16[384,128]{1,0:T(8,128)(2,1)}, bf16[384,128]{1,0:T(8,128)(2,1)S(1)}, u32[]{:S(2)}) copy-start(bf16[384,128]{1,0:T(8,128)(2,1)S(1)} %collective-permute-done.10.p1) | copy-start | bytes 294916
  107.6 5.5 %copy-start.17 = (bf16[384,128]{1,0:T(8,128)(2,1)}, bf16[384,128]{1,0:T(8,128)(2,1)S(1)}, u32[]{:S(2)}) copy-start(bf16[384,128]{1,0:T(8,128)(2,1)S(1)} %collective-permute-done.11.p2) | copy-start | bytes 294916
  107.7 5.5 %copy-start.18 = (bf16[384,128]{1,0:T(8,128)(2,1)}, bf16[384,128]{1,0:T(8,128)(2,1)S(1)}, u32[]{:S(2)}) copy-start(bf16[384,128]{1,0:T(8,128)(2,1)S(1)} %collective-permute-done.12.p3) | copy-start | bytes 294916
  107.7 8.5 %collective-permute-start.13 = (bf16[8,256,128]{2,1,0:T(8,128)(2,1)}, bf16[8,256,128]{2,1,0:T(8,128)(2,1)}, u32[]{:S(2)}, u32[]{:S(2)}) collective-permute-start(bf16[8,256,128]{2,1,0:T(8,128)(2,1)} %collective-permute-done.8.refs_4_), channel_id=1, source_target_pairs={{0,1},{1,0},{2,3},{3,2},{4,5},{5,4},{6,7},{7,6},{8,9},{9,8},{10,11... | collective-permute-start | bytes 1572872 | tf_op jit(solution)/shard_map/ppermute | solution.py:281
  108.9 7.4 %collective-permute-start.14 = (bf16[8,256,128]{2,1,0:T(8,128)(2,1)}, bf16[8,256,128]{2,1,0:T(8,128)(2,1)}, u32[]{:S(2)}, u32[]{:S(2)}) collective-permute-start(bf16[8,256,128]{2,1,0:T(8,128)(2,1)} %collective-permute-done.9.refs_5_), channel_id=1, source_target_pairs={{0,1},{1,0},{2,3},{3,2},{4,5},{5,4},{6,7},{7,6},{8,9},{9,8},{10,11... | collective-permute-start | bytes 1572872 | tf_op jit(solution)/shard_map/ppermute | solution.py:281
  109.0 14.5 %all-to-all-start.5 = ((bf16[16,48,128]{2,1,0:T(8,128)(2,1)}), bf16[16,48,128]{2,1,0:T(8,128)(2,1)S(1)}, u32[]{:S(2)}, u32[]{:S(2)}) async-start(bf16[16,48,128]{2,1,0:T(8,128)(2,1)} %shard_map.99), calls=%async_computation.5 | async-start | bytes 393216 | tf_op jit(solution)/shard_map/all_to_all | solution.py:266
  116.2 7.3 %copy-start.2 = (bf16[128,512]{1,0:T(8,128)(2,1)S(1)}, bf16[128,512]{1,0:T(8,128)(2,1)}, u32[]{:S(2)}) copy-start(bf16[128,512]{1,0:T(8,128)(2,1)} %k.5) | copy-start | bytes 393220
  116.2 7.3 %copy-start.3 = (bf16[128,512]{1,0:T(8,128)(2,1)S(1)}, bf16[128,512]{1,0:T(8,128)(2,1)}, u32[]{:S(2)}) copy-start(bf16[128,512]{1,0:T(8,128)(2,1)} %v.5) | copy-start | bytes 393220
  116.2 7.3 %copy-start.4 = (f32[128,512]{1,0:T(8,128)S(1)}, f32[128,512]{1,0:T(8,128)}, u32[]{:S(2)}) copy-start(f32[128,512]{1,0:T(8,128)} %get-tuple-element.122.kg_local) | copy-start | bytes 786436
  116.2 7.3 %copy-start.5 = (f32[128,512]{1,0:T(8,128)S(1)}, f32[128,512]{1,0:T(8,128)}, u32[]{:S(2)}) copy-start(f32[128,512]{1,0:T(8,128)} %get-tuple-element.123.vg_local) | copy-start | bytes 786436

commit v5 on v4

--- a/solution.py
+++ b/solution.py
@@ -187,8 +187,9 @@
         out[:, j * SHARE : (j + 1) * SHARE] = mul(left, right, NT).astype(BF16)
 
 
-def weight_kernel(c0, c1, c2, c3, a0, a1, a2, a3, out, cots, sems):
+def weight_kernel(c0, c1, c2, c3, a0, a1, a2, a3, out, cots, result, sems, out_sems):
     width = MODEL // CHUNKS
+    part = GROUPS // CHUNKS
     copies = []
     for step in range(CHUNKS):
         at = pl.ds(step * width, width)
@@ -202,16 +203,24 @@
         for copy in group:
             copy.start()
     turned = jnp.concatenate([a[...].T for a in (a0, a1, a2, a3)], axis=1)
-    for j in range(GROUPS):
-        if j % (GROUPS // CHUNKS) == 0:
-            for copy in copies[j // (GROUPS // CHUNKS)]:
-                copy.wait()
-        at = slice(j * SHARE, (j + 1) * SHARE)
-        right = cots[:, :, at].reshape(4 * TOKENS, SHARE)
-        term = mul(turned, right, NN).astype(BF16)
-        for half in range(2):
-            out[j, half * HEAD : (half + 1) * HEAD, :] = term[:, half * HEAD : (half + 1) * HEAD]
-        out[j, SHARE:, :] = jnp.zeros((STATE_ROWS, HEAD), BF16)
+    backs = []
+    for step in range(CHUNKS):
+        for copy in copies[step]:
+            copy.wait()
+        for j in range(step * part, (step + 1) * part):
+            at = slice(j * SHARE, (j + 1) * SHARE)
+            right = cots[:, :, at].reshape(4 * TOKENS, SHARE)
+            term = mul(turned, right, NN).astype(BF16)
+            for half in range(2):
+                result[j, half * HEAD : (half + 1) * HEAD, :] = term[
+                    :, half * HEAD : (half + 1) * HEAD
+                ]
+            result[j, SHARE:, :] = jnp.zeros((STATE_ROWS, HEAD), BF16)
+        at = pl.ds(step * part, part)
+        backs.append(pltpu.make_async_copy(result.at[at], out.at[at], out_sems.at[step]))
+        backs[-1].start()
+    for back in backs:
+        back.wait()
 
 
 def local_kernel(me, q, k, v, g0, s0, p1, p2, p3, qg, kg, vg, by_head):
@@ -348,18 +357,20 @@
     )
     fourth = exchange(sent, ZC)
     width = SHARE + STATE_ROWS
-    terms = call(
+    terms = pl.pallas_call(
         weight_kernel,
-        [HBM] * 4 + [VMEM] * 4,
-        [shape((GROUPS, width, HEAD), BF16)],
-        (cotangent, cot_c, cot_z, cot_zc, a0, a1, a2, a3),
-        large,
-        limit=SOME,
+        in_specs=[HBM] * 4 + [VMEM] * 4,
+        out_specs=HBM,
+        out_shape=shape((GROUPS, width, HEAD), BF16),
         scratch_shapes=[
             pltpu.VMEM((4, TOKENS, MODEL), BF16),
+            pltpu.VMEM((GROUPS, width, HEAD), BF16),
             pltpu.SemaphoreType.DMA((CHUNKS, 4)),
+            pltpu.SemaphoreType.DMA((CHUNKS,)),
         ],
-    )
+        compiler_params=pltpu.CompilerParams(vmem_limit_bytes=SOME),
+        cost_estimate=pl.CostEstimate(flops=large, bytes_accessed=6 << 20, transcendentals=0),
+    )(cotangent, cot_c, cot_z, cot_zc, a0, a1, a2, a3)
     fourth, terms = lax.optimization_barrier((fourth, terms))
     inside, total = call(
         after_kernel,

time: 125 us -> 125 us (level)
    pallas_call x11 -> x10, Pallas kernels: 25.8 us -> 21.4 us  [call(): pl.pallas_call(kernel, in_specs=ins, out_specs=VMEM if one else [VMEM] *...]
    pallas_call x0 -> x1, Pallas kernels: none -> 4.17 us  [body(): pl.pallas_call(weight_kernel, in_specs=[HBM] * 4 + [VMEM] * 4, out_specs=...]
where the time goes in v5:
time: 125 us; the launch traced here: 124 us
  waiting for transfers between devices  49.9 us (40%)
  starting transfers between devices  44.3 us (35%)
  Pallas kernels  25.5 us (20%)
  local copies, waits for them, and re-layouts  3.53 us (3%)
    all_to_all x6, starting transfers between devices, exchange(): return lax.all_to_all(value, axes, 0, 0, tiled=True)  32.7 us
    all_to_all x6, waiting for transfers between devices, exchange(): return lax.all_to_all(value, axes, 0, 0, tiled=True)  32.2 us
    pallas_call x10, Pallas kernels, call(): pl.pallas_call(kernel, in_specs=ins, out_specs=VMEM if one else [VMEM] *...  21.4 us
    ppermute x3, waiting for transfers between devices, to_odd(): return lax.ppermute(x, 'z', [(i, i ^ 1) for i in range(8)])  17.5 us
    ppermute x8, starting transfers between devices, to_core(): return lax.ppermute(x, 'c', [(0, 1), (1, 0)])  6.06 us
    pallas_call x1, Pallas kernels, body(): pl.pallas_call(weight_kernel, in_specs=[HBM] * 4 + [VMEM] * 4, out_specs=...  4.17 us
  transfers between devices with their start and end apart: 21, of which 8 were waited for; matrix products, arithmetic and copies ran while one was open for 1% of the time, Pallas kernels for 20%

profile of v5, /device:TPU:1, one launch (start us, length us, event | category | flops | bytes accessed | tf_op | source)
XLA Modules:
  0.0 124.2 jit_solution(16324378663689160190)
XLA Ops:
  0.6 3.3 %collective-permute-start = (bf16[128,4096]{1,0:T(8,128)(2,1)}, bf16[128,4096]{1,0:T(8,128)(2,1)S(1)}, u32[]{:S(2)}, u32[]{:S(2)}) collective-permute-start(bf16[128,4096]{1,0:T(8,128)(2,1)} %c0.3), channel_id=1, source_target_pairs={{0,1},{1,0},{2,3},{3,2},{4,5},{5,4},{6,7},{7,6},{8,9},{9,8},{10,11... | collective-permute-start | bytes 3145736 | tf_op jit(solution)/shard_map/ppermute | solution.py:290
  4.0 1.9 %shard_map.92 = (bf16[16,48,128]{2,1,0:T(8,128)(2,1)}, bf16[384,128]{1,0:T(8,128)(2,1)}, bf16[384,128]{1,0:T(8,128)(2,1)}, bf16[384,128]{1,0:T(8,128)(2,1)}, bf16[384,128]{1,0:T(8,128)(2,1)}) custom-call(s32[1]{0:T(128)} %bitcast.1.me, bf16[128,512]{1,0:T(8,128)(2,1)} %k.5, bf16[128,512]{1,0:T(8,128)(2,1)} %v.5, bf16[16,512]{1,0:T(8,128)(2,1)} %w.1, ...), custom_call_target="tpu_custom_call" | custom-call | flops 16777216 | bytes 999428 | tf_op jit(solution)/shard_map/pallas_call | solution.py:48
  5.9 6.9 %all-to-all-start = ((bf16[16,48,128]{2,1,0:T(8,128)(2,1)}), bf16[16,48,128]{2,1,0:T(8,128)(2,1)S(1)}, u32[]{:S(2)}, u32[]{:S(2)}) async-start(bf16[16,48,128]{2,1,0:T(8,128)(2,1)} %get-tuple-element.72), calls=%async_computation | async-start | bytes 393216 | tf_op jit(solution)/shard_map/all_to_all | solution.py:275
  12.8 0.2 collective-permute-start.1
  12.9 1.6 %collective-permute-start.2 = (bf16[384,128]{1,0:T(8,128)(2,1)}, bf16[384,128]{1,0:T(8,128)(2,1)S(1)}, u32[]{:S(2)}, u32[]{:S(2)}) collective-permute-start(bf16[384,128]{1,0:T(8,128)(2,1)} %get-tuple-element.75), channel_id=1, source_target_pairs={{0,2},{2,0},{4,6},{6,4},{8,10},{10,8},{12,14},{14,12},{1,3},{3,1},... | collective-permute-start | bytes 294920 | tf_op jit(solution)/shard_map/ppermute | solution.py:293
  14.5 0.4 collective-permute-start.3
  14.9 8.5 %all-to-all-done.first = bf16[16,48,128]{2,1,0:T(8,128)(2,1)S(1)} async-done(((bf16[16,48,128]{2,1,0:T(8,128)(2,1)}), bf16[16,48,128]{2,1,0:T(8,128)(2,1)S(1)}, u32[]{:S(2)}, u32[]{:S(2)}) %all-to-all-start) | async-done | bytes 196640 | tf_op jit(solution)/shard_map/all_to_all | solution.py:275
  23.4 1.2 shard_map.93
  24.7 0.0 copy-start.6
  24.7 0.1 collective-permute-start.4
  24.8 0.5 copy-done.13
  25.3 0.1 copy-done.14
  25.4 0.1 copy-done.15
  25.4 0.3 copy-done.6
  25.7 6.8 %all-to-all-start.1 = ((bf16[16,288,128]{2,1,0:T(8,128)(2,1)}), bf16[16,288,128]{2,1,0:T(8,128)(2,1)S(1)}, u32[]{:S(2)}, u32[]{:S(2)}) async-start(bf16[16,288,128]{2,1,0:T(8,128)(2,1)} %get-tuple-element.77), calls=%async_computation.1 | async-start | bytes 2359296 | tf_op jit(solution)/shard_map/all_to_all | solution.py:275
  32.5 17.5 %collective-permute-done.4.c2 = bf16[128,4096]{1,0:T(8,128)(2,1)S(1)} collective-permute-done((bf16[128,4096]{1,0:T(8,128)(2,1)}, bf16[128,4096]{1,0:T(8,128)(2,1)S(1)}, u32[]{:S(2)}, u32[]{:S(2)}) %collective-permute-start.4) | collective-permute-done | bytes 1048608 | tf_op jit(solution)/shard_map/ppermute | solution.py:293
  50.0 0.2 collective-permute-start.5
  50.2 1.7 %all-to-all-done.1.second.w = bf16[16,288,128]{2,1,0:T(8,128)(2,1)S(1)} async-done(((bf16[16,288,128]{2,1,0:T(8,128)(2,1)}), bf16[16,288,128]{2,1,0:T(8,128)(2,1)S(1)}, u32[]{:S(2)}, u32[]{:S(2)}) %all-to-all-start.1) | async-done | bytes 1179680 | tf_op jit(solution)/shard_map/all_to_all | solution.py:275
  51.9 0.8 shard_map.94
  52.7 5.9 %all-to-all-start.2 = ((bf16[16,32,128]{2,1,0:T(8,128)(2,1)}), bf16[16,32,128]{2,1,0:T(8,128)(2,1)S(1)}, u32[]{:S(2)}, u32[]{:S(2)}) async-start(bf16[16,32,128]{2,1,0:T(8,128)(2,1)} %shard_map.94), calls=%async_computation.2 | async-start | bytes 262144 | tf_op jit(solution)/shard_map/all_to_all | solution.py:275
  58.6 0.9 copy-done.8
  59.6 5.5 %shard_map.95 = (bf16[128,128]{1,0:T(8,128)(2,1)}, bf16[128,128]{1,0:T(8,128)(2,1)}, bf16[128,128]{1,0:T(8,128)(2,1)}, bf16[128,128]{1,0:T(8,128)(2,1)}, bf16[16,32,128]{2,1,0:T(8,128)(2,1)}) custom-call(s32[1]{0:T(128)} %bitcast.2.base, s32[1]{0:T(128)} %bitcast.3.place, bf16[128,4096]{1,0:T(8,128)(2,1)} %c0.3, bf16[128,4096]{1,0:T(8,128)(2,1)} %copy-done.6, ...), custom_call_target="tpu_custom_call" | custom-call | flops 536870912 | bytes 6029320 | tf_op jit(solution)/shard_map/pallas_call | solution.py:48
  65.1 2.6 %all-to-all-done.2.got = bf16[16,32,128]{2,1,0:T(8,128)(2,1)S(1)} async-done(((bf16[16,32,128]{2,1,0:T(8,128)(2,1)}), bf16[16,32,128]{2,1,0:T(8,128)(2,1)S(1)}, u32[]{:S(2)}, u32[]{:S(2)}) %all-to-all-start.2) | async-done | bytes 131104 | tf_op jit(solution)/shard_map/all_to_all | solution.py:275
  67.8 4.6 %all-to-all-start.3 = ((bf16[16,32,128]{2,1,0:T(8,128)(2,1)}), bf16[16,32,128]{2,1,0:T(8,128)(2,1)S(1)}, u32[]{:S(2)}, u32[]{:S(2)}) async-start(bf16[16,32,128]{2,1,0:T(8,128)(2,1)} %get-tuple-element.87), calls=%async_computation.3 | async-start | bytes 262144 | tf_op jit(solution)/shard_map/all_to_all | solution.py:275
  72.4 2.2 %shard_map.96 = (bf16[128,128]{1,0:T(8,128)(2,1)}, bf16[128,128]{1,0:T(8,128)(2,1)}, bf16[128,128]{1,0:T(8,128)(2,1)}, bf16[128,128]{1,0:T(8,128)(2,1)}, bf16[12...) custom-call(s32[1]{0:T(128)} %bitcast.2.base, ...), custom_call_target="tpu_custom_call" | custom-call | flops 50331648 | bytes 1081352 | tf_op jit(solution)/shard_map/pallas_call | solution.py:48
  74.6 4.2 %shard_map.97 = bf16[16,288,128]{2,1,0:T(8,128)(2,1)} custom-call(bf16[128,4096]{1,0:T(8,128)(2,1)} %c0.3, bf16[128,4096]{1,0:T(8,128)(2,1)} %copy-done.6, bf16[128,4096]{1,0:T(8,128)(2,1)} %copy-done.7, bf16[128,4096]{1,0:T(8,128)(2,1)} %copy-done.8, bf16[128,128]{1,0:T(8,128)(2,1)} %get-tuple-element.92.a0, bf16[128,128]{1,0:T(8,128)(2,1)} %get-tuple-element.93.a1, ...), custom_call_target="tpu_custom_call" | custom-call | flops 536870912 | bytes 6291456 | tf_op jit(solution)/shard_map/pallas_call | solution.py:360
  78.8 2.7 %all-to-all-done.3.first = bf16[16,32,128]{2,1,0:T(8,128)(2,1)S(1)} async-done(((bf16[16,32,128]{2,1,0:T(8,128)(2,1)}), bf16[16,32,128]{2,1,0:T(8,128)(2,1)S(1)}, u32[]{:S(2)}, u32[]{:S(2)}) %all-to-all-start.3) | async-done | bytes 131104 | tf_op jit(solution)/shard_map/all_to_all | solution.py:275
  81.6 0.7 broadcast_dynamic-update-slice_fusion
  82.3 4.7 %all-to-all-start.4 = ((bf16[16,288,128]{2,1,0:T(8,128)(2,1)}), bf16[16,288,128]{2,1,0:T(8,128)(2,1)S(1)}, u32[]{:S(2)}, u32[]{:S(2)}) async-start(bf16[16,288,128]{2,1,0:T(8,128)(2,1)} %broadcast_dynamic-update-slice_fusion), calls=%async_computation.4 | async-start | bytes 2359296 | tf_op jit(solution)/shard_map/all_to_all | solution.py:275
  87.0 0.9 fusion
  87.9 0.5 collective-permute-start.6
  88.4 0.0 collective-permute-start.9
  88.4 1.4 %collective-permute-start.8 = (bf16[8,256,128]{2,1,0:T(8,128)(2,1)}, bf16[8,256,128]{2,1,0:T(8,128)(2,1)}, u32[]{:S(2)}, u32[]{:S(2)}) collective-permute-start(bf16[8,256,128]{2,1,0:T(8,128)(2,1)} %get-tuple-element.128.refs_0_), channel_id=1, source_target_pairs={{0,2},{2,4},{4,6},{6,8},{8,10},{10,12},{12,14},{14,0},{1,3},{3,5},... | collective-permute-start | bytes 1572872 | tf_op jit(solution)/shard_map/ppermute | solution.py:391
  89.9 0.6 collective-permute-start.10
  90.4 0.1 collective-permute-done.7.refs_3_
  90.5 0.2 collective-permute-start.11
  90.7 0.0 collective-permute-done.6.refs_2_
  90.8 1.8 %collective-permute-start.12 = (bf16[384,128]{1,0:T(8,128)(2,1)S(1)}, bf16[384,128]{1,0:T(8,128)(2,1)S(1)}, u32[]{:S(2)}, u32[]{:S(2)}) collective-permute-start(bf16[384,128]{1,0:T(8,128)(2,1)S(1)} %copy-done.19), channel_id=1, source_target_pairs={{0,3},{1,2},{2,1},{3,0},{4,7},{5,6},{6,5},{7,4},{8,11},{9,10},{10,... | collective-permute-start | bytes 294920 | tf_op jit(solution)/shard_map/ppermute | solution.py:296
  92.6 14.2 %all-to-all-done.4.got = bf16[16,288,128]{2,1,0:T(8,128)(2,1)S(1)} async-done(((bf16[16,288,128]{2,1,0:T(8,128)(2,1)}), bf16[16,288,128]{2,1,0:T(8,128)(2,1)S(1)}, u32[]{:S(2)}, u32[]{:S(2)}) %all-to-all-start.4) | async-done | bytes 1179680 | tf_op jit(solution)/shard_map/all_to_all | solution.py:275
  106.7 0.9 shard_map.99
  107.7 1.2 collective-permute-start.13
  108.9 0.1 collective-permute-start.14
  109.0 3.9 %all-to-all-start.5 = ((bf16[16,48,128]{2,1,0:T(8,128)(2,1)}), bf16[16,48,128]{2,1,0:T(8,128)(2,1)S(1)}, u32[]{:S(2)}, u32[]{:S(2)}) async-start(bf16[16,48,128]{2,1,0:T(8,128)(2,1)} %shard_map.99), calls=%async_computation.5 | async-start | bytes 393216 | tf_op jit(solution)/shard_map/all_to_all | solution.py:275
  112.9 2.9 %shard_map.101 = (bf16[128,512]{1,0:T(8,128)(2,1)}, f32[128,512]{1,0:T(8,128)}, f32[128,512]{1,0:T(8,128)}) custom-call(s32[1]{0:T(128)} %bitcast.1.me, bf16[128,512]{1,0:T(8,128)(2,1)} %q.3, bf16[128,512]{1,0:T(8,128)(2,1)} %k.5, bf16[128,512]{1,0:T(8,128)(2,1)} %v.5, bf16[128,128]{1,0:T(8,128)(2,1)} %get-tuple-element.116.g0, ...), custom_call_target="tpu_custom_call" | custom-call | flops 100663296 | bytes 1409028 | tf_op jit(solution)/shard_map/pallas_call | solution.py:48
  115.9 0.0 copy-start.3
  116.0 4.8 %shard_map.100 = bf16[128,4096]{1,0:T(8,128)(2,1)} custom-call(bf16[128,128]{1,0:T(8,128)(2,1)} %get-tuple-element.92.a0, bf16[384,128]{1,0:T(8,128)(2,1)} %copy-done.16, bf16[384,128]{1,0:T(8,128)(2,1)} %copy-done.17, bf16[384,128]{1,0:T(8,128)(2,1)} %copy-done.18, bf16[8,256,128]{2,1,0:T(8,128)(2,1)} %get-tuple-element.128.refs_0_, ...), custom_call_target="tpu_custom_call" | custom-call | flops 536870912 | bytes 5570560 | tf_op jit(solution)/shard_map/pallas_call | solution.py:48
  120.8 2.5 %all-to-all-done.5.got = bf16[16,48,128]{2,1,0:T(8,128)(2,1)S(1)} async-done(((bf16[16,48,128]{2,1,0:T(8,128)(2,1)}), bf16[16,48,128]{2,1,0:T(8,128)(2,1)S(1)}, u32[]{:S(2)}, u32[]{:S(2)}) %all-to-all-start.5) | async-done | bytes 196640 | tf_op jit(solution)/shard_map/all_to_all | solution.py:275
  123.3 1.0 shard_map.102
  (49 shorter events, 0.1 us)
Async XLA Ops:
  0.6 24.1 %collective-permute-start = (bf16[128,4096]{1,0:T(8,128)(2,1)}, bf16[128,4096]{1,0:T(8,128)(2,1)S(1)}, u32[]{:S(2)}, u32[]{:S(2)}) collective-permute-start(bf16[128,4096]{1,0:T(8,128)(2,1)} %c0.3), channel_id=1, source_target_pairs={{0,1},{1,0},{2,3},{3,2},{4,5},{5,4},{6,7},{7,6},{8,9},{9,8},{10,11... | collective-permute-start | bytes 3145736 | tf_op jit(solution)/shard_map/ppermute | solution.py:290
  5.9 17.5 %all-to-all-start = ((bf16[16,48,128]{2,1,0:T(8,128)(2,1)}), bf16[16,48,128]{2,1,0:T(8,128)(2,1)S(1)}, u32[]{:S(2)}, u32[]{:S(2)}) async-start(bf16[16,48,128]{2,1,0:T(8,128)(2,1)} %get-tuple-element.72), calls=%async_computation | async-start | bytes 393216 | tf_op jit(solution)/shard_map/all_to_all | solution.py:275
  12.8 11.9 %collective-permute-start.1 = (bf16[384,128]{1,0:T(8,128)(2,1)}, bf16[384,128]{1,0:T(8,128)(2,1)S(1)}, u32[]{:S(2)}, u32[]{:S(2)}) collective-permute-start(bf16[384,128]{1,0:T(8,128)(2,1)} %get-tuple-element.74), channel_id=1, source_target_pairs={{0,1},{1,0},{2,3},{3,2},{4,5},{5,4},{6,7},{7,6},{8,9},{9,8},{10,11... | collective-permute-start | bytes 294920 | tf_op jit(solution)/shard_map/ppermute | solution.py:290
  12.9 11.7 %collective-permute-start.2 = (bf16[384,128]{1,0:T(8,128)(2,1)}, bf16[384,128]{1,0:T(8,128)(2,1)S(1)}, u32[]{:S(2)}, u32[]{:S(2)}) collective-permute-start(bf16[384,128]{1,0:T(8,128)(2,1)} %get-tuple-element.75), channel_id=1, source_target_pairs={{0,2},{2,0},{4,6},{6,4},{8,10},{10,8},{12,14},{14,12},{1,3},{3,1},... | collective-permute-start | bytes 294920 | tf_op jit(solution)/shard_map/ppermute | solution.py:293
  14.5 10.2 %collective-permute-start.3 = (bf16[384,128]{1,0:T(8,128)(2,1)}, bf16[384,128]{1,0:T(8,128)(2,1)S(1)}, u32[]{:S(2)}, u32[]{:S(2)}) collective-permute-start(bf16[384,128]{1,0:T(8,128)(2,1)} %get-tuple-element.76), channel_id=1, source_target_pairs={{0,3},{1,2},{2,1},{3,0},{4,7},{5,6},{6,5},{7,4},{8,11},{9,10},{10,... | collective-permute-start | bytes 294920 | tf_op jit(solution)/shard_map/ppermute | solution.py:296
  24.7 0.6 copy-start.13
  24.7 0.7 copy-start.14
  24.7 0.7 copy-start.15
  24.7 1.0 copy-start.6
  24.7 25.3 %collective-permute-start.4 = (bf16[128,4096]{1,0:T(8,128)(2,1)}, bf16[128,4096]{1,0:T(8,128)(2,1)S(1)}, u32[]{:S(2)}, u32[]{:S(2)}) collective-permute-start(bf16[128,4096]{1,0:T(8,128)(2,1)} %c0.3), channel_id=1, source_target_pairs={{0,2},{2,0},{4,6},{6,4},{8,10},{10,8},{12,14},{14,12},{1,3},{3,1},... | collective-permute-start | bytes 3145736 | tf_op jit(solution)/shard_map/ppermute | solution.py:293
  25.7 26.2 %all-to-all-start.1 = ((bf16[16,288,128]{2,1,0:T(8,128)(2,1)}), bf16[16,288,128]{2,1,0:T(8,128)(2,1)S(1)}, u32[]{:S(2)}, u32[]{:S(2)}) async-start(bf16[16,288,128]{2,1,0:T(8,128)(2,1)} %get-tuple-element.77), calls=%async_computation.1 | async-start | bytes 2359296 | tf_op jit(solution)/shard_map/all_to_all | solution.py:275
  50.0 8.6 %copy-start.7 = (bf16[128,4096]{1,0:T(8,128)(2,1)}, bf16[128,4096]{1,0:T(8,128)(2,1)S(1)}, u32[]{:S(2)}) copy-start(bf16[128,4096]{1,0:T(8,128)(2,1)S(1)} %collective-permute-done.4.c2) | copy-start | bytes 3145732
  50.0 8.6 %collective-permute-start.5 = (bf16[128,4096]{1,0:T(8,128)(2,1)S(1)}, bf16[128,4096]{1,0:T(8,128)(2,1)S(1)}, u32[]{:S(2)}, u32[]{:S(2)}) collective-permute-start(bf16[128,4096]{1,0:T(8,128)(2,1)S(1)} %collective-permute-done.4.c2), channel_id=1, source_target_pairs={{0,1},{1,0},{2,3},{3,2},{4,5},{5,4},{6,7},{7,6},{8,9},{9,8},{10,11... | collective-permute-start | bytes 3145736 | tf_op jit(solution)/shard_map/ppermute | solution.py:290
  51.9 6.7 %copy-start = (bf16[16,288,128]{2,1,0:T(8,128)(2,1)}, bf16[16,288,128]{2,1,0:T(8,128)(2,1)S(1)}, u32[]{:S(2)}) copy-start(bf16[16,288,128]{2,1,0:T(8,128)(2,1)S(1)} %all-to-all-done.1.second.w) | copy-start | bytes 3538948
  52.7 15.1 %all-to-all-start.2 = ((bf16[16,32,128]{2,1,0:T(8,128)(2,1)}), bf16[16,32,128]{2,1,0:T(8,128)(2,1)S(1)}, u32[]{:S(2)}, u32[]{:S(2)}) async-start(bf16[16,32,128]{2,1,0:T(8,128)(2,1)} %shard_map.94), calls=%async_computation.2 | async-start | bytes 262144 | tf_op jit(solution)/shard_map/all_to_all | solution.py:275
  58.6 1.0 copy-start.8
  67.8 4.6 %copy-start.10 = (bf16[16,32,128]{2,1,0:T(8,128)(2,1)}, bf16[16,32,128]{2,1,0:T(8,128)(2,1)S(1)}, u32[]{:S(2)}) copy-start(bf16[16,32,128]{2,1,0:T(8,128)(2,1)S(1)} %all-to-all-done.2.got) | copy-start | bytes 393220
  67.8 13.8 %all-to-all-start.3 = ((bf16[16,32,128]{2,1,0:T(8,128)(2,1)}), bf16[16,32,128]{2,1,0:T(8,128)(2,1)S(1)}, u32[]{:S(2)}, u32[]{:S(2)}) async-start(bf16[16,32,128]{2,1,0:T(8,128)(2,1)} %get-tuple-element.87), calls=%async_computation.3 | async-start | bytes 262144 | tf_op jit(solution)/shard_map/all_to_all | solution.py:275
  82.3 4.7 %copy-start.1 = (bf16[16,288,128]{2,1,0:T(8,128)(2,1)S(1)}, bf16[16,288,128]{2,1,0:T(8,128)(2,1)}, u32[]{:S(2)}) copy-start(bf16[16,288,128]{2,1,0:T(8,128)(2,1)} %copy-done) | copy-start | bytes 3538948
  82.3 24.5 %all-to-all-start.4 = ((bf16[16,288,128]{2,1,0:T(8,128)(2,1)}), bf16[16,288,128]{2,1,0:T(8,128)(2,1)S(1)}, u32[]{:S(2)}, u32[]{:S(2)}) async-start(bf16[16,288,128]{2,1,0:T(8,128)(2,1)} %broadcast_dynamic-update-slice_fusion), calls=%async_computation.4 | async-start | bytes 2359296 | tf_op jit(solution)/shard_map/all_to_all | solution.py:275
  86.9 3.6 %copy-start.20 = (bf16[384,128]{1,0:T(8,128)(2,1)S(1)}, bf16[384,128]{1,0:T(8,128)(2,1)}, u32[]{:S(2)}) copy-start(bf16[384,128]{1,0:T(8,128)(2,1)} %get-tuple-element.106) | copy-start | bytes 294916
  86.9 3.8 %copy-start.19 = (bf16[384,128]{1,0:T(8,128)(2,1)S(1)}, bf16[384,128]{1,0:T(8,128)(2,1)}, u32[]{:S(2)}) copy-start(bf16[384,128]{1,0:T(8,128)(2,1)} %get-tuple-element.107) | copy-start | bytes 294916
  87.9 28.0 %copy-start.9 = (bf16[8,256,128]{2,1,0:T(8,128)(2,1)}, bf16[8,256,128]{2,1,0:T(8,128)(2,1)S(1)}, u32[]{:S(2)}) copy-start(bf16[8,256,128]{2,1,0:T(8,128)(2,1)S(1)} %get-tuple-element.127.refs_1_) | copy-start | bytes 1572868
  87.9 2.6 %collective-permute-start.7 = (bf16[8,256,128]{2,1,0:T(8,128)(2,1)S(1)}, bf16[8,256,128]{2,1,0:T(8,128)(2,1)S(1)}, u32[]{:S(2)}, u32[]{:S(2)}) collective-permute-start(bf16[8,256,128]{2,1,0:T(8,128)(2,1)S(1)} %get-tuple-element.127.refs_1_), channel_id=1, source_target_pairs={{0,1},{1,0},{2,3},{3,2},{4,5},{5,4},{6,7},{7,6},{8,9},{9,8},{10,11... | collective-permute-start | bytes 1572872 | tf_op jit(solution)/shard_map/ppermute | solution.py:290
  87.9 2.9 %collective-permute-start.6 = (bf16[8,256,128]{2,1,0:T(8,128)(2,1)}, bf16[8,256,128]{2,1,0:T(8,128)(2,1)S(1)}, u32[]{:S(2)}, u32[]{:S(2)}) collective-permute-start(bf16[8,256,128]{2,1,0:T(8,128)(2,1)} %get-tuple-element.128.refs_0_), channel_id=1, source_target_pairs={{0,1},{1,0},{2,3},{3,2},{4,5},{5,4},{6,7},{7,6},{8,9},{9,8},{10,11... | collective-permute-start | bytes 1572872 | tf_op jit(solution)/shard_map/ppermute | solution.py:290
  88.4 19.3 %collective-permute-start.9 = (bf16[8,256,128]{2,1,0:T(8,128)(2,1)S(1)}, bf16[8,256,128]{2,1,0:T(8,128)(2,1)}, u32[]{:S(2)}, u32[]{:S(2)}) collective-permute-start(bf16[8,256,128]{2,1,0:T(8,128)(2,1)S(1)} %get-tuple-element.127.refs_1_), channel_id=1, source_target_pairs={{2,0},{4,2},{6,4},{8,6},{10,8},{12,10},{14,12},{0,14},{3,1},{5,3},... | collective-permute-start | bytes 1572872 | tf_op jit(solution)/shard_map/ppermute | solution.py:391
  88.4 19.3 %collective-permute-start.8 = (bf16[8,256,128]{2,1,0:T(8,128)(2,1)}, bf16[8,256,128]{2,1,0:T(8,128)(2,1)}, u32[]{:S(2)}, u32[]{:S(2)}) collective-permute-start(bf16[8,256,128]{2,1,0:T(8,128)(2,1)} %get-tuple-element.128.refs_0_), channel_id=1, source_target_pairs={{0,2},{2,4},{4,6},{6,8},{8,10},{10,12},{12,14},{14,0},{1,3},{3,5},... | collective-permute-start | bytes 1572872 | tf_op jit(solution)/shard_map/ppermute | solution.py:391
  89.9 17.8 %collective-permute-start.10 = (bf16[384,128]{1,0:T(8,128)(2,1)}, bf16[384,128]{1,0:T(8,128)(2,1)S(1)}, u32[]{:S(2)}, u32[]{:S(2)}) collective-permute-start(bf16[384,128]{1,0:T(8,128)(2,1)} %get-tuple-element.105), channel_id=1, source_target_pairs={{0,1},{1,0},{2,3},{3,2},{4,5},{5,4},{6,7},{7,6},{8,9},{9,8},{10,11... | collective-permute-start | bytes 294920 | tf_op jit(solution)/shard_map/ppermute | solution.py:290
  90.5 25.4 %copy-start.11 = (bf16[8,256,128]{2,1,0:T(8,128)(2,1)}, bf16[8,256,128]{2,1,0:T(8,128)(2,1)S(1)}, u32[]{:S(2)}) copy-start(bf16[8,256,128]{2,1,0:T(8,128)(2,1)S(1)} %collective-permute-done.7.refs_3_) | copy-start | bytes 1572868
  90.5 17.1 %collective-permute-start.11 = (bf16[384,128]{1,0:T(8,128)(2,1)S(1)}, bf16[384,128]{1,0:T(8,128)(2,1)S(1)}, u32[]{:S(2)}, u32[]{:S(2)}) collective-permute-start(bf16[384,128]{1,0:T(8,128)(2,1)S(1)} %copy-done.20), channel_id=1, source_target_pairs={{0,2},{2,0},{4,6},{6,4},{8,10},{10,8},{12,14},{14,12},{1,3},{3,1},... | collective-permute-start | bytes 294920 | tf_op jit(solution)/shard_map/ppermute | solution.py:293
  90.8 25.1 %copy-start.12 = (bf16[8,256,128]{2,1,0:T(8,128)(2,1)}, bf16[8,256,128]{2,1,0:T(8,128)(2,1)S(1)}, u32[]{:S(2)}) copy-start(bf16[8,256,128]{2,1,0:T(8,128)(2,1)S(1)} %collective-permute-done.6.refs_2_) | copy-start | bytes 1572868
  90.8 16.9 %collective-permute-start.12 = (bf16[384,128]{1,0:T(8,128)(2,1)S(1)}, bf16[384,128]{1,0:T(8,128)(2,1)S(1)}, u32[]{:S(2)}, u32[]{:S(2)}) collective-permute-start(bf16[384,128]{1,0:T(8,128)(2,1)S(1)} %copy-done.19), channel_id=1, source_target_pairs={{0,3},{1,2},{2,1},{3,0},{4,7},{5,6},{6,5},{7,4},{8,11},{9,10},{10,... | collective-permute-start | bytes 294920 | tf_op jit(solution)/shard_map/ppermute | solution.py:296
  107.6 5.3 %copy-start.16 = (bf16[384,128]{1,0:T(8,128)(2,1)}, bf16[384,128]{1,0:T(8,128)(2,1)S(1)}, u32[]{:S(2)}) copy-start(bf16[384,128]{1,0:T(8,128)(2,1)S(1)} %collective-permute-done.10.p1) | copy-start | bytes 294916
  107.6 5.3 %copy-start.17 = (bf16[384,128]{1,0:T(8,128)(2,1)}, bf16[384,128]{1,0:T(8,128)(2,1)S(1)}, u32[]{:S(2)}) copy-start(bf16[384,128]{1,0:T(8,128)(2,1)S(1)} %collective-permute-done.11.p2) | copy-start | bytes 294916
  107.7 5.3 %copy-start.18 = (bf16[384,128]{1,0:T(8,128)(2,1)}, bf16[384,128]{1,0:T(8,128)(2,1)S(1)}, u32[]{:S(2)}) copy-start(bf16[384,128]{1,0:T(8,128)(2,1)S(1)} %collective-permute-done.12.p3) | copy-start | bytes 294916
  107.7 8.2 %collective-permute-start.13 = (bf16[8,256,128]{2,1,0:T(8,128)(2,1)}, bf16[8,256,128]{2,1,0:T(8,128)(2,1)}, u32[]{:S(2)}, u32[]{:S(2)}) collective-permute-start(bf16[8,256,128]{2,1,0:T(8,128)(2,1)} %collective-permute-done.8.refs_4_), channel_id=1, source_target_pairs={{0,1},{1,0},{2,3},{3,2},{4,5},{5,4},{6,7},{7,6},{8,9},{9,8},{10,11... | collective-permute-start | bytes 1572872 | tf_op jit(solution)/shard_map/ppermute | solution.py:290
  108.9 7.1 %collective-permute-start.14 = (bf16[8,256,128]{2,1,0:T(8,128)(2,1)}, bf16[8,256,128]{2,1,0:T(8,128)(2,1)}, u32[]{:S(2)}, u32[]{:S(2)}) collective-permute-start(bf16[8,256,128]{2,1,0:T(8,128)(2,1)} %collective-permute-done.9.refs_5_), channel_id=1, source_target_pairs={{0,1},{1,0},{2,3},{3,2},{4,5},{5,4},{6,7},{7,6},{8,9},{9,8},{10,11... | collective-permute-start | bytes 1572872 | tf_op jit(solution)/shard_map/ppermute | solution.py:290
  109.0 14.3 %all-to-all-start.5 = ((bf16[16,48,128]{2,1,0:T(8,128)(2,1)}), bf16[16,48,128]{2,1,0:T(8,128)(2,1)S(1)}, u32[]{:S(2)}, u32[]{:S(2)}) async-start(bf16[16,48,128]{2,1,0:T(8,128)(2,1)} %shard_map.99), calls=%async_computation.5 | async-start | bytes 393216 | tf_op jit(solution)/shard_map/all_to_all | solution.py:275
  115.9 7.3 %copy-start.2 = (bf16[128,512]{1,0:T(8,128)(2,1)S(1)}, bf16[128,512]{1,0:T(8,128)(2,1)}, u32[]{:S(2)}) copy-start(bf16[128,512]{1,0:T(8,128)(2,1)} %k.5) | copy-start | bytes 393220
  115.9 7.3 %copy-start.3 = (bf16[128,512]{1,0:T(8,128)(2,1)S(1)}, bf16[128,512]{1,0:T(8,128)(2,1)}, u32[]{:S(2)}) copy-start(bf16[128,512]{1,0:T(8,128)(2,1)} %v.5) | copy-start | bytes 393220
  115.9 7.3 %copy-start.4 = (f32[128,512]{1,0:T(8,128)S(1)}, f32[128,512]{1,0:T(8,128)}, u32[]{:S(2)}) copy-start(f32[128,512]{1,0:T(8,128)} %get-tuple-element.122.kg_local) | copy-start | bytes 786436
  115.9 7.3 %copy-start.5 = (f32[128,512]{1,0:T(8,128)S(1)}, f32[128,512]{1,0:T(8,128)}, u32[]{:S(2)}) copy-start(f32[128,512]{1,0:T(8,128)} %get-tuple-element.123.vg_local) | copy-start | bytes 786436

commit v6 on v5

--- a/solution.py
+++ b/solution.py
@@ -16,6 +16,7 @@
 SHARE = MODEL // GROUPS
 STATE_ROWS = FEATURES // MEMBERS
 CHUNKS = 4
+PIECES = 2
 LIMIT = 63_000_000
 SOME = 60_000_000
 ROOM = 32_000_000
@@ -188,10 +189,10 @@
 
 
 def weight_kernel(c0, c1, c2, c3, a0, a1, a2, a3, out, cots, result, sems, out_sems):
-    width = MODEL // CHUNKS
-    part = GROUPS // CHUNKS
+    width = MODEL // PIECES
+    part = GROUPS // PIECES
     copies = []
-    for step in range(CHUNKS):
+    for step in range(PIECES):
         at = pl.ds(step * width, width)
         copies.append(
             [
@@ -204,7 +205,7 @@
             copy.start()
     turned = jnp.concatenate([a[...].T for a in (a0, a1, a2, a3)], axis=1)
     backs = []
-    for step in range(CHUNKS):
+    for step in range(PIECES):
         for copy in copies[step]:
             copy.wait()
         for j in range(step * part, (step + 1) * part):
@@ -365,8 +366,8 @@
         scratch_shapes=[
             pltpu.VMEM((4, TOKENS, MODEL), BF16),
             pltpu.VMEM((GROUPS, width, HEAD), BF16),
-            pltpu.SemaphoreType.DMA((CHUNKS, 4)),
-            pltpu.SemaphoreType.DMA((CHUNKS,)),
+            pltpu.SemaphoreType.DMA((PIECES, 4)),
+            pltpu.SemaphoreType.DMA((PIECES,)),
         ],
         compiler_params=pltpu.CompilerParams(vmem_limit_bytes=SOME),
         cost_estimate=pl.CostEstimate(flops=large, bytes_accessed=6 << 20, transcendentals=0),
@@ -386,6 +387,7 @@
     p1, p2, p3, weight, _ = lax.optimization_barrier((p1, p2, p3, second, total))
     w0 = [weight[: GROUPS // 2, STATE_ROWS:], weight[GROUPS // 2 :, STATE_ROWS:]]
     p1, p2, p3 = to_core(p1), to_odd(p2), to_both(p3)
+    w0, p1 = lax.optimization_barrier((w0, p1))
     w1 = [to_core(w) for w in w0]
     ring = [(i, (i + 1) % 8) for i in range(8)]
     w2 = [lax.ppermute(w0[0], "z", ring), lax.ppermute(w0[1], "z", [(j, i) for i, j in ring])]

time: 125 us -> 125 us (level)
  waiting for transfers between devices: 49.9 us -> 48.3 us
  starting transfers between devices: 44.3 us -> 45.8 us
    ppermute x1, starting transfers between devices: 0.02 us -> 2.6 us  [body(): lax.ppermute(w0[1], 'z', [(j, i) for i, j in ring])]
    all_to_all x6, waiting for transfers between devices: 32.2 us -> 30.4 us  [exchange(): return lax.all_to_all(value, axes, 0, 0, tiled=True)]
    ppermute x1, starting transfers between devices: 1.45 us -> 0.08 us  [body(): lax.ppermute(w0[0], 'z', ring)]
where the time goes in v6:
time: 125 us; the launch traced here: 124 us
  waiting for transfers between devices  48.3 us (39%)
  starting transfers between devices  45.8 us (37%)
  Pallas kernels  25.7 us (21%)
  local copies, waits for them, and re-layouts  3.52 us (3%)
    all_to_all x6, starting transfers between devices, exchange(): return lax.all_to_all(value, axes, 0, 0, tiled=True)  32.9 us
    all_to_all x6, waiting for transfers between devices, exchange(): return lax.all_to_all(value, axes, 0, 0, tiled=True)  30.4 us
    pallas_call x10, Pallas kernels, call(): pl.pallas_call(kernel, in_specs=ins, out_specs=VMEM if one else [VMEM] *...  21.4 us
    ppermute x3, waiting for transfers between devices, to_odd(): return lax.ppermute(x, 'z', [(i, i ^ 1) for i in range(8)])  17.5 us
    ppermute x8, starting transfers between devices, to_core(): return lax.ppermute(x, 'c', [(0, 1), (1, 0)])  5.59 us
    pallas_call x1, Pallas kernels, body(): pl.pallas_call(weight_kernel, in_specs=[HBM] * 4 + [VMEM] * 4, out_specs=...  4.31 us
    ppermute x2, starting transfers between devices, to_both(): return lax.ppermute(x, ZC, [(i, i ^ 3) for i in range(MEMBERS)])  3 us
    ppermute x1, starting transfers between devices, body(): lax.ppermute(w0[1], 'z', [(j, i) for i, j in ring])  2.6 us
  transfers between devices with their start and end apart: 21, of which 8 were waited for; matrix products, arithmetic and copies ran while one was open for 1% of the time, Pallas kernels for 20%

profile of v6, /device:TPU:1, one launch (start us, length us, event | category | flops | bytes accessed | tf_op | source)
XLA Modules:
  0.0 124.3 jit_solution(718613994636655775)
XLA Ops:
  0.6 3.3 %collective-permute-start = (bf16[128,4096]{1,0:T(8,128)(2,1)}, bf16[128,4096]{1,0:T(8,128)(2,1)S(1)}, u32[]{:S(2)}, u32[]{:S(2)}) collective-permute-start(bf16[128,4096]{1,0:T(8,128)(2,1)} %c0.3), channel_id=1, source_target_pairs={{0,1},{1,0},{2,3},{3,2},{4,5},{5,4},{6,7},{7,6},{8,9},{9,8},{10,11... | collective-permute-start | bytes 3145736 | tf_op jit(solution)/shard_map/ppermute | solution.py:291
  4.0 1.9 %shard_map.92 = (bf16[16,48,128]{2,1,0:T(8,128)(2,1)}, bf16[384,128]{1,0:T(8,128)(2,1)}, bf16[384,128]{1,0:T(8,128)(2,1)}, bf16[384,128]{1,0:T(8,128)(2,1)}, bf16[384,128]{1,0:T(8,128)(2,1)}) custom-call(s32[1]{0:T(128)} %bitcast.1.me, bf16[128,512]{1,0:T(8,128)(2,1)} %k.5, bf16[128,512]{1,0:T(8,128)(2,1)} %v.5, bf16[16,512]{1,0:T(8,128)(2,1)} %w.1, ...), custom_call_target="tpu_custom_call" | custom-call | flops 16777216 | bytes 999428 | tf_op jit(solution)/shard_map/pallas_call | solution.py:49
  5.9 6.9 %all-to-all-start = ((bf16[16,48,128]{2,1,0:T(8,128)(2,1)}), bf16[16,48,128]{2,1,0:T(8,128)(2,1)S(1)}, u32[]{:S(2)}, u32[]{:S(2)}) async-start(bf16[16,48,128]{2,1,0:T(8,128)(2,1)} %get-tuple-element.75), calls=%async_computation | async-start | bytes 393216 | tf_op jit(solution)/shard_map/all_to_all | solution.py:276
  12.8 0.2 collective-permute-start.1
  12.9 1.6 %collective-permute-start.2 = (bf16[384,128]{1,0:T(8,128)(2,1)}, bf16[384,128]{1,0:T(8,128)(2,1)S(1)}, u32[]{:S(2)}, u32[]{:S(2)}) collective-permute-start(bf16[384,128]{1,0:T(8,128)(2,1)} %get-tuple-element.78), channel_id=1, source_target_pairs={{0,2},{2,0},{4,6},{6,4},{8,10},{10,8},{12,14},{14,12},{1,3},{3,1},... | collective-permute-start | bytes 294920 | tf_op jit(solution)/shard_map/ppermute | solution.py:294
  14.5 0.4 collective-permute-start.3
  14.9 8.5 %all-to-all-done.first = bf16[16,48,128]{2,1,0:T(8,128)(2,1)S(1)} async-done(((bf16[16,48,128]{2,1,0:T(8,128)(2,1)}), bf16[16,48,128]{2,1,0:T(8,128)(2,1)S(1)}, u32[]{:S(2)}, u32[]{:S(2)}) %all-to-all-start) | async-done | bytes 196640 | tf_op jit(solution)/shard_map/all_to_all | solution.py:276
  23.4 1.2 shard_map.93
  24.7 0.0 copy-start.6
  24.7 0.1 collective-permute-start.4
  24.8 0.5 copy-done.13
  25.3 0.1 copy-done.14
  25.4 0.0 copy-done.15
  25.4 0.3 copy-done.6
  25.7 6.8 %all-to-all-start.1 = ((bf16[16,288,128]{2,1,0:T(8,128)(2,1)}), bf16[16,288,128]{2,1,0:T(8,128)(2,1)S(1)}, u32[]{:S(2)}, u32[]{:S(2)}) async-start(bf16[16,288,128]{2,1,0:T(8,128)(2,1)} %get-tuple-element.80), calls=%async_computation.1 | async-start | bytes 2359296 | tf_op jit(solution)/shard_map/all_to_all | solution.py:276
  32.5 17.5 %collective-permute-done.4.c2 = bf16[128,4096]{1,0:T(8,128)(2,1)S(1)} collective-permute-done((bf16[128,4096]{1,0:T(8,128)(2,1)}, bf16[128,4096]{1,0:T(8,128)(2,1)S(1)}, u32[]{:S(2)}, u32[]{:S(2)}) %collective-permute-start.4) | collective-permute-done | bytes 1048608 | tf_op jit(solution)/shard_map/ppermute | solution.py:294
  50.0 0.2 collective-permute-start.5
  50.2 1.7 %all-to-all-done.1.second.w = bf16[16,288,128]{2,1,0:T(8,128)(2,1)S(1)} async-done(((bf16[16,288,128]{2,1,0:T(8,128)(2,1)}), bf16[16,288,128]{2,1,0:T(8,128)(2,1)S(1)}, u32[]{:S(2)}, u32[]{:S(2)}) %all-to-all-start.1) | async-done | bytes 1179680 | tf_op jit(solution)/shard_map/all_to_all | solution.py:276
  51.9 0.8 shard_map.94
  52.7 5.9 %all-to-all-start.2 = ((bf16[16,32,128]{2,1,0:T(8,128)(2,1)}), bf16[16,32,128]{2,1,0:T(8,128)(2,1)S(1)}, u32[]{:S(2)}, u32[]{:S(2)}) async-start(bf16[16,32,128]{2,1,0:T(8,128)(2,1)} %shard_map.94), calls=%async_computation.2 | async-start | bytes 262144 | tf_op jit(solution)/shard_map/all_to_all | solution.py:276
  58.6 0.9 copy-done.8
  59.6 5.5 %shard_map.95 = (bf16[128,128]{1,0:T(8,128)(2,1)}, bf16[128,128]{1,0:T(8,128)(2,1)}, bf16[128,128]{1,0:T(8,128)(2,1)}, bf16[128,128]{1,0:T(8,128)(2,1)}, bf16[16,32,128]{2,1,0:T(8,128)(2,1)}) custom-call(s32[1]{0:T(128)} %bitcast.2.base, s32[1]{0:T(128)} %bitcast.3.place, bf16[128,4096]{1,0:T(8,128)(2,1)} %c0.3, bf16[128,4096]{1,0:T(8,128)(2,1)} %copy-done.6, ...), custom_call_target="tpu_custom_call" | custom-call | flops 536870912 | bytes 6029320 | tf_op jit(solution)/shard_map/pallas_call | solution.py:49
  65.1 2.7 %all-to-all-done.2.got = bf16[16,32,128]{2,1,0:T(8,128)(2,1)S(1)} async-done(((bf16[16,32,128]{2,1,0:T(8,128)(2,1)}), bf16[16,32,128]{2,1,0:T(8,128)(2,1)S(1)}, u32[]{:S(2)}, u32[]{:S(2)}) %all-to-all-start.2) | async-done | bytes 131104 | tf_op jit(solution)/shard_map/all_to_all | solution.py:276
  67.8 4.6 %all-to-all-start.3 = ((bf16[16,32,128]{2,1,0:T(8,128)(2,1)}), bf16[16,32,128]{2,1,0:T(8,128)(2,1)S(1)}, u32[]{:S(2)}, u32[]{:S(2)}) async-start(bf16[16,32,128]{2,1,0:T(8,128)(2,1)} %get-tuple-element.90), calls=%async_computation.3 | async-start | bytes 262144 | tf_op jit(solution)/shard_map/all_to_all | solution.py:276
  72.4 2.3 %shard_map.96 = (bf16[128,128]{1,0:T(8,128)(2,1)}, bf16[128,128]{1,0:T(8,128)(2,1)}, bf16[128,128]{1,0:T(8,128)(2,1)}, bf16[128,128]{1,0:T(8,128)(2,1)}, bf16[12...) custom-call(s32[1]{0:T(128)} %bitcast.2.base, ...), custom_call_target="tpu_custom_call" | custom-call | flops 50331648 | bytes 1081352 | tf_op jit(solution)/shard_map/pallas_call | solution.py:49
  74.6 4.3 %shard_map.97 = bf16[16,288,128]{2,1,0:T(8,128)(2,1)} custom-call(bf16[128,4096]{1,0:T(8,128)(2,1)} %c0.3, bf16[128,4096]{1,0:T(8,128)(2,1)} %copy-done.6, bf16[128,4096]{1,0:T(8,128)(2,1)} %copy-done.7, bf16[128,4096]{1,0:T(8,128)(2,1)} %copy-done.8, bf16[128,128]{1,0:T(8,128)(2,1)} %get-tuple-element.95.a0, bf16[128,128]{1,0:T(8,128)(2,1)} %get-tuple-element.96.a1, ...), custom_call_target="tpu_custom_call" | custom-call | flops 536870912 | bytes 6291456 | tf_op jit(solution)/shard_map/pallas_call | solution.py:361
  79.0 2.6 %all-to-all-done.3.first = bf16[16,32,128]{2,1,0:T(8,128)(2,1)S(1)} async-done(((bf16[16,32,128]{2,1,0:T(8,128)(2,1)}), bf16[16,32,128]{2,1,0:T(8,128)(2,1)S(1)}, u32[]{:S(2)}, u32[]{:S(2)}) %all-to-all-start.3) | async-done | bytes 131104 | tf_op jit(solution)/shard_map/all_to_all | solution.py:276
  81.6 0.7 broadcast_dynamic-update-slice_fusion
  82.3 4.7 %all-to-all-start.4 = ((bf16[16,288,128]{2,1,0:T(8,128)(2,1)}), bf16[16,288,128]{2,1,0:T(8,128)(2,1)S(1)}, u32[]{:S(2)}, u32[]{:S(2)}) async-start(bf16[16,288,128]{2,1,0:T(8,128)(2,1)} %broadcast_dynamic-update-slice_fusion), calls=%async_computation.4 | async-start | bytes 2359296 | tf_op jit(solution)/shard_map/all_to_all | solution.py:276
  86.9 0.1 collective-permute-start.6
  87.1 0.9 fusion
  88.0 0.3 collective-permute-done.6.p1
  88.3 0.2 collective-permute-start.7
  88.5 0.4 collective-permute-start.8
  88.8 0.1 collective-permute-start.9
  88.9 2.6 %collective-permute-start.10 = (bf16[8,256,128]{2,1,0:T(8,128)(2,1)S(1)}, bf16[8,256,128]{2,1,0:T(8,128)(2,1)}, u32[]{:S(2)}, u32[]{:S(2)}) collective-permute-start(bf16[8,256,128]{2,1,0:T(8,128)(2,1)S(1)} %get-tuple-element.108.refs_1_), channel_id=1, source_target_pairs={{2,0},{4,2},{6,4},{8,6},{10,8},{12,10},{14,12},{0,14},{3,1},{5,3},... | collective-permute-start | bytes 1572872 | tf_op jit(solution)/shard_map/ppermute | solution.py:393
  91.6 2.6 %collective-permute-start.12 = (bf16[384,128]{1,0:T(8,128)(2,1)S(1)}, bf16[384,128]{1,0:T(8,128)(2,1)S(1)}, u32[]{:S(2)}, u32[]{:S(2)}) collective-permute-start(bf16[384,128]{1,0:T(8,128)(2,1)S(1)} %copy-done.19), channel_id=1, source_target_pairs={{0,3},{1,2},{2,1},{3,0},{4,7},{5,6},{6,5},{7,4},{8,11},{9,10},{10,... | collective-permute-start | bytes 294920 | tf_op jit(solution)/shard_map/ppermute | solution.py:297
  94.2 12.5 %all-to-all-done.4.got = bf16[16,288,128]{2,1,0:T(8,128)(2,1)S(1)} async-done(((bf16[16,288,128]{2,1,0:T(8,128)(2,1)}), bf16[16,288,128]{2,1,0:T(8,128)(2,1)S(1)}, u32[]{:S(2)}, u32[]{:S(2)}) %all-to-all-start.4) | async-done | bytes 1179680 | tf_op jit(solution)/shard_map/all_to_all | solution.py:276
  106.7 0.9 shard_map.99
  107.6 1.2 collective-permute-start.13
  108.8 0.1 collective-permute-start.14
  108.9 4.1 %all-to-all-start.5 = ((bf16[16,48,128]{2,1,0:T(8,128)(2,1)}), bf16[16,48,128]{2,1,0:T(8,128)(2,1)S(1)}, u32[]{:S(2)}, u32[]{:S(2)}) async-start(bf16[16,48,128]{2,1,0:T(8,128)(2,1)} %shard_map.99), calls=%async_computation.5 | async-start | bytes 393216 | tf_op jit(solution)/shard_map/all_to_all | solution.py:276
  113.0 3.0 %shard_map.101 = (bf16[128,512]{1,0:T(8,128)(2,1)}, f32[128,512]{1,0:T(8,128)}, f32[128,512]{1,0:T(8,128)}) custom-call(s32[1]{0:T(128)} %bitcast.1.me, bf16[128,512]{1,0:T(8,128)(2,1)} %q.3, bf16[128,512]{1,0:T(8,128)(2,1)} %k.5, bf16[128,512]{1,0:T(8,128)(2,1)} %v.5, bf16[128,128]{1,0:T(8,128)(2,1)} %get-tuple-element.122.g0, ...), custom_call_target="tpu_custom_call" | custom-call | flops 100663296 | bytes 1409028 | tf_op jit(solution)/shard_map/pallas_call | solution.py:49
  116.0 0.0 copy-start.2
  116.0 0.0 copy-start.3
  116.1 4.8 %shard_map.100 = bf16[128,4096]{1,0:T(8,128)(2,1)} custom-call(bf16[128,128]{1,0:T(8,128)(2,1)} %get-tuple-element.95.a0, bf16[384,128]{1,0:T(8,128)(2,1)} %copy-done.16, bf16[384,128]{1,0:T(8,128)(2,1)} %copy-done.17, bf16[384,128]{1,0:T(8,128)(2,1)} %copy-done.18, bf16[8,256,128]{2,1,0:T(8,128)(2,1)} %get-tuple-element.107.refs_0_, ...), custom_call_target="tpu_custom_call" | custom-call | flops 536870912 | bytes 5570560 | tf_op jit(solution)/shard_map/pallas_call | solution.py:49
  120.9 2.4 %all-to-all-done.5.got = bf16[16,48,128]{2,1,0:T(8,128)(2,1)S(1)} async-done(((bf16[16,48,128]{2,1,0:T(8,128)(2,1)}), bf16[16,48,128]{2,1,0:T(8,128)(2,1)S(1)}, u32[]{:S(2)}, u32[]{:S(2)}) %all-to-all-start.5) | async-done | bytes 196640 | tf_op jit(solution)/shard_map/all_to_all | solution.py:276
  123.4 1.0 shard_map.102
  (51 shorter events, 0.1 us)
Async XLA Ops:
  0.6 24.1 %collective-permute-start = (bf16[128,4096]{1,0:T(8,128)(2,1)}, bf16[128,4096]{1,0:T(8,128)(2,1)S(1)}, u32[]{:S(2)}, u32[]{:S(2)}) collective-permute-start(bf16[128,4096]{1,0:T(8,128)(2,1)} %c0.3), channel_id=1, source_target_pairs={{0,1},{1,0},{2,3},{3,2},{4,5},{5,4},{6,7},{7,6},{8,9},{9,8},{10,11... | collective-permute-start | bytes 3145736 | tf_op jit(solution)/shard_map/ppermute | solution.py:291
  5.9 17.5 %all-to-all-start = ((bf16[16,48,128]{2,1,0:T(8,128)(2,1)}), bf16[16,48,128]{2,1,0:T(8,128)(2,1)S(1)}, u32[]{:S(2)}, u32[]{:S(2)}) async-start(bf16[16,48,128]{2,1,0:T(8,128)(2,1)} %get-tuple-element.75), calls=%async_computation | async-start | bytes 393216 | tf_op jit(solution)/shard_map/all_to_all | solution.py:276
  12.8 11.9 %collective-permute-start.1 = (bf16[384,128]{1,0:T(8,128)(2,1)}, bf16[384,128]{1,0:T(8,128)(2,1)S(1)}, u32[]{:S(2)}, u32[]{:S(2)}) collective-permute-start(bf16[384,128]{1,0:T(8,128)(2,1)} %get-tuple-element.77), channel_id=1, source_target_pairs={{0,1},{1,0},{2,3},{3,2},{4,5},{5,4},{6,7},{7,6},{8,9},{9,8},{10,11... | collective-permute-start | bytes 294920 | tf_op jit(solution)/shard_map/ppermute | solution.py:291
  12.9 11.7 %collective-permute-start.2 = (bf16[384,128]{1,0:T(8,128)(2,1)}, bf16[384,128]{1,0:T(8,128)(2,1)S(1)}, u32[]{:S(2)}, u32[]{:S(2)}) collective-permute-start(bf16[384,128]{1,0:T(8,128)(2,1)} %get-tuple-element.78), channel_id=1, source_target_pairs={{0,2},{2,0},{4,6},{6,4},{8,10},{10,8},{12,14},{14,12},{1,3},{3,1},... | collective-permute-start | bytes 294920 | tf_op jit(solution)/shard_map/ppermute | solution.py:294
  14.5 10.2 %collective-permute-start.3 = (bf16[384,128]{1,0:T(8,128)(2,1)}, bf16[384,128]{1,0:T(8,128)(2,1)S(1)}, u32[]{:S(2)}, u32[]{:S(2)}) collective-permute-start(bf16[384,128]{1,0:T(8,128)(2,1)} %get-tuple-element.79), channel_id=1, source_target_pairs={{0,3},{1,2},{2,1},{3,0},{4,7},{5,6},{6,5},{7,4},{8,11},{9,10},{10,... | collective-permute-start | bytes 294920 | tf_op jit(solution)/shard_map/ppermute | solution.py:297
  24.7 0.6 copy-start.13
  24.7 0.7 copy-start.14
  24.7 0.7 copy-start.15
  24.7 1.0 copy-start.6
  24.7 25.3 %collective-permute-start.4 = (bf16[128,4096]{1,0:T(8,128)(2,1)}, bf16[128,4096]{1,0:T(8,128)(2,1)S(1)}, u32[]{:S(2)}, u32[]{:S(2)}) collective-permute-start(bf16[128,4096]{1,0:T(8,128)(2,1)} %c0.3), channel_id=1, source_target_pairs={{0,2},{2,0},{4,6},{6,4},{8,10},{10,8},{12,14},{14,12},{1,3},{3,1},... | collective-permute-start | bytes 3145736 | tf_op jit(solution)/shard_map/ppermute | solution.py:294
  25.7 26.2 %all-to-all-start.1 = ((bf16[16,288,128]{2,1,0:T(8,128)(2,1)}), bf16[16,288,128]{2,1,0:T(8,128)(2,1)S(1)}, u32[]{:S(2)}, u32[]{:S(2)}) async-start(bf16[16,288,128]{2,1,0:T(8,128)(2,1)} %get-tuple-element.80), calls=%async_computation.1 | async-start | bytes 2359296 | tf_op jit(solution)/shard_map/all_to_all | solution.py:276
  50.0 8.6 %copy-start.7 = (bf16[128,4096]{1,0:T(8,128)(2,1)}, bf16[128,4096]{1,0:T(8,128)(2,1)S(1)}, u32[]{:S(2)}) copy-start(bf16[128,4096]{1,0:T(8,128)(2,1)S(1)} %collective-permute-done.4.c2) | copy-start | bytes 3145732
  50.0 8.6 %collective-permute-start.5 = (bf16[128,4096]{1,0:T(8,128)(2,1)S(1)}, bf16[128,4096]{1,0:T(8,128)(2,1)S(1)}, u32[]{:S(2)}, u32[]{:S(2)}) collective-permute-start(bf16[128,4096]{1,0:T(8,128)(2,1)S(1)} %collective-permute-done.4.c2), channel_id=1, source_target_pairs={{0,1},{1,0},{2,3},{3,2},{4,5},{5,4},{6,7},{7,6},{8,9},{9,8},{10,11... | collective-permute-start | bytes 3145736 | tf_op jit(solution)/shard_map/ppermute | solution.py:291
  51.9 6.7 %copy-start = (bf16[16,288,128]{2,1,0:T(8,128)(2,1)}, bf16[16,288,128]{2,1,0:T(8,128)(2,1)S(1)}, u32[]{:S(2)}) copy-start(bf16[16,288,128]{2,1,0:T(8,128)(2,1)S(1)} %all-to-all-done.1.second.w) | copy-start | bytes 3538948
  52.7 15.1 %all-to-all-start.2 = ((bf16[16,32,128]{2,1,0:T(8,128)(2,1)}), bf16[16,32,128]{2,1,0:T(8,128)(2,1)S(1)}, u32[]{:S(2)}, u32[]{:S(2)}) async-start(bf16[16,32,128]{2,1,0:T(8,128)(2,1)} %shard_map.94), calls=%async_computation.2 | async-start | bytes 262144 | tf_op jit(solution)/shard_map/all_to_all | solution.py:276
  58.6 1.0 copy-start.8
  67.8 4.6 %copy-start.10 = (bf16[16,32,128]{2,1,0:T(8,128)(2,1)}, bf16[16,32,128]{2,1,0:T(8,128)(2,1)S(1)}, u32[]{:S(2)}) copy-start(bf16[16,32,128]{2,1,0:T(8,128)(2,1)S(1)} %all-to-all-done.2.got) | copy-start | bytes 393220
  67.8 13.8 %all-to-all-start.3 = ((bf16[16,32,128]{2,1,0:T(8,128)(2,1)}), bf16[16,32,128]{2,1,0:T(8,128)(2,1)S(1)}, u32[]{:S(2)}, u32[]{:S(2)}) async-start(bf16[16,32,128]{2,1,0:T(8,128)(2,1)} %get-tuple-element.90), calls=%async_computation.3 | async-start | bytes 262144 | tf_op jit(solution)/shard_map/all_to_all | solution.py:276
  82.2 4.7 %copy-start.21 = (bf16[384,128]{1,0:T(8,128)(2,1)S(1)}, bf16[384,128]{1,0:T(8,128)(2,1)}, u32[]{:S(2)}) copy-start(bf16[384,128]{1,0:T(8,128)(2,1)} %get-tuple-element.106) | copy-start | bytes 294916
  82.2 4.8 %copy-start.1 = (bf16[16,288,128]{2,1,0:T(8,128)(2,1)S(1)}, bf16[16,288,128]{2,1,0:T(8,128)(2,1)}, u32[]{:S(2)}) copy-start(bf16[16,288,128]{2,1,0:T(8,128)(2,1)} %copy-done) | copy-start | bytes 3538948
  82.3 24.5 %all-to-all-start.4 = ((bf16[16,288,128]{2,1,0:T(8,128)(2,1)}), bf16[16,288,128]{2,1,0:T(8,128)(2,1)S(1)}, u32[]{:S(2)}, u32[]{:S(2)}) async-start(bf16[16,288,128]{2,1,0:T(8,128)(2,1)} %broadcast_dynamic-update-slice_fusion), calls=%async_computation.4 | async-start | bytes 2359296 | tf_op jit(solution)/shard_map/all_to_all | solution.py:276
  86.9 4.6 %copy-start.20 = (bf16[384,128]{1,0:T(8,128)(2,1)S(1)}, bf16[384,128]{1,0:T(8,128)(2,1)}, u32[]{:S(2)}) copy-start(bf16[384,128]{1,0:T(8,128)(2,1)} %get-tuple-element.112) | copy-start | bytes 294916
  86.9 4.6 %copy-start.19 = (bf16[384,128]{1,0:T(8,128)(2,1)S(1)}, bf16[384,128]{1,0:T(8,128)(2,1)}, u32[]{:S(2)}) copy-start(bf16[384,128]{1,0:T(8,128)(2,1)} %get-tuple-element.113) | copy-start | bytes 294916
  86.9 1.4 %collective-permute-start.6 = (bf16[384,128]{1,0:T(8,128)(2,1)S(1)}, bf16[384,128]{1,0:T(8,128)(2,1)S(1)}, u32[]{:S(2)}, u32[]{:S(2)}) collective-permute-start(bf16[384,128]{1,0:T(8,128)(2,1)S(1)} %copy-done.21), channel_id=1, source_target_pairs={{0,1},{1,0},{2,3},{3,2},{4,5},{5,4},{6,7},{7,6},{8,9},{9,8},{10,11... | collective-permute-start | bytes 294920 | tf_op jit(solution)/shard_map/ppermute | solution.py:291
  88.0 28.0 %copy-start.9 = (bf16[8,256,128]{2,1,0:T(8,128)(2,1)}, bf16[8,256,128]{2,1,0:T(8,128)(2,1)S(1)}, u32[]{:S(2)}) copy-start(bf16[8,256,128]{2,1,0:T(8,128)(2,1)S(1)} %get-tuple-element.108.refs_1_) | copy-start | bytes 1572868
  88.3 24.7 %copy-start.16 = (bf16[384,128]{1,0:T(8,128)(2,1)}, bf16[384,128]{1,0:T(8,128)(2,1)S(1)}, u32[]{:S(2)}) copy-start(bf16[384,128]{1,0:T(8,128)(2,1)S(1)} %collective-permute-done.6.p1) | copy-start | bytes 294916
  88.3 3.2 %collective-permute-start.7 = (bf16[8,256,128]{2,1,0:T(8,128)(2,1)}, bf16[8,256,128]{2,1,0:T(8,128)(2,1)S(1)}, u32[]{:S(2)}, u32[]{:S(2)}) collective-permute-start(bf16[8,256,128]{2,1,0:T(8,128)(2,1)} %get-tuple-element.107.refs_0_), channel_id=1, source_target_pairs={{0,1},{1,0},{2,3},{3,2},{4,5},{5,4},{6,7},{7,6},{8,9},{9,8},{10,11... | collective-permute-start | bytes 1572872 | tf_op jit(solution)/shard_map/ppermute | solution.py:291
  88.5 5.7 %collective-permute-start.8 = (bf16[8,256,128]{2,1,0:T(8,128)(2,1)S(1)}, bf16[8,256,128]{2,1,0:T(8,128)(2,1)S(1)}, u32[]{:S(2)}, u32[]{:S(2)}) collective-permute-start(bf16[8,256,128]{2,1,0:T(8,128)(2,1)S(1)} %get-tuple-element.108.refs_1_), channel_id=1, source_target_pairs={{0,1},{1,0},{2,3},{3,2},{4,5},{5,4},{6,7},{7,6},{8,9},{9,8},{10,11... | collective-permute-start | bytes 1572872 | tf_op jit(solution)/shard_map/ppermute | solution.py:291
  88.8 18.8 %collective-permute-start.9 = (bf16[8,256,128]{2,1,0:T(8,128)(2,1)}, bf16[8,256,128]{2,1,0:T(8,128)(2,1)}, u32[]{:S(2)}, u32[]{:S(2)}) collective-permute-start(bf16[8,256,128]{2,1,0:T(8,128)(2,1)} %get-tuple-element.107.refs_0_), channel_id=1, source_target_pairs={{0,2},{2,4},{4,6},{6,8},{8,10},{10,12},{12,14},{14,0},{1,3},{3,5},... | collective-permute-start | bytes 1572872 | tf_op jit(solution)/shard_map/ppermute | solution.py:393
  88.9 18.7 %collective-permute-start.10 = (bf16[8,256,128]{2,1,0:T(8,128)(2,1)S(1)}, bf16[8,256,128]{2,1,0:T(8,128)(2,1)}, u32[]{:S(2)}, u32[]{:S(2)}) collective-permute-start(bf16[8,256,128]{2,1,0:T(8,128)(2,1)S(1)} %get-tuple-element.108.refs_1_), channel_id=1, source_target_pairs={{2,0},{4,2},{6,4},{8,6},{10,8},{12,10},{14,12},{0,14},{3,1},{5,3},... | collective-permute-start | bytes 1572872 | tf_op jit(solution)/shard_map/ppermute | solution.py:393
  91.5 16.1 %collective-permute-start.11 = (bf16[384,128]{1,0:T(8,128)(2,1)S(1)}, bf16[384,128]{1,0:T(8,128)(2,1)S(1)}, u32[]{:S(2)}, u32[]{:S(2)}) collective-permute-start(bf16[384,128]{1,0:T(8,128)(2,1)S(1)} %copy-done.20), channel_id=1, source_target_pairs={{0,2},{2,0},{4,6},{6,4},{8,10},{10,8},{12,14},{14,12},{1,3},{3,1},... | collective-permute-start | bytes 294920 | tf_op jit(solution)/shard_map/ppermute | solution.py:294
  91.5 24.5 %copy-start.11 = (bf16[8,256,128]{2,1,0:T(8,128)(2,1)}, bf16[8,256,128]{2,1,0:T(8,128)(2,1)S(1)}, u32[]{:S(2)}) copy-start(bf16[8,256,128]{2,1,0:T(8,128)(2,1)S(1)} %collective-permute-done.7.refs_2_) | copy-start | bytes 1572868
  91.6 16.1 %collective-permute-start.12 = (bf16[384,128]{1,0:T(8,128)(2,1)S(1)}, bf16[384,128]{1,0:T(8,128)(2,1)S(1)}, u32[]{:S(2)}, u32[]{:S(2)}) collective-permute-start(bf16[384,128]{1,0:T(8,128)(2,1)S(1)} %copy-done.19), channel_id=1, source_target_pairs={{0,3},{1,2},{2,1},{3,0},{4,7},{5,6},{6,5},{7,4},{8,11},{9,10},{10,... | collective-permute-start | bytes 294920 | tf_op jit(solution)/shard_map/ppermute | solution.py:297
  94.2 21.8 %copy-start.12 = (bf16[8,256,128]{2,1,0:T(8,128)(2,1)}, bf16[8,256,128]{2,1,0:T(8,128)(2,1)S(1)}, u32[]{:S(2)}) copy-start(bf16[8,256,128]{2,1,0:T(8,128)(2,1)S(1)} %collective-permute-done.8.refs_3_) | copy-start | bytes 1572868
  107.6 5.4 %copy-start.17 = (bf16[384,128]{1,0:T(8,128)(2,1)}, bf16[384,128]{1,0:T(8,128)(2,1)S(1)}, u32[]{:S(2)}) copy-start(bf16[384,128]{1,0:T(8,128)(2,1)S(1)} %collective-permute-done.11.p2) | copy-start | bytes 294916
  107.6 5.4 %copy-start.18 = (bf16[384,128]{1,0:T(8,128)(2,1)}, bf16[384,128]{1,0:T(8,128)(2,1)S(1)}, u32[]{:S(2)}) copy-start(bf16[384,128]{1,0:T(8,128)(2,1)S(1)} %collective-permute-done.12.p3) | copy-start | bytes 294916
  107.6 8.4 %collective-permute-start.13 = (bf16[8,256,128]{2,1,0:T(8,128)(2,1)}, bf16[8,256,128]{2,1,0:T(8,128)(2,1)}, u32[]{:S(2)}, u32[]{:S(2)}) collective-permute-start(bf16[8,256,128]{2,1,0:T(8,128)(2,1)} %collective-permute-done.9.refs_4_), channel_id=1, source_target_pairs={{0,1},{1,0},{2,3},{3,2},{4,5},{5,4},{6,7},{7,6},{8,9},{9,8},{10,11... | collective-permute-start | bytes 1572872 | tf_op jit(solution)/shard_map/ppermute | solution.py:291
  108.8 7.3 %collective-permute-start.14 = (bf16[8,256,128]{2,1,0:T(8,128)(2,1)}, bf16[8,256,128]{2,1,0:T(8,128)(2,1)}, u32[]{:S(2)}, u32[]{:S(2)}) collective-permute-start(bf16[8,256,128]{2,1,0:T(8,128)(2,1)} %collective-permute-done.10.refs_5_), channel_id=1, source_target_pairs={{0,1},{1,0},{2,3},{3,2},{4,5},{5,4},{6,7},{7,6},{8,9},{9,8},{10,11... | collective-permute-start | bytes 1572872 | tf_op jit(solution)/shard_map/ppermute | solution.py:291
  108.9 14.4 %all-to-all-start.5 = ((bf16[16,48,128]{2,1,0:T(8,128)(2,1)}), bf16[16,48,128]{2,1,0:T(8,128)(2,1)S(1)}, u32[]{:S(2)}, u32[]{:S(2)}) async-start(bf16[16,48,128]{2,1,0:T(8,128)(2,1)} %shard_map.99), calls=%async_computation.5 | async-start | bytes 393216 | tf_op jit(solution)/shard_map/all_to_all | solution.py:276
  116.0 7.3 %copy-start.2 = (bf16[128,512]{1,0:T(8,128)(2,1)S(1)}, bf16[128,512]{1,0:T(8,128)(2,1)}, u32[]{:S(2)}) copy-start(bf16[128,512]{1,0:T(8,128)(2,1)} %k.5) | copy-start | bytes 393220
  116.0 7.3 %copy-start.3 = (bf16[128,512]{1,0:T(8,128)(2,1)S(1)}, bf16[128,512]{1,0:T(8,128)(2,1)}, u32[]{:S(2)}) copy-start(bf16[128,512]{1,0:T(8,128)(2,1)} %v.5) | copy-start | bytes 393220
  116.0 7.3 %copy-start.4 = (f32[128,512]{1,0:T(8,128)S(1)}, f32[128,512]{1,0:T(8,128)}, u32[]{:S(2)}) copy-start(f32[128,512]{1,0:T(8,128)} %get-tuple-element.128.kg_local) | copy-start | bytes 786436
  116.0 7.3 %copy-start.5 = (f32[128,512]{1,0:T(8,128)S(1)}, f32[128,512]{1,0:T(8,128)}, u32[]{:S(2)}) copy-start(f32[128,512]{1,0:T(8,128)} %get-tuple-element.129.vg_local) | copy-start | bytes 786436
